TPU v7x, 32 devices: a whole 2x2x4 slice. The times are simulated.
32 devices in a mesh: section: 2 (over y), dp: 16 (over z, x, core).
Axes of the slice: x: 2, y: 2, z: 4, core: 2. Of those that a mesh axis runs over, the one named last changes fastest.
Arguments:
- node_input: bfloat16 [32, 384, 128], P('dp', 'section'), may hold values from -6 to 6
- edge_input: bfloat16 [32, 384, 48, 128], P('dp', 'section'), may hold values from -6 to 6
- neighbors: int32 [32, 384, 48], P('dp'), may hold values from 0 to 383
- residue_mask: int32 [32, 384], P('dp'), may hold values 0 or 1
- decode_order: int32 [32, 384], P('dp'), may hold values from 0 to 383, each once within a row
- node_cotangent: bfloat16 [32, 384, 128], P('dp', 'section'), may hold values from -6 to 6
- edge_cotangent: bfloat16 [32, 384, 48, 128], P('dp', 'section'), may hold values from -6 to 6
- message_w1: bfloat16 [2, 384, 128], P('section'), may hold values from -0.3125 to 0.3125
- message_w2: bfloat16 [2, 128, 128], P('section'), may hold values from -0.5 to 0.5
- message_w3: bfloat16 [2, 128, 128], P('section'), may hold values from -2 to 2
- inner_w: bfloat16 [2, 128, 512], P('section'), may hold values from -0.5 to 0.5
- inner_bias: float32 [2, 512], P('section'), may hold values from -3 to 3
- outer_w: bfloat16 [2, 512, 128], P('section'), may hold values from -0.25 to 0.25
- update_w1: bfloat16 [2, 384, 128], P('section'), may hold values from -0.3125 to 0.3125
- update_w2: bfloat16 [2, 128, 128], P('section'), may hold values from -0.5 to 0.5
- update_w3: bfloat16 [2, 128, 128], P('section'), may hold values from -0.5 to 0.5
- biases: float32 [2, 10, 128], P('section'), may hold values from -3 to 3
- norm_gains: float32 [2, 3, 128], P('section'), may hold values from 0.5 to 1.5
Outputs:
- decoded_nodes: bfloat16 [32, 384, 128], P('dp', 'section')
- decoded_edges: bfloat16 [32, 384, 48, 128], P('dp', 'section')
- node_grad: bfloat16 [32, 384, 128], P('dp', 'section')
- edge_grad: bfloat16 [32, 384, 48, 128], P('dp', 'section')
- message_w1_grad: float32 [2, 384, 128], P('section')
- message_w2_grad: float32 [2, 128, 128], P('section')
- message_w3_grad: float32 [2, 128, 128], P('section')
- inner_w_grad: float32 [2, 128, 512], P('section')
- inner_bias_grad: float32 [2, 512], P('section')
- outer_w_grad: float32 [2, 512, 128], P('section')
- update_w1_grad: float32 [2, 384, 128], P('section')
- update_w2_grad: float32 [2, 128, 128], P('section')
- update_w3_grad: float32 [2, 128, 128], P('section')
- biases_grad: float32 [2, 10, 128], P('section')
- norm_gains_grad: float32 [2, 3, 128], P('section')
Inputs may be any that keep to these rules, and one draw needn't show every extreme that they name: Each row of decode_order holds every step once.
All inputs are finite; a program needn't handle non-finite values. No bound on the sum of `residue_mask` on one device may be relied on, other than what follows from the above.
Results may differ from a plain program's by a relative error of at most 0.029.
Values may be sent and summed in bfloat16 or wider, within the bound.
A program may use at most 640 MiB of HBM per device.

v0:
```python
import jax
import jax.numpy as jnp
from jax import lax
from jax.sharding import PartitionSpec as P


def partner(x, axis, bit):
    return lax.ppermute(x, axis, [(i, i ^ 1 << bit) for i in range(lax.axis_size(axis))])


def shifted(block, axis, distance):
    devices = range(lax.axis_size(axis))
    route = [(i - distance, i) for i in devices if i - distance in devices]
    return lax.ppermute(block, axis, route)


def gelu_act(values):
    return jax.nn.gelu(values, approximate=True)


def gelu_back(pre_act, grad_out):
    return jax.vjp(gelu_act, pre_act)[1](grad_out)[0]


def layer_norm(resid, norm_gain, norm_shift):
    centered = resid - jnp.mean(resid, axis=-1, keepdims=True)
    spread_sq = jnp.mean(centered * centered, axis=-1, keepdims=True)
    return centered * lax.rsqrt(spread_sq + 1e-05) * norm_gain + norm_shift


def pick_batch(stacked, batch_index):
    return lax.dynamic_index_in_dim(stacked, batch_index, 0, keepdims=False)


def table_rows(neighbor_ids, length_rows):
    positions = jnp.arange(length_rows, dtype=jnp.int32)
    return (neighbor_ids.reshape(-1)[:, None] == positions[None, :]).astype(jnp.bfloat16)


def make_masks(neighbor_ids, live_row, order_row):
    length_rows = live_row.shape[0]
    positions = jnp.arange(length_rows, dtype=jnp.int32)
    table_three = (neighbor_ids[:, :, None] == positions[None, None, :]).astype(jnp.bfloat16)
    live_near = jnp.einsum(
        "ikj,j->ik", table_three, live_row.astype(jnp.bfloat16), preferred_element_type=jnp.float32
    )
    before_matrix = (order_row[None, :] < order_row[:, None]).astype(jnp.bfloat16)
    earlier = jnp.einsum(
        "ikj,ij->ik", table_three, before_matrix, preferred_element_type=jnp.float32
    )
    return (live_near, earlier)


def assemble(node_rows, edge_rows, table):
    local_rows = jnp.broadcast_to(node_rows[:, None, :], edge_rows.shape)
    near_rows = jnp.dot(table, node_rows, preferred_element_type=jnp.float32).astype(jnp.bfloat16)
    joined = jnp.concatenate([local_rows, edge_rows, near_rows.reshape(edge_rows.shape)], axis=-1)
    return joined.reshape(-1, 3 * node_rows.shape[1])


def spread_back(grad_joined, table, edge_shape):
    length_rows, near_count, feature_width = edge_shape
    shaped = grad_joined.reshape(length_rows, near_count, 3 * feature_width)
    local_grad = jnp.sum(shaped[:, :, :feature_width], axis=1)
    edge_part = shaped[:, :, feature_width : 2 * feature_width]
    near_part = shaped[:, :, 2 * feature_width :].reshape(-1, feature_width)
    high_part = near_part.astype(jnp.bfloat16)
    rest_one = near_part - high_part.astype(jnp.float32)
    middle_part = rest_one.astype(jnp.bfloat16)
    last_part = (rest_one - middle_part.astype(jnp.float32)).astype(jnp.bfloat16)
    near_grad = jnp.zeros((length_rows, feature_width), jnp.float32)
    for piece in (last_part, middle_part, high_part):
        near_grad = near_grad + jnp.einsum(
            "rl,rh->lh", table, piece, preferred_element_type=jnp.float32
        )
    return (local_grad + near_grad, edge_part)


def weight_grad(activ, grad_low):
    return jnp.einsum("ri,ro->io", activ, grad_low, preferred_element_type=jnp.float32)


def input_grad(grad_low, weight):
    return jnp.dot(grad_low, weight.T, preferred_element_type=jnp.float32)


def perceptron_forward(joined, first_w, second_w, third_w, bias_rows, offset):
    pre_one = jnp.dot(joined, first_w, preferred_element_type=jnp.float32) + bias_rows[offset]
    act_one = gelu_act(pre_one).astype(jnp.bfloat16)
    pre_two = jnp.dot(act_one, second_w, preferred_element_type=jnp.float32) + bias_rows[offset + 1]
    act_two = gelu_act(pre_two).astype(jnp.bfloat16)
    result = jnp.dot(act_two, third_w, preferred_element_type=jnp.float32) + bias_rows[offset + 2]
    return (result, (pre_one, pre_two))


def perceptron_backward(joined, first_w, second_w, third_w, stored, grad_out):
    pre_one, pre_two = stored
    act_one = gelu_act(pre_one).astype(jnp.bfloat16)
    act_two = gelu_act(pre_two).astype(jnp.bfloat16)
    low_three = grad_out.astype(jnp.bfloat16)
    grad_pre_two = gelu_back(pre_two, input_grad(low_three, third_w))
    low_two = grad_pre_two.astype(jnp.bfloat16)
    grad_pre_one = gelu_back(pre_one, input_grad(low_two, second_w))
    low_one = grad_pre_one.astype(jnp.bfloat16)
    weight_grads = (
        weight_grad(joined, low_one),
        weight_grad(act_one, low_two),
        weight_grad(act_two, low_three),
    )
    bias_grads = (
        jnp.sum(grad_pre_one, axis=0),
        jnp.sum(grad_pre_two, axis=0),
        jnp.sum(grad_out, axis=0),
    )
    return (input_grad(low_one, first_w), weight_grads, bias_grads)


def layer_forward(node_rows, edge_rows, neighbor_ids, attend, live_mask, weights):
    (
        weight_one,
        weight_two,
        weight_three,
        inner_weight,
        inner_offset,
        outer_weight,
        edge_one,
        edge_two,
        edge_three,
        bias_rows,
        gain_rows,
    ) = weights
    table = table_rows(neighbor_ids, node_rows.shape[0])
    joined = assemble(node_rows, edge_rows, table)
    message, message_kept = perceptron_forward(
        joined, weight_one, weight_two, weight_three, bias_rows, 0
    )
    update = jnp.sum(attend[:, :, None] * message.reshape(edge_rows.shape), axis=1) / 30.0
    resid_one = node_rows.astype(jnp.float32) + update
    normed_one = layer_norm(resid_one, gain_rows[0], bias_rows[7])
    normed_low = normed_one.astype(jnp.bfloat16)
    inner_pre = jnp.dot(normed_low, inner_weight, preferred_element_type=jnp.float32) + inner_offset
    hidden = gelu_act(inner_pre).astype(jnp.bfloat16)
    resid_two = normed_one + (
        jnp.dot(hidden, outer_weight, preferred_element_type=jnp.float32) + bias_rows[3]
    )
    node_out = (layer_norm(resid_two, gain_rows[1], bias_rows[8]) * live_mask[:, None]).astype(
        jnp.bfloat16
    )
    joined_edge = assemble(node_out, edge_rows, table)
    edge_message, edge_kept = perceptron_forward(
        joined_edge, edge_one, edge_two, edge_three, bias_rows, 4
    )
    resid_three = edge_rows.astype(jnp.float32) + edge_message.reshape(edge_rows.shape)
    edge_out = layer_norm(resid_three, gain_rows[2], bias_rows[9]).astype(jnp.bfloat16)
    stored = (
        node_rows,
        edge_rows,
        message_kept,
        resid_one,
        normed_low,
        inner_pre,
        hidden,
        resid_two,
        node_out,
        edge_kept,
        resid_three,
    )
    return (node_out, edge_out, stored)


def layer_backward(
    neighbor_ids, attend, live_mask, weights, stored, grad_nodes_out, grad_edges_out
):
    (
        weight_one,
        weight_two,
        weight_three,
        inner_weight,
        inner_offset,
        outer_weight,
        edge_one,
        edge_two,
        edge_three,
        bias_rows,
        gain_rows,
    ) = weights
    (
        node_rows,
        edge_rows,
        message_kept,
        resid_one,
        normed_low,
        inner_pre,
        hidden,
        resid_two,
        node_out,
        edge_kept,
        resid_three,
    ) = stored
    edge_shape = resid_three.shape
    feature_width = edge_shape[2]
    table = table_rows(neighbor_ids, node_rows.shape[0])
    joined_edge = assemble(node_out, edge_rows, table)
    grad_resid_three, grad_gain_three, grad_shift_three = jax.vjp(
        layer_norm, resid_three, gain_rows[2], bias_rows[9]
    )[1](grad_edges_out)
    grad_joined_edge, edge_wgrads, edge_bgrads = perceptron_backward(
        joined_edge,
        edge_one,
        edge_two,
        edge_three,
        edge_kept,
        grad_resid_three.reshape(-1, feature_width),
    )
    node_part, edge_part = spread_back(grad_joined_edge, table, edge_shape)
    grad_edges = grad_resid_three + edge_part
    grad_node_out = grad_nodes_out + node_part

    def masked_norm(resid, norm_gain, norm_shift):
        return layer_norm(resid, norm_gain, norm_shift) * live_mask[:, None]

    grad_resid_two, grad_gain_two, grad_shift_two = jax.vjp(
        masked_norm, resid_two, gain_rows[1], bias_rows[8]
    )[1](grad_node_out)
    low_outer = grad_resid_two.astype(jnp.bfloat16)
    grad_inner = gelu_back(inner_pre, input_grad(low_outer, outer_weight))
    low_inner = grad_inner.astype(jnp.bfloat16)
    grad_normed = grad_resid_two + input_grad(low_inner, inner_weight)
    grad_resid_one, grad_gain_one, grad_shift_one = jax.vjp(
        layer_norm, resid_one, gain_rows[0], bias_rows[7]
    )[1](grad_normed)
    grad_message = (attend[:, :, None] * grad_resid_one[:, None, :] / 30.0).reshape(
        -1, feature_width
    )
    joined = assemble(node_rows, edge_rows, table)
    grad_joined, message_wgrads, message_bgrads = perceptron_backward(
        joined, weight_one, weight_two, weight_three, message_kept, grad_message
    )
    node_part, edge_part = spread_back(grad_joined, table, edge_shape)
    grad_nodes = grad_resid_one + node_part
    grad_edges = grad_edges + edge_part
    bias_grads = jnp.stack(
        [
            message_bgrads[0],
            message_bgrads[1],
            message_bgrads[2],
            jnp.sum(grad_resid_two, axis=0),
            edge_bgrads[0],
            edge_bgrads[1],
            edge_bgrads[2],
            grad_shift_one,
            grad_shift_two,
            grad_shift_three,
        ]
    )
    gain_grads = jnp.stack([grad_gain_one, grad_gain_two, grad_gain_three])
    all_grads = (
        message_wgrads[0],
        message_wgrads[1],
        message_wgrads[2],
        weight_grad(normed_low, low_inner),
        jnp.sum(grad_inner, axis=0),
        weight_grad(hidden, low_outer),
        edge_wgrads[0],
        edge_wgrads[1],
        edge_wgrads[2],
        bias_grads,
        gain_grads,
    )
    return (grad_nodes, grad_edges, all_grads)


def per_device(
    node_input,
    edge_input,
    neighbors,
    residue_mask,
    decode_order,
    node_cotangent,
    edge_cotangent,
    message_w1,
    message_w2,
    message_w3,
    inner_w,
    inner_bias,
    outer_w,
    update_w1,
    update_w2,
    update_w3,
    biases,
    norm_gains,
):
    section_index = lax.axis_index("section")
    is_first = section_index == 0
    micro_count = node_input.shape[0]
    half_rows = node_input.shape[1]
    live_all = residue_mask.astype(jnp.float32)
    live_near, earlier = jax.vmap(make_masks)(neighbors, residue_mask, decode_order)
    send_nodes = jnp.where(is_first, node_cotangent, node_input)
    send_edges = jnp.where(is_first, edge_cotangent, edge_input)
    got_nodes, got_edges = partner((send_nodes, send_edges), "section", 0)
    full_nodes = jnp.concatenate(
        [
            jnp.where(is_first, node_input, got_nodes),
            jnp.where(is_first, got_nodes, node_cotangent),
        ],
        axis=1,
    )
    full_edges = jnp.concatenate(
        [
            jnp.where(is_first, edge_input, got_edges),
            jnp.where(is_first, got_edges, edge_cotangent),
        ],
        axis=1,
    )
    weights = (
        message_w1[0],
        message_w2[0],
        message_w3[0],
        inner_w[0],
        inner_bias[0],
        outer_w[0],
        update_w1[0],
        update_w2[0],
        update_w3[0],
        biases[0],
        norm_gains[0],
    )
    attend_all = live_near * jnp.where(is_first, jnp.ones_like(earlier), earlier)
    zero_nodes = jnp.zeros(full_nodes.shape[1:], jnp.bfloat16)
    zero_edges = jnp.zeros(full_edges.shape[1:], jnp.bfloat16)
    recv_nodes, recv_edges = (zero_nodes, zero_edges)
    tick_kept = []
    tick_outputs = []
    for tick_index in range(micro_count + 1):
        batch_index = jnp.clip(tick_index - section_index, 0, micro_count - 1)
        in_nodes = jnp.where(is_first, pick_batch(full_nodes, batch_index), recv_nodes)
        in_edges = jnp.where(is_first, pick_batch(full_edges, batch_index), recv_edges)
        out_nodes, out_edges, kept_values = layer_forward(
            in_nodes,
            in_edges,
            pick_batch(neighbors, batch_index),
            pick_batch(attend_all, batch_index),
            pick_batch(live_all, batch_index),
            weights,
        )
        tick_kept.append(kept_values)
        tick_outputs.append((out_nodes, out_edges))
        if tick_index < micro_count:
            recv_nodes, recv_edges = shifted((out_nodes, out_edges), "section", 1)
    kept_stack = jax.tree.map(lambda *values: jnp.stack(values), *tick_kept)
    grad_total = tuple((jnp.zeros(tensor.shape, jnp.float32) for tensor in weights))
    back_nodes, back_edges = (zero_nodes, zero_edges)
    grad_list = []
    for tick_index in range(micro_count + 1):
        batch_index = jnp.clip(jnp.where(is_first, tick_index - 1, tick_index), 0, micro_count - 1)
        kept_index = jnp.where(is_first, max(tick_index - 1, 0), min(tick_index + 1, micro_count))
        stored = jax.tree.map(lambda values: pick_batch(values, kept_index), kept_stack)
        cot_nodes = jnp.where(is_first, back_nodes, pick_batch(full_nodes, batch_index)).astype(
            jnp.float32
        )
        cot_edges = jnp.where(is_first, back_edges, pick_batch(full_edges, batch_index)).astype(
            jnp.float32
        )
        neighbor_ids = pick_batch(neighbors, batch_index)
        attend = pick_batch(attend_all, batch_index)
        live_mask = pick_batch(live_all, batch_index)
        grad_nodes, grad_edges, all_grads = layer_backward(
            neighbor_ids, attend, live_mask, weights, stored, cot_nodes, cot_edges
        )
        is_valid = jnp.where(is_first, tick_index >= 1, tick_index < micro_count).astype(
            jnp.float32
        )
        grad_total = tuple(
            (tensor + is_valid * update_term for tensor, update_term in zip(grad_total, all_grads))
        )
        sent_nodes = grad_nodes.astype(jnp.bfloat16)
        sent_edges = grad_edges.astype(jnp.bfloat16)
        if tick_index < micro_count:
            back_nodes, back_edges = shifted((sent_nodes, sent_edges), "section", -1)
        if tick_index >= 1:
            grad_list.append((sent_nodes, sent_edges))
    dec_nodes = jnp.stack([tick_outputs[batch_slot + 1][0] for batch_slot in range(micro_count)])
    dec_edges = jnp.stack([tick_outputs[batch_slot + 1][1] for batch_slot in range(micro_count)])
    input_nodes_grad = jnp.stack([grad_list[batch_slot][0] for batch_slot in range(micro_count)])
    input_edges_grad = jnp.stack([grad_list[batch_slot][1] for batch_slot in range(micro_count)])
    send_nodes = jnp.where(is_first, input_nodes_grad[:, half_rows:], dec_nodes[:, :half_rows])
    send_edges = jnp.where(is_first, input_edges_grad[:, half_rows:], dec_edges[:, :half_rows])
    got_nodes, got_edges = partner((send_nodes, send_edges), "section", 0)
    decoded_nodes = jnp.where(is_first, got_nodes, dec_nodes[:, half_rows:])
    decoded_edges = jnp.where(is_first, got_edges, dec_edges[:, half_rows:])
    node_grad = jnp.where(is_first, input_nodes_grad[:, :half_rows], got_nodes)
    edge_grad = jnp.where(is_first, input_edges_grad[:, :half_rows], got_edges)
    summed = lax.psum(
        (
            grad_total[0],
            grad_total[1],
            grad_total[2],
            grad_total[3],
            grad_total[4],
            grad_total[5],
            grad_total[6],
            grad_total[7],
            grad_total[8],
            grad_total[9],
            grad_total[10],
        ),
        "dp",
    )
    return (
        decoded_nodes,
        decoded_edges,
        node_grad,
        edge_grad,
        summed[0][None],
        summed[1][None],
        summed[2][None],
        summed[3][None],
        summed[4][None],
        summed[5][None],
        summed[6][None],
        summed[7][None],
        summed[8][None],
        summed[9][None],
        summed[10][None],
    )


def solution(mesh):
    in_specs = (
        P("dp", "section", None),
        P("dp", "section", None, None),
        P("dp", None, None),
        P("dp", None),
        P("dp", None),
        P("dp", "section", None),
        P("dp", "section", None, None),
        P("section", None, None),
        P("section", None, None),
        P("section", None, None),
        P("section", None, None),
        P("section", None),
        P("section", None, None),
        P("section", None, None),
        P("section", None, None),
        P("section", None, None),
        P("section", None, None),
        P("section", None, None),
    )
    out_specs = (
        P("dp", "section", None),
        P("dp", "section", None, None),
        P("dp", "section", None),
        P("dp", "section", None, None),
        P("section", None, None),
        P("section", None, None),
        P("section", None, None),
        P("section", None, None),
        P("section", None),
        P("section", None, None),
        P("section", None, None),
        P("section", None, None),
        P("section", None, None),
        P("section", None, None),
        P("section", None, None),
    )
    return jax.shard_map(
        per_device, mesh=mesh, in_specs=in_specs, out_specs=out_specs, check_vma=False
    )
```

profile of v0, /device:TPU:0, one launch (start us, length us, event | category | flops | bytes accessed | tf_op | source)
XLA Modules:
  0.0 2216.6 jit_solution(2771744659676940652)
XLA Ops:
  33.1 24.0 %fusion.1 = f32[2,1,384,48]{3,1,2,0:T(1,128)S(1)} fusion(s32[2,384,48]{2,1,0:T(8,128)S(1)} %copy.166, bf16[2,384,1,1]{1,0,2,3:T(2,128)(2,1)S(1)} %get-tuple-element.259), kind=kOutput, calls=%fused_computation.2 | convolution fusion | flops 42467328 | bytes 296448 | tf_op jit(solution)/shard_map/vmap(ikj,j->ik)/dot_general | solution.py:44
  90.4 32.8 %collective-permute-done.1 = bf16[2,192,48,128]{3,1,2,0:T(8,128)(2,1)} collective-permute-done((bf16[2,192,48,128]{3,1,2,0:T(8,128)(2,1)}, bf16[2,192,48,128]{3,1,2,0:T(8,128)(2,1)}, u32[]{:S(2)}, u32[]{:S(2)}) %collective-permute-start.1) | collective-permute-done | bytes 4718624 | tf_op jit(solution)/shard_map/ppermute | solution.py:8
  241.1 98.7 %collective-permute-done.3 = bf16[384,128]{1,0:T(8,128)(2,1)S(1)} collective-permute-done((bf16[384,128]{1,0:T(8,128)(2,1)S(1)}, bf16[384,128]{1,0:T(8,128)(2,1)S(1)}, u32[]{:S(2)}, u32[]{:S(2)}) %collective-permute-start.3) | collective-permute-done | bytes 98336 | tf_op jit(solution)/shard_map/ppermute | solution.py:14
  498.5 82.3 %collective-permute-done.5 = bf16[384,128]{1,0:T(8,128)(2,1)S(1)} collective-permute-done((bf16[384,128]{1,0:T(8,128)(2,1)S(1)}, bf16[384,128]{1,0:T(8,128)(2,1)S(1)}, u32[]{:S(2)}, u32[]{:S(2)}) %collective-permute-start.5) | collective-permute-done | bytes 98336 | tf_op jit(solution)/shard_map/ppermute | solution.py:14
  780.3 13.5 pad_maximum_fusion
  814.0 13.6 fusion.147
  827.6 20.3 fusion.541
  901.6 14.0 fusion.471
  1011.5 23.2 %pad_maximum_fusion.4 = f32[3,18432,128]{2,1,0:T(8,128)} fusion(f32[1,18432,128]{2,1,0:T(8,128)} %bitcast.1106, f32[1,18432,128]{2,1,0:T(8,128)} %bitcast.1102, f32[1,18432,128]{2,1,0:T(8,128)} %bitcast.1100), kind=kLoop, calls=%fused_computation.7 | loop fusion | flops 14155776 | bytes 56623104 | tf_op jit(solution)/shard_map/stack | solution.py:351
  1055.4 18.1 fusion.1049
  1193.4 13.1 fusion.20
  1280.1 58.8 %collective-permute-done.7 = bf16[384,48,128]{2,0,1:T(8,128)(2,1)} collective-permute-done((bf16[384,48,128]{2,0,1:T(8,128)(2,1)}, bf16[384,48,128]{2,0,1:T(8,128)(2,1)}, u32[]{:S(2)}, u32[]{:S(2)}) %collective-permute-start.7) | collective-permute-done | bytes 4718624 | tf_op jit(solution)/shard_map/ppermute | solution.py:14
  1349.4 13.6 fusion.1035
  1518.6 21.0 fusion.369
  1580.5 13.0 fusion.634
  1619.5 64.0 %collective-permute-done.9 = bf16[384,48,128]{2,0,1:T(8,128)(2,1)} collective-permute-done((bf16[384,48,128]{2,0,1:T(8,128)(2,1)}, bf16[384,48,128]{2,0,1:T(8,128)(2,1)}, u32[]{:S(2)}, u32[]{:S(2)}) %collective-permute-start.9) | collective-permute-done | bytes 4718624 | tf_op jit(solution)/shard_map/ppermute | solution.py:14
  1683.6 22.2 %multiply_reduce_fusion.1 = (f32[384,48]{0,1:T(8,128)S(1)}, f32[384,48]{0,1:T(8,128)S(1)}, f32[128]{0:T(128)}, f32[128]{0:T(128)}, f32[128]{0:T(128)}, /*index=5*/f32[128]{0:T(128)}, bf16[384,48,128]{2,0,1:T(8,128)(2,1)S(1)}) fusion(f32[3,384,48,128]{3,1,2,0:T(8,128)} %pad_maximum_fusion, s32[]{:T(128)S(6)} %select_n.287, f32[384,48]{0,1:T(8,128)S(1)} %copy-done.79, ...), kind=kLoop, calls=%fused_computation.559 | loop fusion | flops 61304320 | bytes 42985996 | tf_op jit(solution)/shard_map/jvp()/reduce_sum | solution.py:27
  1705.9 13.3 fusion.1036
  1719.9 13.4 add_convert_fusion.2
  1774.7 13.8 fusion.463
  1900.0 18.6 fusion.319
  1931.6 57.6 %all-reduce = (f32[1,512]{1,0:T(1,128)}, f32[1,10,128]{2,1,0:T(8,128)S(1)}, f32[1,3,128]{2,1,0:T(4,128)S(1)}) all-reduce(f32[1,512]{1,0:T(1,128)S(1)} %bitcast.1165, f32[1,10,128]{2,1,0:T(8,128)S(1)} %add_bitcast_fusion, f32[1,3,128]{2,1,0:T(4,128)S(1)} %fusion.899), channel_id=1, replica_groups=mesh['section'=2,'dp'=16] {'dp'}, use_global_device_ids=true, to_apply=%region_70.71 | all-reduce | flops 2176 | bytes 17408 | tf_op jit(solution)/shard_map/psum | solution.py:394
  2052.7 13.9 fusion.595
  2124.5 72.6 %all-reduce.4.cloned.1.call-done = (f32[1,384,128]{2,1,0:T(8,128)}, f32[1,128,128]{2,1,0:T(8,128)}, f32[1,128,128]{2,1,0:T(8,128)}, f32[1,128,512]{2,1,0:T(8,128...) async-done(((f32[1,384,128]{2,1,0:T(8,128)}, f32[1,128,128]{2,1,0:T(8,128)}, f32[1,128,128]{2,1,0:T(8,128)}, ...) | async-done | bytes 1179664 | tf_op jit(solution)/shard_map/psum | solution.py:394
  (1146 shorter events, 1447.7 us)
Async XLA Ops:
  7.2 160.4 %copy-start = (bf16[1,512,128]{2,1,0:T(8,128)(2,1)S(1)}, bf16[1,512,128]{2,1,0:T(8,128)(2,1)}, u32[]{:S(2)}) copy-start(bf16[1,512,128]{2,1,0:T(8,128)(2,1)} %param.30) | copy-start | bytes 393220
  7.2 2189.8 %all-reduce.4.cloned.1.call-start = ((), (), s32[]{:S(2)}) async-start(), calls=%async_computation | async-start | bytes 2359296 | tf_op jit(solution)/shard_map/psum | solution.py:394
  8.3 60.0 %collective-permute-start = (bf16[2,192,128]{2,1,0:T(8,128)(2,1)S(1)}, bf16[2,192,128]{2,1,0:T(8,128)(2,1)S(1)}, u32[]{:S(2)}, u32[]{:S(2)}) collective-permute-start(bf16[2,192,128]{2,1,0:T(8,128)(2,1)S(1)} %broadcast_select_fusion.5), channel_id=1, source_target_pairs={{0,16},{16,0},{1,17},{17,1},{2,18},{18,2},{3,19},{19,3},{4,20},{20... | collective-permute-start | bytes 294920 | tf_op jit(solution)/shard_map/ppermute | solution.py:8
  19.6 103.6 %collective-permute-start.1 = (bf16[2,192,48,128]{3,1,2,0:T(8,128)(2,1)}, bf16[2,192,48,128]{3,1,2,0:T(8,128)(2,1)}, u32[]{:S(2)}, u32[]{:S(2)}) collective-permute-start(bf16[2,192,48,128]{3,1,2,0:T(8,128)(2,1)} %broadcast_select_fusion.2), channel_id=1, source_target_pairs={{0,16},{16,0},{1,17},{17,1},{2,18},{18,2},{3,19},{19,3},{4,20},{20... | collective-permute-start | bytes 14155784 | tf_op jit(solution)/shard_map/ppermute | solution.py:8
  19.7 684.6 %copy-start.166 = (f32[128]{0:T(128)}, f32[128]{0:T(128)S(1)}, u32[]{:S(2)}) copy-start(f32[128]{0:T(128)S(1)} %get-tuple-element.262) | copy-start | bytes 1540
  19.7 686.9 %copy-start.170 = (f32[128]{0:T(128)}, f32[128]{0:T(128)S(1)}, u32[]{:S(2)}) copy-start(f32[128]{0:T(128)S(1)} %get-tuple-element.261) | copy-start | bytes 1540
  19.7 807.9 %copy-start.152 = (f32[128]{0:T(128)}, f32[128]{0:T(128)S(1)}, u32[]{:S(2)}) copy-start(f32[128]{0:T(128)S(1)} %get-tuple-element.260) | copy-start | bytes 1540
  20.2 359.6 %copy-start.242 = (f32[128]{0:T(128)}, f32[128]{0:T(128)S(1)}, u32[]{:S(2)}) copy-start(f32[128]{0:T(128)S(1)} %get-tuple-element.256) | copy-start | bytes 1540
  68.3 512.6 %copy-start.92 = (bf16[2,192,128]{2,1,0:T(8,128)(2,1)}, bf16[2,192,128]{2,1,0:T(8,128)(2,1)S(1)}, u32[]{:S(2)}) copy-start(bf16[2,192,128]{2,1,0:T(8,128)(2,1)S(1)} %get-tuple-element.240) | copy-start | bytes 294916
  68.3 512.6 %copy-start.96 = (bf16[2,192,128]{2,1,0:T(8,128)(2,1)}, bf16[2,192,128]{2,1,0:T(8,128)(2,1)S(1)}, u32[]{:S(2)}) copy-start(bf16[2,192,128]{2,1,0:T(8,128)(2,1)S(1)} %get-tuple-element.241) | copy-start | bytes 294916
  235.1 127.3 %collective-permute-start.2 = (bf16[384,48,128]{2,0,1:T(8,128)(2,1)}, bf16[384,48,128]{2,0,1:T(8,128)(2,1)}, u32[]{:S(2)}, u32[]{:S(2)}) collective-permute-start(bf16[384,48,128]{2,0,1:T(8,128)(2,1)} %fusion.146), channel_id=1, source_target_pairs={{0,16},{1,17},{2,18},{3,19},{4,20},{5,21},{6,22},{7,23},{8,24},{9,... | collective-permute-start | bytes 14155784 | tf_op jit(solution)/shard_map/ppermute | solution.py:14
  239.6 100.3 %collective-permute-start.3 = (bf16[384,128]{1,0:T(8,128)(2,1)S(1)}, bf16[384,128]{1,0:T(8,128)(2,1)S(1)}, u32[]{:S(2)}, u32[]{:S(2)}) collective-permute-start(bf16[384,128]{1,0:T(8,128)(2,1)S(1)} %multiply_convert_fusion.2), channel_id=1, source_target_pairs={{0,16},{1,17},{2,18},{3,19},{4,20},{5,21},{6,22},{7,23},{8,24},{9,... | collective-permute-start | bytes 294920 | tf_op jit(solution)/shard_map/ppermute | solution.py:14
  473.4 195.8 %collective-permute-start.4 = (bf16[384,48,128]{2,0,1:T(8,128)(2,1)}, bf16[384,48,128]{2,0,1:T(8,128)(2,1)}, u32[]{:S(2)}, u32[]{:S(2)}) collective-permute-start(bf16[384,48,128]{2,0,1:T(8,128)(2,1)} %add_convert_fusion.1), channel_id=1, source_target_pairs={{0,16},{1,17},{2,18},{3,19},{4,20},{5,21},{6,22},{7,23},{8,24},{9,... | collective-permute-start | bytes 14155784 | tf_op jit(solution)/shard_map/ppermute | solution.py:14
  481.6 149.7 %copy-start.156 = (s32[18432]{0:T(1024)}, s32[18432]{0:T(1024)S(1)}, u32[]{:S(2)}) copy-start(s32[18432]{0:T(1024)S(1)} %eq.130) | copy-start | bytes 221188
  482.2 174.3 %copy-start.164 = (s32[18432]{0:T(1024)}, s32[18432]{0:T(1024)S(1)}, u32[]{:S(2)}) copy-start(s32[18432]{0:T(1024)S(1)} %eq.118) | copy-start | bytes 221188
  482.6 161.4 %copy-start.159 = (s32[18432]{0:T(1024)}, s32[18432]{0:T(1024)S(1)}, u32[]{:S(2)}) copy-start(s32[18432]{0:T(1024)S(1)} %eq.126) | copy-start | bytes 221188
  496.4 84.5 %collective-permute-start.5 = (bf16[384,128]{1,0:T(8,128)(2,1)S(1)}, bf16[384,128]{1,0:T(8,128)(2,1)S(1)}, u32[]{:S(2)}, u32[]{:S(2)}) collective-permute-start(bf16[384,128]{1,0:T(8,128)(2,1)S(1)} %multiply_convert_fusion.1), channel_id=1, source_target_pairs={{0,16},{1,17},{2,18},{3,19},{4,20},{5,21},{6,22},{7,23},{8,24},{9,... | collective-permute-start | bytes 294920 | tf_op jit(solution)/shard_map/ppermute | solution.py:14
  1191.6 171.5 %copy-start.69 = (f32[384,48]{0,1:T(8,128)}, f32[384,48]{0,1:T(8,128)S(1)}, u32[]{:S(2)}) copy-start(f32[384,48]{0,1:T(8,128)S(1)} %broadcast_multiply_fusion.2) | copy-start | bytes 221188
  1230.1 232.9 %collective-permute-start.6 = (bf16[384,128]{1,0:T(8,128)(2,1)}, bf16[384,128]{1,0:T(8,128)(2,1)}, u32[]{:S(2)}, u32[]{:S(2)}) collective-permute-start(bf16[384,128]{1,0:T(8,128)(2,1)} %fusion.635), channel_id=1, source_target_pairs={{16,0},{17,1},{18,2},{19,3},{20,4},{21,5},{22,6},{23,7},{24,8},{25... | collective-permute-start | bytes 294920 | tf_op jit(solution)/shard_map/ppermute | solution.py:14
  1231.5 107.4 %collective-permute-start.7 = (bf16[384,48,128]{2,0,1:T(8,128)(2,1)}, bf16[384,48,128]{2,0,1:T(8,128)(2,1)}, u32[]{:S(2)}, u32[]{:S(2)}) collective-permute-start(bf16[384,48,128]{2,0,1:T(8,128)(2,1)} %get-tuple-element.173), channel_id=1, source_target_pairs={{16,0},{17,1},{18,2},{19,3},{20,4},{21,5},{22,6},{23,7},{24,8},{25... | collective-permute-start | bytes 14155784 | tf_op jit(solution)/shard_map/ppermute | solution.py:14
  1578.9 104.7 %collective-permute-start.9 = (bf16[384,48,128]{2,0,1:T(8,128)(2,1)}, bf16[384,48,128]{2,0,1:T(8,128)(2,1)}, u32[]{:S(2)}, u32[]{:S(2)}) collective-permute-start(bf16[384,48,128]{2,0,1:T(8,128)(2,1)} %get-tuple-element.169), channel_id=1, source_target_pairs={{16,0},{17,1},{18,2},{19,3},{20,4},{21,5},{22,6},{23,7},{24,8},{25... | collective-permute-start | bytes 14155784 | tf_op jit(solution)/shard_map/ppermute | solution.py:14
  1593.5 243.5 %collective-permute-start.8 = (bf16[384,128]{1,0:T(8,128)(2,1)}, bf16[384,128]{1,0:T(8,128)(2,1)}, u32[]{:S(2)}, u32[]{:S(2)}) collective-permute-start(bf16[384,128]{1,0:T(8,128)(2,1)} %fusion.634), channel_id=1, source_target_pairs={{16,0},{17,1},{18,2},{19,3},{20,4},{21,5},{22,6},{23,7},{24,8},{25... | collective-permute-start | bytes 294920 | tf_op jit(solution)/shard_map/ppermute | solution.py:14
  1997.7 109.5 %collective-permute-start.11 = (bf16[2,192,48,128]{3,1,2,0:T(8,128)(2,1)}, bf16[2,192,48,128]{3,1,2,0:T(8,128)(2,1)}, u32[]{:S(2)}, u32[]{:S(2)}) collective-permute-start(bf16[2,192,48,128]{3,1,2,0:T(8,128)(2,1)} %fusion.416), channel_id=1, source_target_pairs={{0,16},{16,0},{1,17},{17,1},{2,18},{18,2},{3,19},{19,3},{4,20},{20... | collective-permute-start | bytes 14155784 | tf_op jit(solution)/shard_map/ppermute | solution.py:8
  2030.3 75.3 %collective-permute-start.10 = (bf16[2,192,128]{2,1,0:T(8,128)(2,1)}, bf16[2,192,128]{2,1,0:T(8,128)(2,1)}, u32[]{:S(2)}, u32[]{:S(2)}) collective-permute-start(bf16[2,192,128]{2,1,0:T(8,128)(2,1)} %fusion.792), channel_id=1, source_target_pairs={{0,16},{16,0},{1,17},{17,1},{2,18},{18,2},{3,19},{19,3},{4,20},{20... | collective-permute-start | bytes 294920 | tf_op jit(solution)/shard_map/ppermute | solution.py:8
  (366 other events, 6096.4 us)
Sparse Core Ops, SparseCore 0:
  2105.7 91.3 all-reduce.3
where the time goes:
time: 2220 us
  matrix products  874 us (39%)
  other arithmetic  519 us (23%)
  waiting for transfers between devices  409 us (18%)
  local copies, waits for them, and re-layouts  312 us (14%)
  blocking collectives  57.6 us (3%)
  starting transfers between devices  26.2 us (1%)
    ppermute x8, waiting for transfers between devices, shifted(): return lax.ppermute(block, axis, route)  304 us
    dot_general x24, matrix products, input_grad(): return jnp.dot(grad_low, weight.T, preferred_element_type=jnp.float32)  216 us
    dot_general x18, matrix products, spread_back(): jnp.einsum('rl,rh->lh', table, piece, preferred_element_type=jnp.float32)  208 us
    dot_general x24, matrix products, weight_grad(): jnp.einsum('ri,ro->io', activ, grad_low, preferred_element_type=jnp.float32)  154 us
    dot_general x12, matrix products, assemble(): jnp.dot(table, node_rows, preferred_element_type=jnp.float32)  151 us
    concatenate x17, local copies, waits for them, and re-layouts, assemble(): jnp.concatenate([local_rows, edge_rows, near_rows.reshape(edge_rows.shape...  115 us
    another operation x18, other arithmetic, per_device(): kept_stack = jax.tree.map(lambda *values: jnp.stack(values), *tick_kept)  88.1 us
    reduce_sum x14, other arithmetic, layer_norm(): spread_sq = jnp.mean(centered * centered, axis=-1, keepdims=True)  79.6 us
  transfers between devices with their start and end apart: 13, of which 6 were waited for; matrix products, arithmetic and copies ran while one was open for 31% of the time, Pallas kernels for 0%

commit v1 on v0

v1 whole, which is shorter than its diff:
```python
import types

import jax
import jax.numpy as jnp
import numpy as np
from jax import lax
from jax.experimental import pallas as pl
from jax.experimental.pallas import tpu as pltpu
from jax.sharding import PartitionSpec as P

BF = jnp.bfloat16
F32 = jnp.float32
C1 = 0.7978845608
C2 = C1 * 0.044715
EPS = 1e-5
BLOCK_RES = 32
EXTRA = 16
SMALL = 32
MESH = pl.DeviceIdType.MESH


def mm(a, b, ca=1, cb=0):
    return lax.dot_general(a, b, (((ca,), (cb,)), ((), ())), preferred_element_type=F32)


def mm_exact(a, b, ca=1, cb=0):
    return lax.dot_general(
        a, b, (((ca,), (cb,)), ((), ())), precision=lax.Precision.HIGHEST, preferred_element_type=F32
    )


def gelu_pair(x):
    x2 = x * x
    t = jnp.tanh(x * (x2 * C2 + C1)).astype(BF)
    h = BF(0.5) * t + BF(0.5)
    g = x.astype(BF) * h
    d = h + (g * (BF(1.0) - h)) * (x2.astype(BF) * BF(6 * C2) + BF(2 * C1))
    return g, d


def gelu_pair_wide(x):
    x2 = x * x
    h = 0.5 * jnp.tanh(x * (x2 * C2 + C1)) + 0.5
    g = x * h
    d = h + (g * (1.0 - h)) * (x2 * (6 * C2) + 2 * C1)
    return g, d


def lane_sum(x):
    total = x[:, :128]
    for at in range(128, x.shape[1], 128):
        total = total + x[:, at : at + 128]
    return total


def to_row(acc):
    return mm_exact(jnp.ones((8, acc.shape[1]), F32), acc, 1, 1)[0:1]


def norm_rows(r):
    c = r - jnp.mean(r, axis=-1, keepdims=True)
    rs = lax.rsqrt(jnp.mean(c * c, axis=-1, keepdims=True) + EPS)
    return c * rs, rs


def norm_back_rows(dxh, xh, rs):
    m1 = jnp.mean(dxh, axis=-1, keepdims=True)
    m2 = jnp.mean(dxh * xh, axis=-1, keepdims=True)
    return (dxh - m1 - xh * m2) * rs


def norm_back(dy, xh, rs, gain_col):
    dxh = dy * gain_col
    m1 = jnp.mean(dxh, axis=0, keepdims=True)
    m2 = jnp.mean(dxh * xh, axis=0, keepdims=True)
    return (dxh - m1 - xh * m2) * rs


class Phase:
    def __init__(self, dims, collective_id=None):
        self.grid = (dims.parts, dims.blocks)
        self.collective_id = collective_id
        self.ins, self.outs, self.temps = [], [], []

    def stream_spec(self, shape):
        rest = len(shape) - 2
        return pl.BlockSpec((1, 1) + tuple(shape[2:]), lambda p, b: (p, b) + (0,) * rest)

    def whole_spec(self, shape):
        rank = len(shape)
        return pl.BlockSpec(tuple(shape), lambda p, b: (0,) * rank)

    def stream(self, **arrays):
        self.ins += [(n, a, self.stream_spec(a.shape)) for n, a in arrays.items()]

    def whole(self, **arrays):
        self.ins += [(n, a, self.whole_spec(a.shape)) for n, a in arrays.items()]

    def raw(self, **arrays):
        self.ins += [(n, a, pl.BlockSpec(memory_space=pl.ANY)) for n, a in arrays.items()]

    def edges(self, dims, **arrays):
        spec = pl.BlockSpec((1, dims.res, dims.near, dims.feat), lambda p, b: (p, b, 0, 0))
        self.ins += [(n, a, spec) for n, a in arrays.items()]

    def out_edges(self, dims, **shapes):
        spec = pl.BlockSpec((1, dims.res, dims.near, dims.feat), lambda p, b: (p, b, 0, 0))
        self.outs += [(n, jax.ShapeDtypeStruct(s, BF), spec) for n, s in shapes.items()]

    def out_stream(self, dtype, **shapes):
        self.outs += [(n, jax.ShapeDtypeStruct(s, dtype), self.stream_spec(s)) for n, s in shapes.items()]

    def out_whole(self, dtype, **shapes):
        self.outs += [(n, jax.ShapeDtypeStruct(s, dtype), self.whole_spec(s)) for n, s in shapes.items()]

    def out_raw(self, dtype, **shapes):
        spec = pl.BlockSpec(memory_space=pl.ANY)
        self.outs += [(n, jax.ShapeDtypeStruct(s, dtype), spec) for n, s in shapes.items()]

    def temp(self, dtype, **shapes):
        self.temps += [(n, pltpu.VMEM(s, dtype)) for n, s in shapes.items()]

    def sems(self, **counts):
        self.temps += [(n, pltpu.SemaphoreType.DMA((c,))) for n, c in counts.items()]

    def call(self, name, body):
        names = [n for n, _, _ in self.ins] + [n for n, _, _ in self.outs] + [n for n, _ in self.temps]

        def kernel(*refs):
            body(types.SimpleNamespace(**dict(zip(names, refs))))

        results = pl.pallas_call(
            kernel,
            grid=self.grid,
            in_specs=[s for _, _, s in self.ins],
            out_specs=[s for _, _, s in self.outs],
            out_shape=[s for _, s, _ in self.outs],
            scratch_shapes=[s for _, s in self.temps],
            compiler_params=pltpu.CompilerParams(
                dimension_semantics=(pltpu.ARBITRARY,) * len(self.grid),
                vmem_limit_bytes=58 << 20,
                collective_id=self.collective_id,
                has_side_effects=self.collective_id is not None,
            ),
            name=name,
        )(*[a for _, a, _ in self.ins])
        return types.SimpleNamespace(**dict(zip([n for n, _, _ in self.outs], results)))


def other_section():
    return {AXIS_S: 1 - lax.axis_index(AXIS_S)}


AXIS_S = "section"
AXIS_D = "dp"


def greet_partner():
    barrier = pltpu.get_barrier_semaphore()
    pl.semaphore_signal(barrier, inc=1, device_id=other_section(), device_id_type=MESH)
    pl.semaphore_wait(barrier, 1)


def to_partner(src, dst, send, recv):
    return pltpu.make_async_remote_copy(
        src_ref=src, dst_ref=dst, send_sem=send, recv_sem=recv, device_id=other_section(), device_id_type=MESH
    )


def prepare(dims, idx_row, edge_input, sum_rows, node_input, weights):
    d = dims
    ph = Phase(d, 1)
    ph.stream(idx=idx_row)
    ph.edges(d, edge=edge_input)
    ph.whole(sums=sum_rows)
    ph.raw(nodes=node_input, **{W_IN + n: a for n, a in weights.items()})
    ph.out_stream(
        BF,
        tt=(d.parts, d.blocks, d.length + d.res, d.rows),
        tn=(d.parts, d.blocks, d.rows, d.length + 128),
        et=(d.parts, d.blocks, d.feat, d.rows),
    )
    ph.out_raw(BF, nodes_got=node_input.shape)
    for n, a in weights.items():
        ph.out_raw(a.dtype, **{n: (2,) + a.shape[1:]})
    count = len(weights)
    ph.sems(send=count + 1, recv=count + 1, local=count)

    def body(r):
        p, b = pl.program_id(0), pl.program_id(1)
        section = lax.axis_index(AXIS_S)

        def copies():
            jobs = [to_partner(r.nodes, r.nodes_got, r.send.at[count], r.recv.at[count])]
            for i, n in enumerate(weights):
                src, dst = getattr(r, W_IN + n), getattr(r, n)
                jobs.append(to_partner(src.at[0], dst.at[section], r.send.at[i], r.recv.at[i]))
                jobs.append(pltpu.make_async_copy(src.at[0], dst.at[section], r.local.at[i]))
            return jobs

        @pl.when((p == 0) & (b == 0))
        def _():
            greet_partner()
            for job in copies():
                job.start()

        idx = r.idx[0, 0] - section * d.half
        idx = jnp.where(idx < 0, idx + d.length, idx)
        at = lax.broadcasted_iota(jnp.int32, (d.length, d.rows), 0)
        table = (at == idx).astype(F32).astype(BF)
        r.tt[0, 0, : d.length, :] = table
        sums = r.sums[...]
        r.tt[0, 0, d.length :, :] = sums[: d.res]
        r.tn[0, 0, :, : d.length] = table.T
        r.tn[0, 0, :, d.length :] = sums.T
        r.et[0, 0] = r.edge[0].reshape(d.rows, d.feat).T

        @pl.when((p == d.parts - 1) & (b == d.blocks - 1))
        def _():
            for job in copies():
                job.wait()

    return ph.call("tables", body)


W_IN = "w_"


def weight_args(w, *names):
    return {n: getattr(w, n) for n in names}


def load_cols(r, layer, aux, cols):
    n_bias, n_gain = r.bias.shape[1], r.gain.shape[1]
    aux[...] = jnp.zeros(aux.shape, F32)
    aux[0:n_bias] = r.bias[layer]
    aux[n_bias : n_bias + n_gain] = r.gain[layer]
    cols[...] = aux[...].T


def put_table(d, lhs, at, n_cat, w1, n_blk, bias_col, first):
    @pl.when(first)
    def _():
        lhs[at : at + d.feat, : d.length] = mm(w1[2 * d.feat :, :].T, n_cat[...], 1, 1).astype(BF)

    own = mm(w1[0 : d.feat, :].T, n_blk, 1, 1) + bias_col
    lhs[at : at + d.feat, d.length :] = own.astype(BF)


def message_part(a1, w2t, b2, att):
    g1, d1 = gelu_pair(a1)
    a2 = mm(w2t, g1) + b2
    g2, d2 = gelu_pair(a2)
    attb = att.astype(BF)
    return g1, d1, g2 * attb, d2 * attb


def add_node_outs(ph, d):
    ph.out_whole(BF, node_out=(d.parts, d.half, d.feat))
    shape = (d.parts, d.half, d.feat)
    ph.out_whole(F32, r1=shape, ip=(d.parts, d.half, d.wide), r2=shape, big=shape, cnt=shape)


def node_step(d, r, p, b, g2m, att, rt):
    big = mm(rt, g2m, 1, 1)
    cnt = mm(rt, jnp.broadcast_to(att.astype(BF), (16, att.shape[1])), 1, 1)
    at = pl.ds(pl.multiple_of(b * d.res, d.res), d.res)
    r.big[p, at, :] = big
    r.cnt[p, at, :] = jnp.broadcast_to(cnt[:, 0:1], big.shape)


def node_forward(r, p, n_own, layer, aux):
    big = r.big[p]
    hi = big.astype(BF)
    lo = (big - hi.astype(F32)).astype(BF)
    w3 = r.mw3[layer]
    upd = (mm(hi, w3) + mm(lo, w3) + r.cnt[p] * aux[2:3]) / 30.0
    r1 = n_own.astype(F32) + upd
    xh1, _ = norm_rows(r1)
    normed = xh1 * aux[10:11] + aux[7:8]
    ip = mm(normed.astype(BF), r.inner[layer]) + r.inner_b[layer]
    hid = gelu_pair_wide(ip)[0].astype(BF)
    r2 = normed + (mm(hid, r.outer[layer]) + aux[3:4])
    xh2, _ = norm_rows(r2)
    out = ((xh2 * aux[11:12] + aux[8:9]) * r.mask[p]).astype(BF)
    r.node_out[p] = out
    r.r1[p] = r1
    r.ip[p] = ip
    r.r2[p] = r2
    return out


def node_backward(d, r, p, layer, aux, dn):
    r1, ip, r2, big, cnt = r.r1[p], r.ip[p], r.r2[p], r.big[p], r.cnt[p]
    xh1, rs1 = norm_rows(r1)
    normed = xh1 * aux[10:11] + aux[7:8]
    xh2, rs2 = norm_rows(r2)
    dy2 = dn * r.mask[p]
    dr2 = norm_back_rows(dy2 * aux[11:12], xh2, rs2)
    low_outer = dr2.astype(BF)
    hid, slope = gelu_pair_wide(ip)
    dip = mm(low_outer, r.outer[layer], 1, 1) * slope
    low_inner = dip.astype(BF)
    at = d.at_outer
    r.msg[at : at + d.wide] += mm(hid.astype(BF), low_outer, 0, 0)
    at = d.at_inner
    r.msg[at : at + d.wide] += mm(low_inner, normed.astype(BF), 0, 0)
    dnormed = dr2 + mm(low_inner, r.inner[layer], 1, 1)
    dr1 = norm_back_rows(dnormed * aux[10:11], xh1, rs1)
    du = dr1 / 30.0
    dub = du.astype(BF)
    r.msg[4 * d.feat : 5 * d.feat] += mm(big.astype(BF), dub, 0, 0)
    dib = jnp.sum(dip, axis=0, keepdims=True)
    rows = {
        2: jnp.sum(cnt * du, axis=0, keepdims=True),
        3: jnp.sum(dr2, axis=0, keepdims=True),
        7: jnp.sum(dnormed, axis=0, keepdims=True),
        8: jnp.sum(dy2, axis=0, keepdims=True),
        10: jnp.sum(dnormed * xh1, axis=0, keepdims=True),
        11: jnp.sum(dy2 * xh2, axis=0, keepdims=True),
    }
    for i in range(d.wide // d.feat):
        rows[16 + i] = dib[:, i * d.feat : (i + 1) * d.feat]
    for row, value in rows.items():
        r.msg[d.at_small + row : d.at_small + row + 1] += value
    r.dr1[...] = dr1
    r.dub[...] = dub


def encoder_message(d, st, n_own, n_got, consts):
    ph = Phase(d, 2)
    ph.whole(n_own=n_own, n_got=n_got, rt=consts.sums, mask=consts.mask)
    ph.stream(tt=st.tt, et=st.et, extra=consts.extra)
    ph.whole(**weight_args(st, *NODE_W, *MSG_W))
    act = (d.parts, d.blocks, d.feat, d.rows)
    ph.out_stream(BF, g1=act, d1=act, d2=act)
    ph.out_stream(F32, att=(d.parts, d.blocks, 1, d.rows))
    add_node_outs(ph, d)
    ph.out_raw(BF, got=(d.half, d.feat))
    sq = (d.feat, d.feat)
    ph.temp(BF, n_cat=(d.length, d.feat), lhs=(d.feat + EXTRA, d.length + d.res), w1bt=sq, w2t=sq)
    ph.temp(BF, leave=(d.half, d.feat))
    ph.temp(F32, aux=sq, cols=sq)
    ph.sems(send=1, recv=1)

    def body(r):
        p, b = pl.program_id(0), pl.program_id(1)
        first, last = b == 0, b == d.blocks - 1
        job = to_partner(r.leave, r.got, r.send.at[0], r.recv.at[0])

        @pl.when(first & (p == 0))
        def _():
            greet_partner()
            r.w1bt[...] = r.mw1[0, d.feat : 2 * d.feat, :].T
            r.w2t[...] = r.mw2[0].T
            load_cols(r, 0, r.aux, r.cols)

        @pl.when(first)
        def _():
            r.n_cat[: d.half] = r.n_own[p]
            r.n_cat[d.half :] = r.n_got[p]

        n_blk = r.n_own[p, pl.ds(pl.multiple_of(b * d.res, d.res), d.res), :]
        put_table(d, r.lhs, 0, r.n_cat, r.mw1.at[0], n_blk, r.cols[:, 0:1], first)
        r.lhs[d.feat :, :] = r.extra[0, 0]
        out = mm(r.lhs[...], r.tt[0, 0])
        a1 = out[: d.feat] + mm(r.w1bt[...], r.et[0, 0])
        att = out[d.feat : d.feat + 1]
        r.att[0, 0] = jnp.where(out[d.feat + 1 : d.feat + 2] < 0.0, 1.0, 0.0)
        r.g1[0, 0], r.d1[0, 0], g2m, r.d2[0, 0] = message_part(a1, r.w2t[...], r.cols[:, 1:2], att)
        node_step(d, r, p, b, g2m, att, r.rt[: d.res])

        @pl.when(last)
        def _():
            out = node_forward(r, p, r.n_own[p], 0, r.aux[...])

            @pl.when(p == 0)
            def _():
                r.leave[...] = out
                job.start()

            @pl.when(p == d.parts - 1)
            def _():
                job.wait()

    return ph.call("enc_message", body)


NODE_W = ("mw3", "inner", "inner_b", "outer", "bias", "gain")
MSG_W = ("mw1", "mw2")
UPD_W = ("uw1", "uw2", "uw3")


def update_forward(a1, edge_t, w2t, w3c, b5, b6c):
    g1, d1 = gelu_pair(a1)
    a2 = mm(w2t, g1) + b5
    g2, d2 = gelu_pair(a2)
    feat = g1.shape[0]
    cent = mm(w3c[:, :feat], g2) + mm(w3c[:, feat:], edge_t) + b6c
    var = jnp.mean(cent * cent, axis=0, keepdims=True)
    rs = lax.rsqrt(var + EPS)
    return g1, d1, g2, d2, cent * rs, rs


def centre_weights(w3, cols, w3c, b6c):
    feat = w3.shape[0]
    eye = lax.broadcasted_iota(jnp.int32, w3.shape, 0) == lax.broadcasted_iota(jnp.int32, w3.shape, 1)
    w3f = w3.astype(F32)
    w3c[:, :feat] = (w3f - jnp.mean(w3f, axis=1, keepdims=True)).T.astype(BF)
    w3c[:, feat:] = (eye.astype(F32) - 1.0 / feat).astype(BF)
    b6 = cols[:, 6:7]
    b6c[...] = jnp.broadcast_to(b6 - jnp.mean(b6, axis=0, keepdims=True), b6c.shape)


def encoder_update(d, st, fa, consts):
    ph = Phase(d, 3)
    ph.whole(n_own=fa.node_out, got_a=fa.got, rt=consts.sums, mask=consts.mask)
    ph.stream(tt=st.tt, et=st.et, att=fa.att)
    ph.whole(**weight_args(st, *NODE_W, *MSG_W, *UPD_W))
    act = (d.parts, d.blocks, d.feat, d.rows)
    ph.out_stream(BF, ug1=act, ud1=act, ug2=act, ud2=act, uxh=act, e2=act, g1=act, d1=act, d2=act)
    ph.out_stream(F32, urs=(d.parts, d.blocks, 1, d.rows))
    add_node_outs(ph, d)
    ph.out_whole(BF, got_in=(d.half, d.feat))
    ph.out_raw(BF, got=(d.parts, d.half, d.feat))
    sq = (d.feat, d.feat)
    ph.temp(BF, n_cat=(d.length, d.feat), lhs=(2 * d.feat, d.length + d.res))
    ph.temp(BF, uw1bt=sq, uw2t=sq, mw1bt=sq, mw2t=sq, w3c=(d.feat, 2 * d.feat))
    ph.temp(BF, leave=(d.parts, d.half, d.feat), lead=(d.half, d.feat), arrive=(d.half, d.feat))
    ph.temp(F32, w3c_b=sq, e_aux=sq, e_cols=sq, d_aux=sq, d_cols=sq)
    ph.sems(send=d.parts + 1, recv=d.parts + 1)

    def body(r):
        p, b = pl.program_id(0), pl.program_id(1)
        first, last = b == 0, b == d.blocks - 1
        early = to_partner(r.lead, r.arrive, r.send.at[d.parts], r.recv.at[d.parts])
        jobs = [to_partner(r.leave.at[i], r.got.at[i], r.send.at[i], r.recv.at[i]) for i in range(d.parts)]

        @pl.when(first & (p == 0))
        def _():
            greet_partner()
            r.lead[...] = r.n_own[d.parts - 1]
            early.start()
            r.uw1bt[...] = r.uw1[0, d.feat : 2 * d.feat, :].T
            r.uw2t[...] = r.uw2[0].T
            r.mw1bt[...] = r.mw1[1, d.feat : 2 * d.feat, :].T
            r.mw2t[...] = r.mw2[1].T
            load_cols(r, 0, r.e_aux, r.e_cols)
            load_cols(r, 1, r.d_aux, r.d_cols)
            centre_weights(r.uw3[0], r.e_cols[...], r.w3c, r.w3c_b)
            r.n_cat[d.half :] = r.got_a[...]

        @pl.when(first & (p == 1))
        def _():
            early.wait()
            r.n_cat[d.half :] = r.arrive[...]
            r.got_in[...] = r.arrive[...]

        @pl.when(first)
        def _():
            r.n_cat[: d.half] = r.n_own[p]

        n_blk = r.n_own[p, pl.ds(pl.multiple_of(b * d.res, d.res), d.res), :]
        put_table(d, r.lhs, 0, r.n_cat, r.uw1.at[0], n_blk, r.e_cols[:, 4:5], first)
        put_table(d, r.lhs, d.feat, r.n_cat, r.mw1.at[1], n_blk, r.d_cols[:, 0:1], first)
        out = mm(r.lhs[...], r.tt[0, 0])
        et = r.et[0, 0]
        a1 = out[: d.feat] + mm(r.uw1bt[...], et)
        g1, d1, g2, d2, xh, rs = update_forward(a1, et, r.uw2t[...], r.w3c, r.e_cols[:, 5:6], r.w3c_b[:, 0:1])
        r.ug1[0, 0], r.ud1[0, 0], r.ug2[0, 0], r.ud2[0, 0] = g1, d1, g2, d2
        r.uxh[0, 0] = xh.astype(BF)
        r.urs[0, 0] = rs
        e2 = (xh * r.e_cols[:, 12:13] + r.e_cols[:, 9:10]).astype(BF)
        r.e2[0, 0] = e2
        att = r.att[0, 0]
        a1 = out[d.feat :] + mm(r.mw1bt[...], e2)
        r.g1[0, 0], r.d1[0, 0], g2m, r.d2[0, 0] = message_part(a1, r.mw2t[...], r.d_cols[:, 1:2], att)
        node_step(d, r, p, b, g2m, att, r.rt[: d.res])

        @pl.when(last)
        def _():
            r.leave[p] = node_forward(r, p, r.n_own[p], 1, r.d_aux[...])
            for i in range(d.parts):

                @pl.when(p == i)
                def _(i=i):
                    jobs[i].start()

            @pl.when(p == d.parts - 1)
            def _():
                for job in jobs:
                    job.wait()

    return ph.call("enc_update", body)


def spread_nodes(d, acc, sumk, w1, n_cat, grad, grad_at):
    s = acc.astype(BF)
    sk = jnp.concatenate([x[:, : d.res] for x in sumk], axis=1)
    skb = sk.astype(BF)
    far = mm(s, w1[2 * d.feat :].T, 0, 0)
    own = mm(skb, w1[: d.feat].T, 0, 0)
    grad[grad_at + 2 * d.feat : grad_at + 3 * d.feat, :] += mm(n_cat, s, 0, 1)
    grad[grad_at : grad_at + d.feat, :] += mm(n_cat[: d.half], skb, 0, 1)
    return own + far[: d.half], far[d.half :], to_row(sk)


def update_backward(d, r, dr3, g1, d1, g2, d2, w2, w3, edge_t):
    dr3b = dr3.astype(BF)
    r.upd[4 * d.feat : 5 * d.feat] += mm(g2, dr3b, 1, 1)
    r.a_b6[...] += lane_sum(dr3)
    da2 = mm(w3, dr3b) * d2.astype(F32)
    r.a_b5[...] += lane_sum(da2)
    da2b = da2.astype(BF)
    r.upd[3 * d.feat : 4 * d.feat] += mm(g1, da2b, 1, 1)
    da1b = (mm(w2, da2b) * d1.astype(F32)).astype(BF)
    r.upd[d.feat : 2 * d.feat] += mm(edge_t, da1b, 1, 1)
    return da1b, dr3b


def update_small(d, r, b4):
    at = 5 * d.feat
    r.upd[at + 4 : at + 5] += b4

    @pl.when(pl.program_id(0) == d.parts - 1)
    def _():
        for row, acc in ((5, r.a_b5), (6, r.a_b6), (9, r.a_b9), (12, r.a_g2)):
            r.upd[at + row : at + row + 1] += to_row(acc[...])


def zero(*refs):
    for ref in refs:
        ref[...] = jnp.zeros(ref.shape, ref.dtype)


def decoder_update(d, st, fb, cot):
    ph = Phase(d)
    ph.whole(n_own=fb.node_out, n_got=fb.got)
    ph.stream(tt=st.tt, tn=st.tn, e2=fb.e2)
    ph.edges(d, cot=cot)
    ph.whole(**weight_args(st, *UPD_W, *AUX_W))
    ph.out_edges(d, decoded=cot.shape)
    act = (d.parts, d.blocks, d.feat, d.rows)
    ph.out_stream(BF, da1=act, dr3=act)
    ph.out_whole(F32, upd=(d.upd_rows, d.feat), dn_own=(d.parts, d.half, d.feat))
    ph.out_whole(BF, dn_far=(d.parts, d.half, d.feat))
    sq = (d.feat, d.feat)
    ph.temp(BF, n_cat=(d.length, d.feat), lhs=(d.feat, d.length + d.res), w1bt=sq, w2t=sq)
    ph.temp(BF, w3c=(d.feat, 2 * d.feat))
    ph.temp(F32, w3c_b=sq, aux=sq, cols=sq, a_b5=sq, a_b6=sq, a_b9=sq, a_g2=sq)
    ph.temp(F32, a_s=(d.feat, d.length), a_k=(d.blocks, d.feat, 128))

    def body(r):
        p, b = pl.program_id(0), pl.program_id(1)
        first, last = b == 0, b == d.blocks - 1

        @pl.when(first & (p == 0))
        def _():
            r.w1bt[...] = r.uw1[1, d.feat : 2 * d.feat, :].T
            r.w2t[...] = r.uw2[1].T
            load_cols(r, 1, r.aux, r.cols)
            centre_weights(r.uw3[1], r.cols[...], r.w3c, r.w3c_b)
            zero(r.upd, r.a_b5, r.a_b6, r.a_b9, r.a_g2)

        @pl.when(first)
        def _():
            r.n_cat[: d.half] = r.n_own[p]
            r.n_cat[d.half :] = r.n_got[p]
            zero(r.a_s)

        n_blk = r.n_own[p, pl.ds(pl.multiple_of(b * d.res, d.res), d.res), :]
        put_table(d, r.lhs, 0, r.n_cat, r.uw1.at[1], n_blk, r.cols[:, 4:5], first)
        e2 = r.e2[0, 0]
        a1 = mm(r.lhs[...], r.tt[0, 0]) + mm(r.w1bt[...], e2)
        g1, d1, g2, d2, xh, rs = update_forward(a1, e2, r.w2t[...], r.w3c, r.cols[:, 5:6], r.w3c_b[:, 0:1])
        y = (xh * r.cols[:, 12:13] + r.cols[:, 9:10]).astype(BF)
        r.decoded[0] = y.T.reshape(d.res, d.near, d.feat)
        dy = r.cot[0].reshape(d.rows, d.feat).T.astype(F32)
        r.a_b9[...] += lane_sum(dy)
        r.a_g2[...] += lane_sum(dy * xh)
        dr3 = norm_back(dy, xh, rs, r.cols[:, 12:13])
        da1b, dr3b = update_backward(d, r, dr3, g1, d1, g2, d2, r.uw2[1], r.uw3[1], e2)
        r.da1[0, 0] = da1b
        r.dr3[0, 0] = dr3b
        spread = mm(da1b, r.tn[0, 0])
        r.a_s[...] += spread[:, : d.length]
        r.a_k[b] = spread[:, d.length :]

        @pl.when(last)
        def _():
            own, far, b4 = spread_nodes(
                d, r.a_s[...], [r.a_k[i] for i in range(d.blocks)], r.uw1[1], r.n_cat[...], r.upd, 0
            )
            r.dn_own[p] = own
            r.dn_far[p] = far.astype(BF)
            update_small(d, r, b4)

    return ph.call("dec_update", body)


AUX_W = ("bias", "gain")


def message_backward(d, r, b, layer, d2m, g1, d1, edge_t):
    at = pl.ds(pl.multiple_of(b * d.res, d.res), d.res)
    v = mm(r.mw3[layer], r.dub[at, :], 1, 1).astype(BF)
    da2 = mm(v, r.rt[: d.res]) * d2m.astype(F32)
    r.a_b1[...] += lane_sum(da2)
    da2b = da2.astype(BF)
    r.msg[3 * d.feat : 4 * d.feat] += mm(g1, da2b, 1, 1)
    da1b = (mm(r.mw2[layer], da2b) * d1.astype(F32)).astype(BF)
    r.msg[d.feat : 2 * d.feat] += mm(edge_t, da1b, 1, 1)
    return da1b


def message_small(d, r, b0):
    at = d.at_small
    r.msg[at : at + 1] += b0

    @pl.when(pl.program_id(0) == d.parts - 1)
    def _():
        r.msg[at + 1 : at + 2] += to_row(r.a_b1[...])


def middle_backward(d, st, fa, fb, fd, cot_n, consts):
    ph = Phase(d, 4)
    ph.whole(cot_n=cot_n, dn_a=fd.dn_own, dn_far_in=fd.dn_far, n_own=fa.node_out, got_a=fa.got, got_b=fb.got_in)
    ph.whole(mask=consts.mask, rt=consts.sums, r1=fb.r1, ip=fb.ip, r2=fb.r2, big=fb.big, cnt=fb.cnt)
    ph.stream(tn=st.tn, et=st.et, ug1=fb.ug1, ud1=fb.ud1, ug2=fb.ug2, ud2=fb.ud2, uxh=fb.uxh, urs=fb.urs)
    ph.stream(e2=fb.e2, g1=fb.g1, d1=fb.d1, d2=fb.d2, dec_da1=fd.da1, dec_dr3=fd.dr3)
    ph.whole(**weight_args(st, *NODE_W, *MSG_W, *UPD_W))
    act = (d.parts, d.blocks, d.feat, d.rows)
    ph.out_stream(BF, da1=act, dr3=act)
    ph.out_whole(F32, msg=(d.msg_rows, d.feat), upd=(d.upd_rows, d.feat), dn_own=(d.parts, d.half, d.feat))
    ph.out_raw(BF, got=(d.parts, d.half, d.feat))
    sq = (d.feat, d.feat)
    ph.temp(BF, n_cat=(d.length, d.feat), dub=(d.half, d.feat), back=(d.feat, 2 * d.feat))
    ph.temp(BF, both=(2 * d.feat, d.rows), leave=(d.parts, d.half, d.feat), arrive=(d.parts, d.half, d.feat))
    ph.temp(F32, dr1=(d.half, d.feat), e_aux=sq, e_cols=sq, d_aux=sq, d_cols=sq)
    ph.temp(F32, a_b1=sq, a_b5=sq, a_b6=sq, a_b9=sq, a_g2=sq)
    ph.temp(F32, a_s=(2 * d.feat, d.length), a_k=(d.blocks, 2 * d.feat, 128))
    ph.sems(send=2 * d.parts, recv=2 * d.parts)

    def body(r):
        p, b = pl.program_id(0), pl.program_id(1)
        first, last = b == 0, b == d.blocks - 1
        n = d.parts
        early = [to_partner(r.dn_far_in.at[i], r.arrive.at[i], r.send.at[n + i], r.recv.at[n + i]) for i in range(n)]
        jobs = [to_partner(r.leave.at[i], r.got.at[i], r.send.at[i], r.recv.at[i]) for i in range(n)]

        @pl.when(first & (p == 0))
        def _():
            greet_partner()
            for job in early:
                job.start()
            load_cols(r, 0, r.e_aux, r.e_cols)
            load_cols(r, 1, r.d_aux, r.d_cols)
            r.back[:, : d.feat] = r.mw1[1, d.feat : 2 * d.feat, :]
            r.back[:, d.feat :] = r.uw1[1, d.feat : 2 * d.feat, :]
            zero(r.msg, r.upd, r.a_b1, r.a_b5, r.a_b6, r.a_b9, r.a_g2)
            r.n_cat[d.half :] = r.got_a[...]

        @pl.when(first & (p == 1))
        def _():
            r.n_cat[d.half :] = r.got_b[...]

        for i in range(n):

            @pl.when(first & (p == i))
            def _(i=i):
                early[i].wait()

        @pl.when(first)
        def _():
            r.n_cat[: d.half] = r.n_own[p]
            zero(r.a_s)
            dn = r.cot_n[p].astype(F32) + r.dn_a[p] + r.arrive[p].astype(F32)
            node_backward(d, r, p, 1, r.d_aux[...], dn)

        e2 = r.e2[0, 0]
        da1m = message_backward(d, r, b, 1, r.d2[0, 0], r.g1[0, 0], r.d1[0, 0], e2)
        de = mm(r.back[:, : d.feat], da1m) + mm(r.back[:, d.feat :], r.dec_da1[0, 0])
        dy = (de + r.dec_dr3[0, 0].astype(F32)).astype(BF).astype(F32)
        xh = r.uxh[0, 0].astype(F32)
        r.a_b9[...] += lane_sum(dy)
        r.a_g2[...] += lane_sum(dy * xh)
        dr3 = norm_back(dy, xh, r.urs[0, 0], r.e_cols[:, 12:13])
        da1u, dr3b = update_backward(
            d, r, dr3, r.ug1[0, 0], r.ud1[0, 0], r.ug2[0, 0], r.ud2[0, 0], r.uw2[0], r.uw3[0], r.et[0, 0]
        )
        r.da1[0, 0] = da1u
        r.dr3[0, 0] = dr3b
        r.both[: d.feat] = da1m
        r.both[d.feat :] = da1u
        spread = mm(r.both[...], r.tn[0, 0])
        r.a_s[...] += spread[:, : d.length]
        r.a_k[b] = spread[:, d.length :]

        @pl.when(last)
        def _():
            n_cat = r.n_cat[...]
            a_k = [r.a_k[i] for i in range(d.blocks)]
            own_m, far_m, b0 = spread_nodes(
                d, r.a_s[: d.feat], [x[: d.feat] for x in a_k], r.mw1[1], n_cat, r.msg, 0
            )
            own_u, far_u, b4 = spread_nodes(
                d, r.a_s[d.feat :], [x[d.feat :] for x in a_k], r.uw1[0], n_cat, r.upd, 0
            )
            r.dn_own[p] = own_m + own_u + r.dr1[...]
            r.leave[p] = (far_m + far_u).astype(BF)
            for i in range(n):

                @pl.when(p == i)
                def _(i=i):
                    jobs[i].start()

            message_small(d, r, b0)
            update_small(d, r, b4)

            @pl.when(p == n - 1)
            def _():
                for job in jobs:
                    job.wait()

    return ph.call("dec_message_back", body)


def encoder_message_back(d, st, fa, fe, n_own, n_got, shape, consts):
    ph = Phase(d)
    ph.whole(dn_a=fe.dn_own, dn_b=fe.got, n_own=n_own, n_got=n_got)
    ph.whole(mask=consts.mask, rt=consts.sums, r1=fa.r1, ip=fa.ip, r2=fa.r2, big=fa.big, cnt=fa.cnt)
    ph.stream(tn=st.tn, et=st.et, g1=fa.g1, d1=fa.d1, d2=fa.d2, up_da1=fe.da1, up_dr3=fe.dr3)
    ph.whole(uw1=st.uw1, **weight_args(st, *NODE_W, *MSG_W))
    ph.out_edges(d, edge_grad=shape)
    ph.out_whole(F32, msg=(d.msg_rows, d.feat), dn_own=(d.parts, d.half, d.feat))
    ph.out_whole(BF, dn_far=(d.parts, d.half, d.feat))
    sq = (d.feat, d.feat)
    ph.temp(BF, n_cat=(d.length, d.feat), dub=(d.half, d.feat), back=(d.feat, 2 * d.feat))
    ph.temp(F32, dr1=(d.half, d.feat), aux=sq, cols=sq, a_b1=sq)
    ph.temp(F32, a_s=(d.feat, d.length), a_k=(d.blocks, d.feat, 128))

    def body(r):
        p, b = pl.program_id(0), pl.program_id(1)
        first, last = b == 0, b == d.blocks - 1

        @pl.when(first & (p == 0))
        def _():
            load_cols(r, 0, r.aux, r.cols)
            r.back[:, : d.feat] = r.mw1[0, d.feat : 2 * d.feat, :]
            r.back[:, d.feat :] = r.uw1[0, d.feat : 2 * d.feat, :]
            zero(r.msg, r.a_b1)

        @pl.when(first)
        def _():
            r.n_cat[: d.half] = r.n_own[p]
            r.n_cat[d.half :] = r.n_got[p]
            zero(r.a_s)
            node_backward(d, r, p, 0, r.aux[...], r.dn_a[p] + r.dn_b[p].astype(F32))

        da1m = message_backward(d, r, b, 0, r.d2[0, 0], r.g1[0, 0], r.d1[0, 0], r.et[0, 0])
        de = mm(r.back[:, : d.feat], da1m) + mm(r.back[:, d.feat :], r.up_da1[0, 0])
        de = (de + r.up_dr3[0, 0].astype(F32)).astype(BF)
        r.edge_grad[0] = de.T.reshape(d.res, d.near, d.feat)
        spread = mm(da1m, r.tn[0, 0])
        r.a_s[...] += spread[:, : d.length]
        r.a_k[b] = spread[:, d.length :]

        @pl.when(last)
        def _():
            own, far, b0 = spread_nodes(
                d, r.a_s[...], [r.a_k[i] for i in range(d.blocks)], r.mw1[0], r.n_cat[...], r.msg, 0
            )
            r.dn_own[p] = own + r.dr1[...]
            r.dn_far[p] = far.astype(BF)
            message_small(d, r, b0)

    return ph.call("enc_message_back", body)


def reduce_grads(d, enc_msg, enc_upd, dec_msg, dec_upd, dn_far):
    devices = d.devices
    bits = devices.bit_length() - 1
    unit = 16 * devices
    rows = -(-(d.msg_rows + d.upd_rows) // unit) * unit
    feat = d.feat
    sizes = [rows >> (i + 1) for i in range(bits)]

    def kernel(em, eu, dm, du, far, res, got, acc, *rest):
        halves = rest[: 2 * bits]
        sec_send, sec_recv, gathered, send, recv = rest[2 * bits :]
        section, me = lax.axis_index(AXIS_S), lax.axis_index(AXIS_D)

        def dp_peer(bit):
            flag = lax.rem(me // (1 << bit), 2)
            return {AXIS_D: me + (1 - 2 * flag) * (1 << bit)}, flag

        barrier = pltpu.get_barrier_semaphore()
        pl.semaphore_signal(barrier, inc=1, device_id=other_section(), device_id_type=MESH)
        for bit in range(bits):
            pl.semaphore_signal(barrier, inc=1, device_id=dp_peer(bit)[0], device_id_type=MESH)
        pl.semaphore_wait(barrier, bits + 1)

        def remote(src, dst, at, peer):
            return pltpu.make_async_remote_copy(
                src_ref=src, dst_ref=dst, send_sem=send.at[at], recv_sem=recv.at[at],
                device_id=peer, device_id_type=MESH,
            )

        nodes = remote(far, got, 0, other_section())
        nodes.start()
        m, u = d.msg_rows, d.upd_rows
        for layer, (msg, upd) in enumerate(((em, eu), (dm, du))):
            acc[layer, :m] = msg[...]
            acc[layer, m : m + u] = upd[...]
            if rows > m + u:
                acc[layer, m + u :] = jnp.zeros((rows - m - u, feat), F32)

        start = 0
        for step in range(bits):
            peer, flag = dp_peer(step)
            size = sizes[step]
            keep = pl.multiple_of(start + flag * size, 16)
            give = pl.multiple_of(start + (1 - flag) * size, 16)
            out, into = halves[2 * step], halves[2 * step + 1]
            if step == 0:
                out[...] = acc[:, pl.ds(give, size), :].astype(BF)
            else:
                out[...] = acc[section, pl.ds(give, size), :].astype(BF)
            job = remote(out, into, 1 + step, peer)
            job.start()
            job.wait()
            if step == 0:
                acc[:, pl.ds(keep, size), :] += into[...].astype(F32)
                sec_send[...] = acc[1 - section, pl.ds(keep, size), :].astype(BF)
                job = remote(sec_send, sec_recv, 1 + bits, other_section())
                job.start()
                job.wait()
                acc[section, pl.ds(keep, size), :] += sec_recv[...].astype(F32)
            else:
                acc[section, pl.ds(keep, size), :] += into[...].astype(F32)
            start = keep
        if bits == 0:
            sec_send[...] = acc[1 - section].astype(BF)
            job = remote(sec_send, sec_recv, 1 + bits, other_section())
            job.start()
            job.wait()
            acc[section] += sec_recv[...].astype(F32)
        size = sizes[-1] if bits else rows
        gathered[pl.ds(pl.multiple_of(start, 16), size), :] = acc[section, pl.ds(pl.multiple_of(start, 16), size), :].astype(BF)
        for step in reversed(range(bits)):
            peer, flag = dp_peer(step)
            size = sizes[step]
            part = gathered.at[pl.ds(pl.multiple_of(start, 16), size), :]
            job = remote(part, part, 2 + bits + step, peer)
            job.start()
            job.wait()
            start = start - flag * size
        res[...] = gathered[...]
        nodes.wait()

    vm = pl.BlockSpec(memory_space=pltpu.VMEM)
    scratch = [pltpu.VMEM((2, rows, feat), F32)]
    for step in range(bits):
        shape = (2, sizes[0], feat) if step == 0 else (sizes[step], feat)
        scratch += [pltpu.VMEM(shape, BF)] * 2
    across = sizes[0] if bits else rows
    scratch += [pltpu.VMEM((across, feat), BF)] * 2 + [pltpu.VMEM((rows, feat), BF)]
    scratch += [pltpu.SemaphoreType.DMA((2 * bits + 2,))] * 2
    return pl.pallas_call(
        kernel,
        in_specs=[vm] * 5,
        out_specs=[vm, pl.BlockSpec(memory_space=pl.ANY)],
        out_shape=[
            jax.ShapeDtypeStruct((rows, feat), BF),
            jax.ShapeDtypeStruct(dn_far.shape, BF),
        ],
        scratch_shapes=scratch,
        compiler_params=pltpu.CompilerParams(vmem_limit_bytes=58 << 20, collective_id=5, has_side_effects=True),
        name="reduce",
    )(enc_msg, enc_upd, dec_msg, dec_upd, dn_far)


def unpack(d, total, dn_own, dn_got, n_bias, n_gain):
    f = d.feat
    m = d.msg_rows
    shapes = [(1, 3 * f, f), (1, f, f), (1, f, f), (1, f, d.wide), (1, 1, d.wide), (1, d.wide, f)]
    shapes += [(1, 3 * f, f), (1, f, f), (1, f, f), (1, n_bias, f), (1, n_gain, f)]

    def kernel(t, own, got, node, mw1, mw2, mw3, inner, inner_b, outer, uw1, uw2, uw3, bias, gain):
        node[...] = (own[...] + got[...].astype(F32)).astype(BF)
        for ref, at in ((mw1, 0), (mw2, 3 * f), (mw3, 4 * f), (outer, d.at_outer)):
            ref[0] = t[at : at + ref.shape[1], :].astype(F32)
        for ref, at in ((uw1, m), (uw2, m + 3 * f), (uw3, m + 4 * f)):
            ref[0] = t[at : at + ref.shape[1], :].astype(F32)
        inner[0] = t[d.at_inner : d.at_inner + d.wide, :].astype(F32).T
        small = t[d.at_small : d.at_small + SMALL, :].astype(F32)
        other = t[m + 5 * f : m + 5 * f + SMALL, :].astype(F32)
        both = small + other
        bias[0] = both[:n_bias]
        gain[0] = both[n_bias : n_bias + n_gain]
        for i in range(d.wide // f):
            inner_b[0, :, i * f : (i + 1) * f] = small[16 + i : 17 + i]

    vm = pl.BlockSpec(memory_space=pltpu.VMEM)
    out = [jax.ShapeDtypeStruct(dn_own.shape, BF)] + [jax.ShapeDtypeStruct(s, F32) for s in shapes]
    return pl.pallas_call(kernel, in_specs=[vm] * 3, out_specs=[vm] * len(out), out_shape=out, name="unpack")(
        total, dn_own, dn_got
    )


def per_device(
    node_input,
    edge_input,
    neighbors,
    residue_mask,
    decode_order,
    node_cotangent,
    edge_cotangent,
    message_w1,
    message_w2,
    message_w3,
    inner_w,
    inner_bias,
    outer_w,
    update_w1,
    update_w2,
    update_w3,
    biases,
    norm_gains,
):
    section = lax.axis_index(AXIS_S)
    is_first = section == 0
    parts, half, near, feat = edge_input.shape
    length = neighbors.shape[1]
    wide = inner_w.shape[2]
    res = BLOCK_RES
    rows = res * near
    blocks = half // res
    at_outer = 5 * feat
    at_inner = at_outer + wide
    at_small = at_inner + wide
    d = types.SimpleNamespace(
        parts=parts, half=half, near=near, feat=feat, length=length, wide=wide, res=res, rows=rows, blocks=blocks,
        at_outer=at_outer, at_inner=at_inner, at_small=at_small, msg_rows=at_small + SMALL,
        upd_rows=5 * feat + SMALL, devices=lax.axis_size(AXIS_D),
    )
    weights = dict(
        mw1=message_w1, mw2=message_w2, mw3=message_w3, inner=inner_w, inner_b=inner_bias[:, None, :], outer=outer_w,
        uw1=update_w1, uw2=update_w2, uw3=update_w3, bias=biases, gain=norm_gains,
    )
    own_ids = lax.dynamic_slice_in_dim(neighbors, section * half, half, 1)
    idx_row = own_ids.reshape(parts, blocks, 1, rows)
    sums = np.zeros((128, rows), np.float32)
    sums[np.arange(rows) // near, np.arange(rows)] = 1.0
    sums = jnp.asarray(sums, BF)
    st = prepare(d, idx_row, edge_input, sums, node_input, weights)

    def own_first(x):
        return jnp.where(is_first, x, jnp.roll(x, half, axis=1))

    live = own_first(residue_mask)
    order = own_first(decode_order)
    centre = length // 2
    code = jnp.where(live == 1, order - centre, centre)
    own_code = (order[:, :half] - centre).reshape(parts, blocks, 1, res)
    lead = (parts, blocks, 1, length)
    top = jnp.pad(jnp.broadcast_to(live[:, None, None, :], lead), ((0, 0), (0, 0), (0, 0), (0, res)))
    second = jnp.concatenate([jnp.broadcast_to(code[:, None, None, :], lead), -own_code], axis=3)
    extra = jnp.concatenate([top, second, jnp.zeros((parts, blocks, EXTRA - 2, length + res), top.dtype)], axis=2)
    mask = jnp.broadcast_to(live[:, :half, None].astype(F32), (parts, half, feat))
    consts = types.SimpleNamespace(extra=extra.astype(BF), sums=sums, mask=mask)

    fa = encoder_message(d, st, node_input, st.nodes_got, consts)
    fb = encoder_update(d, st, fa, consts)
    fd = decoder_update(d, st, fb, edge_cotangent)
    fe = middle_backward(d, st, fa, fb, fd, node_cotangent, consts)
    ff = encoder_message_back(d, st, fa, fe, node_input, st.nodes_got, edge_input.shape, consts)
    total, got = reduce_grads(d, ff.msg, fe.upd, fe.msg, fd.upd, ff.dn_far)
    node_grad, mw1, mw2, mw3, inner, inner_b, outer, uw1, uw2, uw3, bias, gain = unpack(
        d, total, ff.dn_own, got, biases.shape[1], norm_gains.shape[1]
    )
    return (
        fb.node_out, fd.decoded, node_grad, ff.edge_grad, mw1, mw2, mw3, inner, inner_b[:, 0], outer,
        uw1, uw2, uw3, bias, gain,
    )


def solution(mesh):
    def split(*axes):
        return P(*axes)

    by_part = split(AXIS_D)
    by_half = split(AXIS_D, AXIS_S)
    by_layer = split(AXIS_S)
    in_specs = (by_half, by_half, by_part, by_part, by_part, by_half, by_half) + (by_layer,) * 11
    out_specs = (by_half,) * 4 + (by_layer,) * 11
    return jax.shard_map(per_device, mesh=mesh, in_specs=in_specs, out_specs=out_specs, check_vma=False)
```

time: 2220 us -> 268 us (0.12)
  matrix products: 874 us -> 0 us
  other arithmetic: 519 us -> 1.57 us
  waiting for transfers between devices: 409 us -> 0 us
  local copies, waits for them, and re-layouts: 312 us -> 9.42 us
  Pallas kernels: 0 us -> 255 us
  blocking collectives: 57.6 us -> 0 us
  starting transfers between devices: 26.2 us -> 0 us
    dot_general x104 -> x0, matrix products: 874 us -> none  [the longest x24 216 us: input_grad(): return jnp.dot(grad_low, weight.T, preferred_element_type=jnp.float32)]
    ppermute x12 -> x0, waiting for transfers between devices: 337 us -> none  [the longest x8 304 us: shifted(): return lax.ppermute(block, axis, route)]
    pallas_call x0 -> x8, Pallas kernels: none -> 255 us  [the longest x6 211 us: call(): pl.pallas_call(kernel, grid=self.grid, in_specs=[s for _, _, s in self.in...]
    reduce_sum x39 -> x0, other arithmetic: 201 us -> none  [the longest x14 79.6 us: layer_norm(): spread_sq = jnp.mean(centered * centered, axis=-1, keepdims=True)]
    concatenate x17 -> x1, local copies, waits for them, and re-layouts: 115 us -> 0.08 us  [per_device(): jnp.concatenate([top, second, jnp.zeros((parts, blocks, EXTRA - 2, length...]
    convert_element_type x22 -> x0, other arithmetic: 99.4 us -> none  [the longest x6 26 us: spread_back(): (rest_one - middle_part.astype(jnp.float32)).astype(jnp.bfloat16)]
    another operation x21 -> x3, other arithmetic: 99 us -> 0.79 us  [the longest x18 88.1 us: per_device(): kept_stack = jax.tree.map(lambda *values: jnp.stack(values), *tick_kept)]
    psum x1 -> x0, waiting for transfers between devices: 72.6 us -> none  [per_device(): lax.psum((grad_total[0], grad_total[1], grad_total[2], grad_total[3], gra...]
  transfers between devices with their start and end apart: 13 -> 0, of which waited for: 6 -> 0; matrix products, arithmetic and copies ran while one was open for 31% -> 0% of each run, Pallas kernels for 0% -> 0%
where the time goes in v1:
time: 268 us; the launch traced here: 267 us
  Pallas kernels  255 us (95%)
  local copies, waits for them, and re-layouts  9.42 us (4%)
    pallas_call x6, Pallas kernels, call(): pl.pallas_call(kernel, grid=self.grid, in_specs=[s for _, _, s in self.in...  211 us
    pallas_call x1, Pallas kernels, reduce_grads(): pl.pallas_call(kernel, in_specs=[vm] * 5, out_specs=[vm, pl.BlockSpec(mem...  42.1 us
    unnamed x11, local copies, waits for them, and re-layouts  5.75 us

profile of v1, /device:TPU:0, one launch (start us, length us, event | category | flops | bytes accessed | tf_op | source)
XLA Modules:
  0.0 267.1 jit_solution(13601980480327979727)
XLA Ops:
  0.6 0.0 copy-start
  0.7 0.1 pad.9.clone
  0.8 1.3 copy.42.refs_14_
  2.0 0.8 fusion.6
  2.8 0.8 fusion.7
  3.7 0.8 fusion.3
  4.5 0.1 neg.16
  4.6 1.3 copy.41.refs_13_
  5.9 0.1 constant_dynamic-slice_fusion
  6.0 0.1 copy.39
  6.1 0.8 reshape.57.refs_0_
  6.9 0.8 fusion.2.refs_6_
  7.7 0.8 broadcast_in_dim.13.refs_3_.refs_6_.refs_4_
  8.5 24.8 %tables.1 = (bf16[2,6,416,1536]{3,2,1,0:T(8,128)(2,1)}, bf16[2,6,1536,512]{3,2,1,0:T(8,128)(2,1)}, bf16[2,6,128,1536]{3,2,1,0:T(8,128)(2,1)}, bf16[2,192,128]{2,...) custom-call(s32[2,6,1,1536]{3,2,1,0:T(1,128)} %reshape.57.refs_0_, ...), custom_call_target="tpu_custom_call" | custom-call | tf_op jit(solution)/shard_map/tables/pallas_call | solution.py:132
  33.3 25.5 %enc_message.1 = (bf16[2,6,128,1536]{3,2,1,0:T(8,128)(2,1)}, bf16[2,6,128,1536]{3,2,1,0:T(8,128)(2,1)}, bf16[2,6,128,1536]{3,2,1,0:T(8,128)(2,1)}, f32[2,6,1,153...) custom-call(bf16[2,192,128]{2,1,0:T(8,128)(2,1)} %refs_2_.4, ...), custom_call_target="tpu_custom_call" | custom-call | tf_op jit(solution)/shard_map/enc_message/pallas_call | solution.py:132
  58.8 44.4 %enc_update.1 = (bf16[2,6,128,1536]{3,2,1,0:T(8,128)(2,1)}, bf16[2,6,128,1536]{3,2,1,0:T(8,128)(2,1)}, bf16[2,6,128,1536]{3,2,1,0:T(8,128)(2,1)}, bf16[2,6,128,1...) custom-call(bf16[2,192,128]{2,1,0:T(8,128)(2,1)} %get-tuple-element., ...), custom_call_target="tpu_custom_call" | custom-call | tf_op jit(solution)/shard_map/enc_update/pallas_call | solution.py:132
  103.2 36.4 %dec_update.1 = (bf16[2,192,48,128]{3,2,1,0:T(8,128)(2,1)}, bf16[2,6,128,1536]{3,2,1,0:T(8,128)(2,1)}, bf16[2,6,128,1536]{3,2,1,0:T(8,128)(2,1)}, f32[672,128]{1...) custom-call(bf16[2,192,128]{2,1,0:T(8,128)(2,1)} %get-tuple-element.217.refs_0_, ...), custom_call_target="tpu_custom_call" | custom-call | tf_op jit(solution)/shard_map/dec_update/pallas_call | solution.py:132
  139.6 51.5 %dec_message_back.1 = (bf16[2,6,128,1536]{3,2,1,0:T(8,128)(2,1)}, bf16[2,6,128,1536]{3,2,1,0:T(8,128)(2,1)}, f32[1696,128]{1,0:T(8,128)}, f32[672,128]{1,0:T(8,1...) custom-call(bf16[2,192,128]{2,1,0:T(8,128)(2,1)} %refs_0_.3, f32[2,192,128]{2,1,0:T(8,128)} %get-tuple-element.111.refs_1_, ...), custom_call_target="tpu_custom_call" | custom-call | tf_op jit(solution)/shard_map/dec_message_back/pallas_call | solution.py:132
  191.1 28.3 %enc_message_back.1 = (bf16[2,192,48,128]{3,2,1,0:T(8,128)(2,1)}, f32[1696,128]{1,0:T(8,128)}, f32[2,192,128]{2,1,0:T(8,128)}, bf16[2,192,128]{2,1,0:T(8,128)(2,1)}) custom-call(f32[2,192,128]{2,1,0:T(8,128)} %get-tuple-element.130.refs_0_, bf16[2,192,128]{2,1,0:T(8,128)(2,1)} %get-tuple-element.131.refs_1_, bf16[2,192,128]{2,1,0:T(8,128)(2,1)} %refs_2_.4, ...), custom_call_target="tpu_custom_call" | custom-call | tf_op jit(solution)/shard_map/enc_message_back/pallas_call | solution.py:132
  219.4 42.1 %reduce.1 = (bf16[2560,128]{1,0:T(8,128)(2,1)}, bf16[2,192,128]{2,1,0:T(8,128)(2,1)}) custom-call(f32[1696,128]{1,0:T(8,128)} %get-tuple-element.142.em, f32[672,128]{1,0:T(8,128)} %get-tuple-element.143.eu, f32[1696,128]{1,0:T(8,128)} %get-tuple-element.144.dm, f32[672,128]{1,0:T(8,128)} %get-tuple-element.145.du, bf16[2,192,128]{2,1,0:T(8,128)(2,1)} %get-tuple-element.146.far), custom_call_target="tpu_custom_call" | custom-call | tf_op jit(solution)/shard_map/reduce/pallas_call | solution.py:869
  261.6 2.3 unpack.1
  263.9 1.2 copy.45
  265.1 1.3 copy.44
  266.4 0.6 copy.47
  (10 shorter events, 0.1 us)
Async XLA Ops:
  0.6 5.2 %copy-start = (s32[2,384,48]{1,2,0:T(8,128)S(1)}, s32[2,384,48]{1,2,0:T(8,128)}, u32[]{:S(2)}) copy-start(s32[2,384,48]{1,2,0:T(8,128)} %param.21) | copy-start | bytes 442372
  191.1 75.3 %copy-start.2 = (bf16[2,192,128]{2,1,0:T(8,128)(2,1)S(1)}, bf16[2,192,128]{2,1,0:T(8,128)(2,1)}, u32[]{:S(2)}) copy-start(bf16[2,192,128]{2,1,0:T(8,128)(2,1)} %get-tuple-element.217.refs_0_) | copy-start | bytes 294916
  191.1 75.9 %copy-start.1 = (s32[2,384,48]{1,2,0:T(8,128)S(1)}, s32[2,384,48]{1,2,0:T(8,128)}, u32[]{:S(2)}) copy-start(s32[2,384,48]{1,2,0:T(8,128)} %param.21) | copy-start | bytes 442372

commit v2 on v1

v2 whole, which is shorter than its diff:
```python
import types

import jax
import jax.numpy as jnp
import numpy as np
from jax import lax
from jax.experimental import pallas as pl
from jax.experimental.pallas import tpu as pltpu
from jax.sharding import PartitionSpec as P

BF = jnp.bfloat16
F32 = jnp.float32
C1 = 0.7978845608
C2 = C1 * 0.044715
EPS = 1e-5
BLOCK_RES = 64
EXTRA = 16
SMALL = 32
MESH = pl.DeviceIdType.MESH


def mm(a, b, ca=1, cb=0):
    return lax.dot_general(a, b, (((ca,), (cb,)), ((), ())), preferred_element_type=F32)


def mm_exact(a, b, ca=1, cb=0):
    return lax.dot_general(
        a, b, (((ca,), (cb,)), ((), ())), precision=lax.Precision.HIGHEST, preferred_element_type=F32
    )


def gelu_pair(x):
    x = x.astype(BF)
    w = x * x * BF(C2)
    h = jnp.tanh(x * (w + BF(C1))) + BF(1.0)
    g = x * h
    d = h + g * (BF(2.0) - h) * (w * BF(3.0) + BF(C1))
    return g, d


def gelu_pair_wide(x):
    x2 = x * x
    h = 0.5 * jnp.tanh(x * (x2 * C2 + C1)) + 0.5
    g = x * h
    d = h + (g * (1.0 - h)) * (x2 * (6 * C2) + 2 * C1)
    return g, d


def lane_sum(x):
    total = x[:, :128]
    for at in range(128, x.shape[1], 128):
        total = total + x[:, at : at + 128]
    return total


def to_row(acc):
    return mm_exact(jnp.ones((8, acc.shape[1]), F32), acc, 1, 1)[0:1]


def norm_rows(r):
    c = r - jnp.mean(r, axis=-1, keepdims=True)
    rs = lax.rsqrt(jnp.mean(c * c, axis=-1, keepdims=True) + EPS)
    return c * rs, rs


def norm_back_rows(dxh, xh, rs):
    m1 = jnp.mean(dxh, axis=-1, keepdims=True)
    m2 = jnp.mean(dxh * xh, axis=-1, keepdims=True)
    return (dxh - m1 - xh * m2) * rs


def norm_back(dy, xh, rs, gain_col):
    dxh = dy * gain_col
    m1 = jnp.mean(dxh, axis=0, keepdims=True)
    m2 = jnp.mean(dxh * xh, axis=0, keepdims=True)
    return (dxh - m1 - xh * m2) * rs


class Refs:
    def __init__(self, plain, slots, waits):
        self.__dict__.update(plain)
        self._slots, self._waits = slots, waits

    def __getattr__(self, name):
        slots = self.__dict__.get(SLOTS, {})
        if name not in slots:
            raise AttributeError(name)
        wait = self._waits.pop(name, None)
        if wait is not None:
            wait()
        return slots[name]


SLOTS = "_slots"


class Phase:
    def __init__(self, dims, collective_id=None):
        self.d = dims
        self.collective_id = collective_id
        self.ins, self.outs, self.temps, self.kinds = [], [], [], {}

    def whole_spec(self, shape):
        rank = len(shape)
        return pl.BlockSpec(tuple(shape), lambda p, b: (0,) * rank)

    def whole(self, **arrays):
        self.ins += [(n, a, self.whole_spec(a.shape)) for n, a in arrays.items()]

    def raw(self, **arrays):
        self.ins += [(n, a, pl.BlockSpec(memory_space=pl.ANY)) for n, a in arrays.items()]

    def stream(self, **arrays):
        self.raw(**arrays)
        self.kinds.update({n: (False, False, a.shape[2:], a.dtype) for n, a in arrays.items()})

    def edges(self, **arrays):
        self.raw(**arrays)
        block = (self.d.res, self.d.near, self.d.feat)
        self.kinds.update({n: (False, True, block, a.dtype) for n, a in arrays.items()})

    def out_whole(self, dtype, **shapes):
        self.outs += [(n, jax.ShapeDtypeStruct(s, dtype), self.whole_spec(s)) for n, s in shapes.items()]

    def out_raw(self, dtype, **shapes):
        spec = pl.BlockSpec(memory_space=pl.ANY)
        self.outs += [(n, jax.ShapeDtypeStruct(s, dtype), spec) for n, s in shapes.items()]

    def out_stream(self, dtype, **shapes):
        self.out_raw(dtype, **shapes)
        self.kinds.update({n: (True, False, s[2:], dtype) for n, s in shapes.items()})

    def out_edges(self, **shapes):
        self.out_raw(BF, **shapes)
        block = (self.d.res, self.d.near, self.d.feat)
        self.kinds.update({n: (True, True, block, BF) for n in shapes})

    def temp(self, dtype, **shapes):
        self.temps += [(n, pltpu.VMEM(s, dtype)) for n, s in shapes.items()]

    def sems(self, **counts):
        self.temps += [(n, pltpu.SemaphoreType.DMA((c,))) for n, c in counts.items()]

    def call(self, name, body):
        d = self.d
        names = [n for n, _, _ in self.ins] + [n for n, _, _ in self.outs] + [n for n, _ in self.temps]
        steps = d.parts * d.blocks
        buffers = [pltpu.VMEM((2,) + tuple(block), dtype) for _, _, block, dtype in self.kinds.values()]
        count = len(self.kinds)

        def kernel(*refs):
            refs, slots, sems = refs[: len(names)], refs[len(names) : len(names) + count], refs[len(names) + count :]
            plain = dict(zip(names, refs))
            step = pl.program_id(0) * d.blocks + pl.program_id(1)
            now = lax.rem(step, 2)

            def copy(i, n, at, slot):
                out, edges, _, _ = self.kinds[n]
                p, b = at // d.blocks, lax.rem(at, d.blocks)
                if edges:
                    far = plain[n].at[p, pl.ds(pl.multiple_of(b * d.res, d.res), d.res)]
                else:
                    far = plain[n].at[p, b]
                near = slots[i].at[slot]
                return pltpu.make_async_copy(*((near, far) if out else (far, near)), sems[i].at[slot])

            into = [(i, n) for i, n in enumerate(self.kinds) if not self.kinds[n][0]]
            outof = [(i, n) for i, n in enumerate(self.kinds) if self.kinds[n][0]]

            @pl.when(step == 0)
            def _():
                for i, n in into:
                    copy(i, n, step, now).start()

            @pl.when(step + 1 < steps)
            def _():
                for i, n in into:
                    copy(i, n, step + 1, 1 - now).start()

            @pl.when(step >= 2)
            def _():
                for i, n in outof:
                    copy(i, n, step - 2, now).wait()

            waits = {n: copy(i, n, step, now).wait for i, n in into}
            named = {n: slots[i].at[now] for i, n in enumerate(self.kinds)}
            body(Refs({n: x for n, x in plain.items() if n not in named}, named, waits))
            for wait in waits.values():
                wait()
            for i, n in outof:
                copy(i, n, step, now).start()

            @pl.when(step == steps - 1)
            def _():
                for i, n in outof:
                    if steps > 1:
                        copy(i, n, step - 1, 1 - now).wait()
                    copy(i, n, step, now).wait()

        results = pl.pallas_call(
            kernel,
            grid=(d.parts, d.blocks),
            in_specs=[s for _, _, s in self.ins],
            out_specs=[s for _, _, s in self.outs],
            out_shape=[s for _, s, _ in self.outs],
            scratch_shapes=[s for _, s in self.temps] + buffers + [pltpu.SemaphoreType.DMA((2,))] * count,
            compiler_params=pltpu.CompilerParams(
                dimension_semantics=(pltpu.ARBITRARY,) * 2,
                vmem_limit_bytes=60 << 20,
                collective_id=self.collective_id,
                has_side_effects=self.collective_id is not None,
            ),
            name=name,
        )(*[a for _, a, _ in self.ins])
        return types.SimpleNamespace(**dict(zip([n for n, _, _ in self.outs], results)))


def other_section():
    return {AXIS_S: 1 - lax.axis_index(AXIS_S)}


AXIS_S = "section"
AXIS_D = "dp"


def greet_partner():
    barrier = pltpu.get_barrier_semaphore()
    pl.semaphore_signal(barrier, inc=1, device_id=other_section(), device_id_type=MESH)
    pl.semaphore_wait(barrier, 1)


def to_partner(src, dst, send, recv):
    return pltpu.make_async_remote_copy(
        src_ref=src, dst_ref=dst, send_sem=send, recv_sem=recv, device_id=other_section(), device_id_type=MESH
    )


def put_one_hot(d, ref, at, idx):
    idx = idx.astype(jnp.int16)
    place = lax.broadcasted_iota(jnp.int16, (d.length, d.rows), 0)
    ref[at : at + d.length, :] = jnp.where(place == idx, jnp.ones((), BF), jnp.zeros((), BF))


def put_one_hot_rows(d, ref, idx):
    centre = d.length // 2
    idx = jnp.broadcast_to((idx - centre).astype(F32).astype(BF), (128, d.rows)).T
    place = lax.broadcasted_iota(jnp.int32, (d.rows, 128), 1)
    for at in range(0, d.length, 128):
        there = (place + (at - centre)).astype(F32).astype(BF)
        ref[:, at : at + 128] = jnp.where(idx == there, jnp.ones((), BF), jnp.zeros((), BF))


def weight_args(w, *names):
    return {n: getattr(w, n) for n in names}


def load_cols(r, layer, aux, cols):
    n_bias, n_gain = r.bias.shape[1], r.gain.shape[1]
    aux[...] = jnp.zeros(aux.shape, F32)
    for i in range(n_bias):
        aux[i : i + 1] = r.bias[layer, i]
    for i in range(n_gain):
        aux[n_bias + i : n_bias + i + 1] = r.gain[layer, i]
    cols[...] = aux[...].T


def put_table(d, lhs, at, left, n_cat, w1, n_blk, bias_col, first):
    @pl.when(first)
    def _():
        lhs[at : at + d.feat, left : left + d.length] = mm(w1[2 * d.feat :, :].T, n_cat[...], 1, 1).astype(BF)

    own = mm(w1[0 : d.feat, :].T, n_blk, 1, 1) + bias_col
    lhs[at : at + d.feat, left + d.length :] = own.astype(BF)


def message_part(a1, w2t, b2, att):
    g1, d1 = gelu_pair(a1)
    a2 = mm(w2t, g1) + b2
    g2, d2 = gelu_pair(a2)
    attb = att.astype(BF)
    return g1, d1, g2 * attb, d2 * attb


def add_node_outs(ph, d):
    ph.out_whole(BF, node_out=(d.parts, d.half, d.feat))
    shape = (d.parts, d.half, d.feat)
    ph.out_whole(F32, r1=shape, ip=(d.parts, d.half, d.wide), r2=shape, big=shape, cnt=shape)


def node_step(d, r, p, b, g2m, att, rt):
    big = mm(rt, g2m, 1, 1) * 0.5
    cnt = mm(rt, jnp.broadcast_to(att.astype(BF), (16, att.shape[1])), 1, 1)
    at = pl.ds(pl.multiple_of(b * d.res, d.res), d.res)
    r.big[p, at, :] = big
    r.cnt[p, at, :] = jnp.broadcast_to(cnt[:, 0:1], big.shape)


def node_forward(r, p, n_own, layer, aux):
    big = r.big[p]
    hi = big.astype(BF)
    lo = (big - hi.astype(F32)).astype(BF)
    w3 = r.mw3[layer]
    upd = (mm(hi, w3) + mm(lo, w3) + r.cnt[p] * aux[2:3]) / 30.0
    r1 = n_own.astype(F32) + upd
    xh1, _ = norm_rows(r1)
    normed = xh1 * aux[10:11] + aux[7:8]
    ip = mm(normed.astype(BF), r.inner[layer]) + r.inner_b[layer]
    hid = gelu_pair_wide(ip)[0].astype(BF)
    r2 = normed + (mm(hid, r.outer[layer]) + aux[3:4])
    xh2, _ = norm_rows(r2)
    out = ((xh2 * aux[11:12] + aux[8:9]) * r.mask[p]).astype(BF)
    r.node_out[p] = out
    r.r1[p] = r1
    r.ip[p] = ip
    r.r2[p] = r2
    return out


def node_backward(d, r, p, layer, aux, dn):
    r1, ip, r2, big, cnt = r.r1[p], r.ip[p], r.r2[p], r.big[p], r.cnt[p]
    xh1, rs1 = norm_rows(r1)
    normed = xh1 * aux[10:11] + aux[7:8]
    xh2, rs2 = norm_rows(r2)
    dy2 = dn * r.mask[p]
    dr2 = norm_back_rows(dy2 * aux[11:12], xh2, rs2)
    low_outer = dr2.astype(BF)
    hid, slope = gelu_pair_wide(ip)
    dip = mm(low_outer, r.outer[layer], 1, 1) * slope
    low_inner = dip.astype(BF)
    at = d.at_outer
    r.msg[at : at + d.wide] += mm(hid.astype(BF), low_outer, 0, 0)
    at = d.at_inner
    r.msg[at : at + d.wide] += mm(low_inner, normed.astype(BF), 0, 0)
    dnormed = dr2 + mm(low_inner, r.inner[layer], 1, 1)
    dr1 = norm_back_rows(dnormed * aux[10:11], xh1, rs1)
    du = dr1 / 30.0
    dub = du.astype(BF)
    r.msg[4 * d.feat : 5 * d.feat] += mm(big.astype(BF), dub, 0, 0)
    dib = jnp.sum(dip, axis=0, keepdims=True)
    rows = {
        2: jnp.sum(cnt * du, axis=0, keepdims=True),
        3: jnp.sum(dr2, axis=0, keepdims=True),
        7: jnp.sum(dnormed, axis=0, keepdims=True),
        8: jnp.sum(dy2, axis=0, keepdims=True),
        10: jnp.sum(dnormed * xh1, axis=0, keepdims=True),
        11: jnp.sum(dy2 * xh2, axis=0, keepdims=True),
    }
    for i in range(d.wide // d.feat):
        rows[16 + i] = dib[:, i * d.feat : (i + 1) * d.feat]
    for row, value in rows.items():
        r.msg[d.at_small + row : d.at_small + row + 1] += value
    r.dr1[...] = dr1
    r.dub[...] = dub


def encoder_message(d, edge_input, node_input, weights, consts):
    ph = Phase(d, 2)
    ph.whole(n_own=node_input, idx=consts.idx, rt=consts.sums, mask=consts.mask, extra=consts.extra)
    ph.edges(edge=edge_input)
    names = tuple(weights)
    own = {W_IN + n: a for n, a in weights.items()}
    ph.raw(**own)
    act = (d.parts, d.blocks, d.feat, d.rows)
    ph.out_stream(BF, g1=with_ones(d), d1=act, d2=act)
    ph.out_whole(F32, att=(d.parts, d.blocks, 1, d.rows))
    add_node_outs(ph, d)
    ph.out_raw(BF, got=(d.half, d.feat), nodes_got=node_input.shape)
    for n, a in weights.items():
        ph.out_raw(a.dtype, **{W_OUT + n: (2,) + a.shape})
        ph.temp(a.dtype, **{n: (2,) + a.shape})
    sq = (d.feat, d.feat)
    wide = d.feat + d.length + d.res
    ph.temp(BF, n_cat=(d.length, d.feat), lhs=(d.feat + EXTRA, wide), w2t=sq, tt=(wide, d.rows))
    ph.temp(BF, leave=(d.half, d.feat), arrive=node_input.shape)
    ph.temp(F32, aux=sq, cols=sq)
    count = len(names)
    ph.sems(send=count + 2, recv=count + 2, local=count, back=2 * count + 1)

    def body(r):
        p, b = pl.program_id(0), pl.program_id(1)
        first, last = b == 0, b == d.blocks - 1
        section = lax.axis_index(AXIS_S)
        job = to_partner(r.leave, r.got, r.send.at[count], r.recv.at[count])
        nodes = to_partner(r.n_own, r.arrive, r.send.at[count + 1], r.recv.at[count + 1])

        def swaps(group):
            out = []
            for n in group:
                i = names.index(n)
                dst = getattr(r, n).at[section]
                out.append(to_partner(getattr(r, W_IN + n), dst, r.send.at[i], r.recv.at[i]))
            return out

        def own_copies():
            return [
                pltpu.make_async_copy(getattr(r, W_IN + n), getattr(r, n).at[section], r.local.at[i])
                for i, n in enumerate(names)
            ]

        def returns():
            out = [pltpu.make_async_copy(r.arrive, r.nodes_got, r.back.at[2 * count])]
            for i, n in enumerate(names):
                src, dst = getattr(r, n), getattr(r, W_OUT + n)
                for layer in range(2):
                    sem = r.back.at[2 * i + layer]
                    out.append(pltpu.make_async_copy(src.at[layer], dst.at[layer], sem))
            return out

        begin = first & (p == 0)
        middle = (p == 1) & (b == 1)
        at_end = last & (p == d.parts - 1)

        @pl.when(begin)
        def _():
            greet_partner()
            nodes.start()
            for item in swaps(GROUP_ONE) + own_copies():
                item.start()
            r.tt[d.feat + d.length :, :] = r.rt[: d.res]

        put_one_hot(d, r.tt, d.feat, r.idx[p, b])
        r.tt[: d.feat, :] = r.edge[...].reshape(d.rows, d.feat).T

        @pl.when(begin)
        def _():
            nodes.wait()
            for item in swaps(GROUP_ONE) + own_copies():
                item.wait()
            for item in swaps(GROUP_TWO):
                item.start()
            r.lhs[: d.feat, : d.feat] = r.mw1[0, d.feat : 2 * d.feat, :].T
            r.lhs[d.feat :, : d.feat] = jnp.zeros((EXTRA, d.feat), BF)
            r.w2t[...] = half_of(r.mw2[0]).T
            load_cols(r, 0, r.aux, r.cols)

        @pl.when(first)
        def _():
            r.n_cat[: d.half] = r.n_own[p]
            r.n_cat[d.half :] = r.arrive[p]

        n_blk = r.n_own[p, pl.ds(pl.multiple_of(b * d.res, d.res), d.res), :]
        put_table(d, r.lhs, 0, d.feat, r.n_cat, r.mw1.at[0], n_blk, r.cols[:, 0:1], first)
        r.lhs[d.feat :, d.feat :] = r.extra[p, b]
        out = mm(r.lhs[...], r.tt[...])
        att = out[d.feat : d.feat + 1]
        r.att[p, b] = jnp.where(out[d.feat + 1 : d.feat + 2] < 0.0, 1.0, 0.0)
        g1, r.d1[...], g2m, r.d2[...] = message_part(out[: d.feat], r.w2t[...], r.cols[:, 1:2], att)
        put_ones(r.g1, g1)
        node_step(d, r, p, b, g2m, att, r.rt[: d.res])

        @pl.when(middle)
        def _():
            for item in swaps(GROUP_TWO):
                item.wait()
            for item in swaps(GROUP_THREE):
                item.start()
            r.leave[...] = node_forward(r, 0, r.n_own[0], 0, r.aux[...])
            job.start()

        @pl.when(at_end)
        def _():
            node_forward(r, d.parts - 1, r.n_own[d.parts - 1], 0, r.aux[...])
            for item in swaps(GROUP_THREE):
                item.wait()
            for item in returns():
                item.start()
            for item in returns():
                item.wait()
            job.wait()

    return ph.call("enc_message", body)


W_IN, W_OUT = "i_", "o_"
GROUP_ONE = ("mw1", "mw2", "bias", "gain")
GROUP_TWO = ("mw3", "inner", "inner_b", "outer")
GROUP_THREE = ("uw1", "uw2", "uw3")
NODE_W = ("mw3", "inner", "inner_b", "outer", "bias", "gain")
MSG_W = ("mw1", "mw2")
UPD_W = ("uw1", "uw2", "uw3")


def with_ones(d):
    return (d.parts, d.blocks, d.feat + 16, d.rows)


def put_ones(ref, g):
    feat, rows = g.shape
    ref[:feat] = g
    ref[feat:] = jnp.ones((16, rows), BF)


def half_of(w):
    return w * BF(0.5)


def update_forward(d, a1, w2t, w3c, b5, b6c, pair, cols):
    f = d.feat
    g1, d1 = gelu_pair(a1)
    a2 = mm(w2t, g1) + b5
    g2, d2 = gelu_pair(a2)
    pair[f : 2 * f] = g2
    cent = mm(w3c[...], pair[: 2 * f]) + b6c
    var = jnp.mean(cent * cent, axis=0, keepdims=True)
    rs = lax.rsqrt(var + EPS)
    xh = cent.astype(BF) * rs.astype(BF)
    y = xh * cols[:, 12:13].astype(BF) + cols[:, 9:10].astype(BF)
    return g1, d1, g2, d2, xh, rs, y


def centre_weights(w3, cols, w3c, b6c):
    feat = w3.shape[0]
    eye = lax.broadcasted_iota(jnp.int32, w3.shape, 0) == lax.broadcasted_iota(jnp.int32, w3.shape, 1)
    w3f = w3.astype(F32)
    w3c[:, feat:] = (0.5 * (w3f - jnp.mean(w3f, axis=1, keepdims=True))).T.astype(BF)
    w3c[:, :feat] = (eye.astype(F32) - 1.0 / feat).astype(BF)
    b6 = cols[:, 6:7]
    b6c[...] = jnp.broadcast_to(b6 - jnp.mean(b6, axis=0, keepdims=True), b6c.shape)


def encoder_update(d, edge_input, st, fa, consts):
    ph = Phase(d, 3)
    ph.whole(n_own=fa.node_out, got_a=fa.got, idx=consts.idx, rt=consts.sums, mask=consts.mask, att=fa.att)
    ph.edges(edge=edge_input)
    ph.whole(**weight_args(st, *NODE_W, *MSG_W, *UPD_W))
    act = (d.parts, d.blocks, d.feat, d.rows)
    tall = with_ones(d)
    ph.out_stream(BF, ug1=tall, ud1=act, ug2=tall, ud2=act, uxh=act, e2=act, g1=tall, d1=act, d2=act)
    ph.out_whole(F32, urs=(d.parts, d.blocks, 1, d.rows))
    add_node_outs(ph, d)
    ph.out_whole(BF, got_in=(d.half, d.feat))
    ph.out_raw(BF, got=(d.parts, d.half, d.feat))
    sq = (d.feat, d.feat)
    wide = d.feat + d.length + d.res
    ph.temp(BF, n_cat=(d.length, d.feat), lhs=(2 * d.feat, wide), tt=(wide, d.rows))
    ph.temp(BF, uw2t=sq, mw1bt=sq, mw2t=sq, w3c=(d.feat, 2 * d.feat), pair=(2 * d.feat, d.rows))
    ph.temp(BF, leave=(d.parts, d.half, d.feat), lead=(d.half, d.feat), arrive=(d.half, d.feat))
    ph.temp(F32, w3c_b=sq, e_aux=sq, e_cols=sq, d_aux=sq, d_cols=sq)
    ph.sems(send=d.parts + 1, recv=d.parts + 1)

    def body(r):
        p, b = pl.program_id(0), pl.program_id(1)
        first, last = b == 0, b == d.blocks - 1
        early = to_partner(r.lead, r.arrive, r.send.at[d.parts], r.recv.at[d.parts])
        jobs = [to_partner(r.leave.at[i], r.got.at[i], r.send.at[i], r.recv.at[i]) for i in range(d.parts)]

        @pl.when(first & (p == 0))
        def _():
            greet_partner()
            r.lead[...] = r.n_own[d.parts - 1]
            early.start()
            r.tt[d.feat + d.length :, :] = r.rt[: d.res]
            r.lhs[: d.feat, : d.feat] = r.uw1[0, d.feat : 2 * d.feat, :].T
            r.lhs[d.feat :, : d.feat] = jnp.zeros((d.feat, d.feat), BF)
            r.uw2t[...] = half_of(r.uw2[0]).T
            r.mw1bt[...] = r.mw1[1, d.feat : 2 * d.feat, :].T
            r.mw2t[...] = half_of(r.mw2[1]).T
            load_cols(r, 0, r.e_aux, r.e_cols)
            load_cols(r, 1, r.d_aux, r.d_cols)
            centre_weights(r.uw3[0], r.e_cols[...], r.w3c, r.w3c_b)
            r.n_cat[d.half :] = r.got_a[...]

        @pl.when(first & (p == 1))
        def _():
            early.wait()
            r.n_cat[d.half :] = r.arrive[...]
            r.got_in[...] = r.arrive[...]

        @pl.when(first)
        def _():
            r.n_cat[: d.half] = r.n_own[p]

        n_blk = r.n_own[p, pl.ds(pl.multiple_of(b * d.res, d.res), d.res), :]
        put_table(d, r.lhs, 0, d.feat, r.n_cat, r.uw1.at[0], n_blk, r.e_cols[:, 4:5], first)
        put_table(d, r.lhs, d.feat, d.feat, r.n_cat, r.mw1.at[1], n_blk, r.d_cols[:, 0:1], first)
        put_one_hot(d, r.tt, d.feat, r.idx[p, b])
        edge_t = r.edge[...].reshape(d.rows, d.feat).T
        r.tt[: d.feat, :] = edge_t
        r.pair[: d.feat] = edge_t
        out = mm(r.lhs[...], r.tt[...])
        g1, d1, g2, d2, xh, rs, e2 = update_forward(
            d, out[: d.feat], r.uw2t[...], r.w3c, r.e_cols[:, 5:6], r.w3c_b[:, 0:1], r.pair, r.e_cols
        )
        put_ones(r.ug1, g1)
        put_ones(r.ug2, g2)
        r.ud1[...], r.ud2[...], r.uxh[...], r.urs[p, b], r.e2[...] = d1, d2, xh, rs, e2
        att = r.att[p, b]
        a1 = out[d.feat :] + mm(r.mw1bt[...], e2)
        g1, r.d1[...], g2m, r.d2[...] = message_part(a1, r.mw2t[...], r.d_cols[:, 1:2], att)
        put_ones(r.g1, g1)
        node_step(d, r, p, b, g2m, att, r.rt[: d.res])

        @pl.when(last)
        def _():
            r.leave[p] = node_forward(r, p, r.n_own[p], 1, r.d_aux[...])
            for i in range(d.parts):

                @pl.when(p == i)
                def _(i=i):
                    jobs[i].start()

            @pl.when(p == d.parts - 1)
            def _():
                for job in jobs:
                    job.wait()

    return ph.call("enc_update", body)


def spread_nodes(d, acc, sumk, w1, n_cat, grad, grad_at):
    s = acc.astype(BF)
    sk = jnp.concatenate([x[:, : d.res] for x in sumk], axis=1)
    skb = sk.astype(BF)
    far = mm(s, w1[2 * d.feat :].T, 0, 0)
    own = mm(skb, w1[: d.feat].T, 0, 0)
    grad[grad_at + 2 * d.feat : grad_at + 3 * d.feat, :] += mm(n_cat, s, 0, 1)
    grad[grad_at : grad_at + d.feat, :] += mm(n_cat[: d.half], skb, 0, 1)
    return own + far[: d.half], far[d.half :], to_row(sk)


def lane_total(x):
    size = x.shape[1] // 4
    x = (x[:, :size] + x[:, size : 2 * size]) + (x[:, 2 * size : 3 * size] + x[:, 3 * size :])
    return lane_sum(x.astype(F32))


def norm_backward(d, r, dy, xh, rs, gain_mat):
    r.a_b9[...] += lane_total(dy)
    r.a_g2[...] += lane_total(dy * xh)
    z = mm(gain_mat, dy).astype(BF)
    m2 = jnp.mean((z * xh).astype(F32), axis=0, keepdims=True)
    return (z - xh * m2.astype(BF)) * rs.astype(BF)


def gain_matrix(cols):
    feat = cols.shape[0]
    shape = (feat, feat)
    eye = lax.broadcasted_iota(jnp.int32, shape, 0) == lax.broadcasted_iota(jnp.int32, shape, 1)
    scaled = jnp.where(eye, jnp.broadcast_to(cols[:, 12:13], shape), 0.0)
    return (scaled - jnp.mean(scaled, axis=0, keepdims=True)).astype(BF)


def update_backward(d, r, dr3, g1, d1, g2, d2, w2, w3, da1):
    r.a_w3[...] += mm(g2, dr3, 1, 1)
    da2 = mm(w3, dr3).astype(BF) * d2
    r.a_w2[...] += mm(g1, da2, 1, 1)
    da1[...] = mm(w2, da2).astype(BF) * d1


def update_small(d, r, b4):
    f = d.feat
    at = 5 * f
    r.upd[at + 4 : at + 5] += b4

    @pl.when(pl.program_id(0) == d.parts - 1)
    def _():
        r.upd[3 * f : 4 * f] = 0.5 * r.a_w2[:f]
        r.upd[4 * f : 5 * f] = 0.5 * r.a_w3[:f]
        r.upd[at + 5 : at + 6] = r.a_w2[f : f + 1]
        r.upd[at + 6 : at + 7] = r.a_w3[f : f + 1]
        r.upd[at + 9 : at + 10] = to_row(r.a_b9[...])
        r.upd[at + 12 : at + 13] = to_row(r.a_g2[...])


def zero(*refs):
    for ref in refs:
        ref[...] = jnp.zeros(ref.shape, ref.dtype)


def decoder_update(d, st, fb, cot, consts):
    ph = Phase(d)
    ph.whole(n_own=fb.node_out, n_got=fb.got, idx=consts.idx, rt=consts.sums)
    ph.stream(e2=fb.e2)
    ph.edges(cot=cot)
    ph.whole(**weight_args(st, *UPD_W, *AUX_W))
    ph.out_edges(decoded=cot.shape)
    ph.out_stream(BF, part=(d.parts, d.blocks, d.feat, d.rows))
    ph.out_whole(F32, upd=(d.upd_rows, d.feat), dn_own=(d.parts, d.half, d.feat))
    ph.out_whole(BF, dn_far=(d.parts, d.half, d.feat))
    sq = (d.feat, d.feat)
    ph.temp(BF, n_cat=(d.length, d.feat), lhs=(d.feat, d.length + d.res), w1bt=sq, w2t=sq, w2h=sq, w3h=sq)
    ph.temp(BF, tt=(d.length + d.res, d.rows), tn=(d.rows, d.length + 128), da1=(d.feat, d.rows))
    ph.temp(BF, w3c=(d.feat, 2 * d.feat), gain_mat=sq, pair=(2 * d.feat + 16, d.rows), one=(d.feat + 16, d.rows))
    tall = (d.feat + 16, d.feat)
    ph.temp(F32, w3c_b=sq, aux=sq, cols=sq, a_w2=tall, a_w3=tall, a_b9=sq, a_g2=sq)
    ph.temp(F32, a_s=(d.feat, d.length), a_k=(d.blocks, d.feat, 128))

    def body(r):
        p, b = pl.program_id(0), pl.program_id(1)
        first, last = b == 0, b == d.blocks - 1

        @pl.when(first & (p == 0))
        def _():
            r.w1bt[...] = r.uw1[1, d.feat : 2 * d.feat, :].T
            r.w2h[...] = half_of(r.uw2[1])
            r.w2t[...] = r.w2h[...].T
            r.w3h[...] = half_of(r.uw3[1])
            load_cols(r, 1, r.aux, r.cols)
            centre_weights(r.uw3[1], r.cols[...], r.w3c, r.w3c_b)
            r.gain_mat[...] = gain_matrix(r.cols[...])
            zero(r.upd, r.a_w2, r.a_w3, r.a_b9, r.a_g2)
            r.pair[2 * d.feat :] = jnp.ones((16, d.rows), BF)
            r.one[d.feat :] = jnp.ones((16, d.rows), BF)
            r.tt[d.length :, :] = r.rt[: d.res]
            r.tn[:, d.length :] = r.rt[...].T

        @pl.when(first)
        def _():
            r.n_cat[: d.half] = r.n_own[p]
            r.n_cat[d.half :] = r.n_got[p]
            zero(r.a_s)

        n_blk = r.n_own[p, pl.ds(pl.multiple_of(b * d.res, d.res), d.res), :]
        put_table(d, r.lhs, 0, 0, r.n_cat, r.uw1.at[1], n_blk, r.cols[:, 4:5], first)
        f = d.feat
        idx = r.idx[p, b]
        put_one_hot(d, r.tt, 0, idx)
        put_one_hot_rows(d, r.tn, idx)
        e2 = r.e2[...]
        r.pair[:f] = e2
        a1 = mm(r.lhs[...], r.tt[...]) + mm(r.w1bt[...], e2)
        g1, d1, _, d2, xh, rs, y = update_forward(
            d, a1, r.w2t[...], r.w3c, r.cols[:, 5:6], r.w3c_b[:, 0:1], r.pair, r.cols
        )
        r.one[:f] = g1
        r.decoded[...] = y.T.reshape(d.res, d.near, f)
        dy = r.cot[...].reshape(d.rows, f).T
        dr3 = norm_backward(d, r, dy, xh, rs, r.gain_mat[...])
        update_backward(d, r, dr3, r.one[...], d1, r.pair[f:], d2, r.w2h[...], r.w3h[...], r.da1)
        r.upd[f : 2 * f] += mm(e2, r.da1[...], 1, 1)
        r.part[...] = (mm(r.uw1[1, f : 2 * f, :], r.da1[...]) + dr3.astype(F32)).astype(BF)
        spread = mm(r.da1[...], r.tn[...])
        r.a_s[...] += spread[:, : d.length]
        r.a_k[b] = spread[:, d.length :]

        @pl.when(last)
        def _():
            own, far, b4 = spread_nodes(
                d, r.a_s[...], [r.a_k[i] for i in range(d.blocks)], r.uw1[1], r.n_cat[...], r.upd, 0
            )
            r.dn_own[p] = own
            r.dn_far[p] = far.astype(BF)
            update_small(d, r, b4)

    return ph.call("dec_update", body)


AUX_W = ("bias", "gain")


def message_backward(d, r, b, layer, da1):
    at = pl.ds(pl.multiple_of(b * d.res, d.res), d.res)
    v = (mm(r.mw3[layer], r.dub[at, :], 1, 1) * 0.5).astype(BF)
    da2 = mm(v, r.rt[: d.res]).astype(BF) * r.d2[...]
    r.m_w2[...] += mm(r.g1[...], da2, 1, 1)
    da1[...] = mm(r.mw2h[...], da2).astype(BF) * r.d1[...]


def message_small(d, r, b0):
    f = d.feat
    at = d.at_small
    r.msg[at : at + 1] += b0

    @pl.when(pl.program_id(0) == d.parts - 1)
    def _():
        r.msg[3 * f : 4 * f] = 0.5 * r.m_w2[:f]
        r.msg[at + 1 : at + 2] = r.m_w2[f : f + 1]


def middle_backward(d, edge_input, st, fa, fb, fd, cot_n, consts):
    ph = Phase(d, 4)
    ph.whole(cot_n=cot_n, dn_a=fd.dn_own, dn_far_in=fd.dn_far, n_own=fa.node_out, got_a=fa.got, got_b=fb.got_in)
    ph.whole(mask=consts.mask, rt=consts.sums, r1=fb.r1, ip=fb.ip, r2=fb.r2, big=fb.big, cnt=fb.cnt)
    ph.whole(urs=fb.urs, idx=consts.idx)
    ph.stream(d2=fb.d2, g1=fb.g1, d1=fb.d1, e2=fb.e2, dec_part=fd.part, uxh=fb.uxh)
    ph.stream(ug2=fb.ug2, ud2=fb.ud2, ug1=fb.ug1, ud1=fb.ud1)
    ph.edges(edge=edge_input)
    ph.whole(**weight_args(st, *NODE_W, *MSG_W, *UPD_W))
    ph.out_stream(BF, part=(d.parts, d.blocks, d.feat, d.rows))
    ph.out_whole(F32, msg=(d.msg_rows, d.feat), upd=(d.upd_rows, d.feat), dn_own=(d.parts, d.half, d.feat))
    ph.out_raw(BF, got=(d.parts, d.half, d.feat))
    sq = (d.feat, d.feat)
    ph.temp(BF, n_cat=(d.length, d.feat), dub=(d.half, d.feat), tn=(d.rows, d.length + 128))
    ph.temp(BF, both=(2 * d.feat, d.rows), w2h=sq, w3h=sq, mw2h=sq, gain_mat=sq)
    ph.temp(BF, leave=(d.parts, d.half, d.feat), arrive=(d.parts, d.half, d.feat))
    ph.temp(F32, dr1=(d.half, d.feat), e_aux=sq, e_cols=sq, d_aux=sq, d_cols=sq)
    tall = (d.feat + 16, d.feat)
    ph.temp(F32, m_w2=tall, a_w2=tall, a_w3=tall, a_b9=sq, a_g2=sq, a_w1=sq)
    ph.temp(F32, a_s=(2 * d.feat, d.length), a_k=(d.blocks, 2 * d.feat, 128))
    ph.sems(send=2 * d.parts, recv=2 * d.parts)

    def body(r):
        p, b = pl.program_id(0), pl.program_id(1)
        first, last = b == 0, b == d.blocks - 1
        n = d.parts
        early = [to_partner(r.dn_far_in.at[i], r.arrive.at[i], r.send.at[n + i], r.recv.at[n + i]) for i in range(n)]
        jobs = [to_partner(r.leave.at[i], r.got.at[i], r.send.at[i], r.recv.at[i]) for i in range(n)]

        @pl.when(first & (p == 0))
        def _():
            greet_partner()
            for job in early:
                job.start()
            load_cols(r, 0, r.e_aux, r.e_cols)
            load_cols(r, 1, r.d_aux, r.d_cols)
            r.tn[:, d.length :] = r.rt[...].T
            r.w2h[...] = half_of(r.uw2[0])
            r.w3h[...] = half_of(r.uw3[0])
            r.mw2h[...] = half_of(r.mw2[1])
            r.gain_mat[...] = gain_matrix(r.e_cols[...])
            zero(r.msg, r.upd, r.m_w2, r.a_w2, r.a_w3, r.a_b9, r.a_g2, r.a_w1)
            r.n_cat[d.half :] = r.got_a[...]

        @pl.when(first & (p == 1))
        def _():
            r.n_cat[d.half :] = r.got_b[...]

        for i in range(n):

            @pl.when(first & (p == i))
            def _(i=i):
                early[i].wait()

        @pl.when(first)
        def _():
            r.n_cat[: d.half] = r.n_own[p]
            zero(r.a_s)
            dn = r.cot_n[p].astype(F32) + r.dn_a[p] + r.arrive[p].astype(F32)
            node_backward(d, r, p, 1, r.d_aux[...], dn)

        f = d.feat
        put_one_hot_rows(d, r.tn, r.idx[p, b])
        message_backward(d, r, b, 1, r.both.at[:f])
        r.msg[f : 2 * f] += mm(r.e2[...], r.both[:f], 1, 1)
        de = mm(r.mw1[1, f : 2 * f, :], r.both[:f])
        dy = (de + r.dec_part[...].astype(F32)).astype(BF)
        dr3 = norm_backward(d, r, dy, r.uxh[...], r.urs[p, b], r.gain_mat[...])
        update_backward(
            d, r, dr3, r.ug1[...], r.ud1[...], r.ug2[...], r.ud2[...], r.w2h[...], r.w3h[...], r.both.at[f:]
        )
        r.a_w1[...] += mm(r.both[f:], r.edge[...].reshape(d.rows, f))
        r.part[...] = (mm(r.uw1[0, f : 2 * f, :], r.both[f:]) + dr3.astype(F32)).astype(BF)
        spread = mm(r.both[...], r.tn[...])
        r.a_s[...] += spread[:, : d.length]
        r.a_k[b] = spread[:, d.length :]

        @pl.when(last)
        def _():
            n_cat = r.n_cat[...]
            a_k = [r.a_k[i] for i in range(d.blocks)]
            own_m, far_m, b0 = spread_nodes(
                d, r.a_s[: d.feat], [x[: d.feat] for x in a_k], r.mw1[1], n_cat, r.msg, 0
            )
            own_u, far_u, b4 = spread_nodes(
                d, r.a_s[d.feat :], [x[d.feat :] for x in a_k], r.uw1[0], n_cat, r.upd, 0
            )
            r.dn_own[p] = own_m + own_u + r.dr1[...]
            r.leave[p] = (far_m + far_u).astype(BF)
            for i in range(n):

                @pl.when(p == i)
                def _(i=i):
                    jobs[i].start()

            message_small(d, r, b0)
            update_small(d, r, b4)

            @pl.when(p == n - 1)
            def _():
                r.upd[d.feat : 2 * d.feat] = r.a_w1[...].T
                for job in jobs:
                    job.wait()

    return ph.call("dec_message_back", body)


def encoder_message_back(d, edge_input, st, fa, fe, n_own, n_got, consts):
    ph = Phase(d)
    ph.whole(dn_a=fe.dn_own, dn_b=fe.got, n_own=n_own, n_got=n_got)
    ph.whole(mask=consts.mask, rt=consts.sums, r1=fa.r1, ip=fa.ip, r2=fa.r2, big=fa.big, cnt=fa.cnt)
    ph.whole(idx=consts.idx)
    ph.stream(d2=fa.d2, g1=fa.g1, d1=fa.d1, up_part=fe.part)
    ph.edges(edge=edge_input)
    ph.whole(**weight_args(st, *NODE_W, *MSG_W))
    ph.out_edges(edge_grad=edge_input.shape)
    ph.out_whole(F32, msg=(d.msg_rows, d.feat), dn_own=(d.parts, d.half, d.feat))
    ph.out_whole(BF, dn_far=(d.parts, d.half, d.feat))
    sq = (d.feat, d.feat)
    ph.temp(BF, n_cat=(d.length, d.feat), dub=(d.half, d.feat), tn=(d.rows, d.length + 128))
    ph.temp(BF, da1=(d.feat, d.rows), mw2h=sq)
    ph.temp(F32, dr1=(d.half, d.feat), aux=sq, cols=sq, a_w1=sq, m_w2=(d.feat + 16, d.feat))
    ph.temp(F32, a_s=(d.feat, d.length), a_k=(d.blocks, d.feat, 128))

    def body(r):
        p, b = pl.program_id(0), pl.program_id(1)
        first, last = b == 0, b == d.blocks - 1

        @pl.when(first & (p == 0))
        def _():
            load_cols(r, 0, r.aux, r.cols)
            r.tn[:, d.length :] = r.rt[...].T
            r.mw2h[...] = half_of(r.mw2[0])
            zero(r.msg, r.m_w2, r.a_w1)

        @pl.when(first)
        def _():
            r.n_cat[: d.half] = r.n_own[p]
            r.n_cat[d.half :] = r.n_got[p]
            zero(r.a_s)
            node_backward(d, r, p, 0, r.aux[...], r.dn_a[p] + r.dn_b[p].astype(F32))

        f = d.feat
        put_one_hot_rows(d, r.tn, r.idx[p, b])
        message_backward(d, r, b, 0, r.da1)
        r.a_w1[...] += mm(r.da1[...], r.edge[...].reshape(d.rows, f))
        de = mm(r.mw1[0, f : 2 * f, :], r.da1[...])
        de = (de + r.up_part[...].astype(F32)).astype(BF)
        r.edge_grad[...] = de.T.reshape(d.res, d.near, f)
        spread = mm(r.da1[...], r.tn[...])
        r.a_s[...] += spread[:, : d.length]
        r.a_k[b] = spread[:, d.length :]

        @pl.when(last)
        def _():
            own, far, b0 = spread_nodes(
                d, r.a_s[...], [r.a_k[i] for i in range(d.blocks)], r.mw1[0], r.n_cat[...], r.msg, 0
            )
            r.dn_own[p] = own + r.dr1[...]
            r.dn_far[p] = far.astype(BF)
            message_small(d, r, b0)

            @pl.when(p == d.parts - 1)
            def _():
                r.msg[d.feat : 2 * d.feat] = r.a_w1[...].T

    return ph.call("enc_message_back", body)


def reduce_grads(d, enc_msg, enc_upd, dec_msg, dec_upd, dn_far):
    devices = d.devices
    bits = devices.bit_length() - 1
    unit = 16 * devices
    feat = d.feat
    need = -(-(d.msg_rows + d.upd_rows) // unit)
    shares = [need // 3 + (1 if need % 3 > i else 0) for i in range(3)]
    groups = [unit * share for share in shares if share]
    rows = sum(groups)
    bases = [sum(groups[:i]) for i in range(len(groups))]
    across = -1
    dims = [across] + list(range(1, bits))
    turn = min(3, len(dims))
    orders = []
    for g in range(len(groups)):
        head = dims[:turn]
        head = head[g % turn :] + head[: g % turn]
        orders.append(([0] if bits else []) + head + dims[turn:])
    stages = len(orders[0])
    plans = []
    for g, order in enumerate(orders):
        size, both, plan = groups[g], True, []
        for dim in order:
            if dim == across:
                both = False
                plan.append((dim, size, False))
            else:
                size //= 2
                plan.append((dim, size, both))
        plans.append(plan)
    turns = len(groups) * stages

    def kernel(em, eu, dm, du, far, res, got, acc, gathered, *rest):
        buffers, (send, recv) = rest[: 2 * turns], rest[2 * turns :]
        section, me = lax.axis_index(AXIS_S), lax.axis_index(AXIS_D)

        def flag(bit):
            return lax.rem(me // (1 << bit), 2)

        def peer(dim):
            if dim == across:
                return other_section()
            return {AXIS_D: me + (1 - 2 * flag(dim)) * (1 << dim)}

        barrier = pltpu.get_barrier_semaphore()
        for dim in [across] + list(range(bits)):
            pl.semaphore_signal(barrier, inc=1, device_id=peer(dim), device_id_type=MESH)
        pl.semaphore_wait(barrier, bits + 1)

        def remote(src, dst, at, dim):
            return pltpu.make_async_remote_copy(
                src_ref=src, dst_ref=dst, send_sem=send.at[at], recv_sem=recv.at[at],
                device_id=peer(dim), device_id_type=MESH,
            )

        nodes = remote(far, got, 2 * turns, across)
        nodes.start()
        m, u = d.msg_rows, d.upd_rows
        for layer, (msg, upd) in enumerate(((em, eu), (dm, du))):
            acc[layer, :m] = msg[...]
            acc[layer, m : m + u] = upd[...]
            if rows > m + u:
                acc[layer, m + u :] = jnp.zeros((rows - m - u, feat), F32)

        def span(start, size):
            return pl.ds(pl.multiple_of(start, 16), size)

        starts = list(bases)
        for k in range(stages):
            jobs, spans = [], []
            for g, plan in enumerate(plans):
                dim, size, both = plan[k]
                at = g * stages + k
                out, into = buffers[2 * at], buffers[2 * at + 1]
                if dim == across:
                    keep = span(starts[g], size)
                    out[...] = acc[1 - section, keep, :].astype(BF)
                else:
                    side = flag(dim)
                    keep = span(starts[g] + side * size, size)
                    give = span(starts[g] + (1 - side) * size, size)
                    if both:
                        out[...] = acc[:, give, :].astype(BF)
                    else:
                        out[...] = acc[section, give, :].astype(BF)
                    starts[g] = starts[g] + side * size
                job = remote(out, into, at, dim)
                job.start()
                jobs.append(job)
                spans.append(keep)
            for g, plan in enumerate(plans):
                dim, size, both = plan[k]
                jobs[g].wait()
                into = buffers[2 * (g * stages + k) + 1]
                if both:
                    acc[:, spans[g], :] += into[...].astype(F32)
                else:
                    acc[section, spans[g], :] += into[...].astype(F32)
        sizes = [plan[-1][1] for plan in plans]
        for g in range(len(groups)):
            keep = span(starts[g], sizes[g])
            gathered[keep, :] = acc[section, keep, :].astype(BF)
        backs = [[step for step in reversed(plan) if step[0] != across] for plan in plans]
        for k in range(bits):
            jobs = []
            for g, back in enumerate(backs):
                dim, size, _ = back[k]
                part = gathered.at[span(starts[g], size), :]
                job = remote(part, part, turns + g * bits + k, dim)
                job.start()
                jobs.append(job)
                starts[g] = starts[g] - flag(dim) * size
            for job in jobs:
                job.wait()
        res[...] = gathered[...]
        nodes.wait()

    vm = pl.BlockSpec(memory_space=pltpu.VMEM)
    scratch = [pltpu.VMEM((2, rows, feat), F32), pltpu.VMEM((rows, feat), BF)]
    for plan in plans:
        for _, size, both in plan:
            scratch += [pltpu.VMEM((2, size, feat) if both else (size, feat), BF)] * 2
    scratch += [pltpu.SemaphoreType.DMA((2 * turns + 1,))] * 2
    return pl.pallas_call(
        kernel,
        in_specs=[vm] * 5,
        out_specs=[vm, pl.BlockSpec(memory_space=pl.ANY)],
        out_shape=[
            jax.ShapeDtypeStruct((rows, feat), BF),
            jax.ShapeDtypeStruct(dn_far.shape, BF),
        ],
        scratch_shapes=scratch,
        compiler_params=pltpu.CompilerParams(vmem_limit_bytes=58 << 20, collective_id=5, has_side_effects=True),
        name="reduce",
    )(enc_msg, enc_upd, dec_msg, dec_upd, dn_far)


def unpack(d, total, dn_own, dn_got, n_bias, n_gain):
    f = d.feat
    m = d.msg_rows
    shapes = [(1, 3 * f, f), (1, f, f), (1, f, f), (1, f, d.wide), (1, 1, d.wide), (1, d.wide, f)]
    shapes += [(1, 3 * f, f), (1, f, f), (1, f, f), (n_bias, 1, f), (n_gain, 1, f)]

    def kernel(t, own, got, node, mw1, mw2, mw3, inner, inner_b, outer, uw1, uw2, uw3, bias, gain):
        node[...] = (own[...] + got[...].astype(F32)).astype(BF)
        for ref, at in ((mw1, 0), (mw2, 3 * f), (mw3, 4 * f), (outer, d.at_outer)):
            ref[0] = t[at : at + ref.shape[1], :].astype(F32)
        for ref, at in ((uw1, m), (uw2, m + 3 * f), (uw3, m + 4 * f)):
            ref[0] = t[at : at + ref.shape[1], :].astype(F32)
        inner[0] = t[d.at_inner : d.at_inner + d.wide, :].astype(F32).T
        small = t[d.at_small : d.at_small + SMALL, :].astype(F32)
        other = t[m + 5 * f : m + 5 * f + SMALL, :].astype(F32)
        both = small + other
        for i in range(n_bias):
            bias[i] = both[i : i + 1]
        for i in range(n_gain):
            gain[i] = both[n_bias + i : n_bias + i + 1]
        for i in range(d.wide // f):
            inner_b[0, :, i * f : (i + 1) * f] = small[16 + i : 17 + i]

    vm = pl.BlockSpec(memory_space=pltpu.VMEM)
    out = [jax.ShapeDtypeStruct(dn_own.shape, BF)] + [jax.ShapeDtypeStruct(s, F32) for s in shapes]
    return pl.pallas_call(kernel, in_specs=[vm] * 3, out_specs=[vm] * len(out), out_shape=out, name="unpack")(
        total, dn_own, dn_got
    )


def per_device(
    node_input,
    edge_input,
    neighbors,
    residue_mask,
    decode_order,
    node_cotangent,
    edge_cotangent,
    message_w1,
    message_w2,
    message_w3,
    inner_w,
    inner_bias,
    outer_w,
    update_w1,
    update_w2,
    update_w3,
    biases,
    norm_gains,
):
    section = lax.axis_index(AXIS_S)
    is_first = section == 0
    parts, half, near, feat = edge_input.shape
    length = neighbors.shape[1]
    wide = inner_w.shape[2]
    res = BLOCK_RES
    rows = res * near
    blocks = half // res
    at_outer = 5 * feat
    at_inner = at_outer + wide
    at_small = at_inner + wide
    d = types.SimpleNamespace(
        parts=parts, half=half, near=near, feat=feat, length=length, wide=wide, res=res, rows=rows, blocks=blocks,
        at_outer=at_outer, at_inner=at_inner, at_small=at_small, msg_rows=at_small + SMALL,
        upd_rows=5 * feat + SMALL, devices=lax.axis_size(AXIS_D),
    )
    weights = dict(
        mw1=message_w1[0], mw2=message_w2[0], mw3=message_w3[0], inner=inner_w[0], inner_b=inner_bias, outer=outer_w[0],
        uw1=update_w1[0], uw2=update_w2[0], uw3=update_w3[0],
        bias=biases.transpose(1, 0, 2), gain=norm_gains.transpose(1, 0, 2),
    )
    own_ids = lax.dynamic_slice_in_dim(neighbors, section * half, half, 1) - section * half
    idx_row = jnp.where(own_ids < 0, own_ids + length, own_ids).reshape(parts, blocks, 1, rows)
    sums = np.zeros((128, rows), np.float32)
    sums[np.arange(rows) // near, np.arange(rows)] = 1.0
    sums = jnp.asarray(sums, BF)

    def own_first(x):
        return jnp.where(is_first, x, jnp.roll(x, half, axis=1))

    live = own_first(residue_mask)
    order = own_first(decode_order)
    centre = length // 2
    code = jnp.where(live == 1, order - centre, centre)
    own_code = (order[:, :half] - centre).reshape(parts, blocks, 1, res)
    lead = (parts, blocks, 1, length)
    top = jnp.pad(jnp.broadcast_to(live[:, None, None, :], lead), ((0, 0), (0, 0), (0, 0), (0, res)))
    second = jnp.concatenate([jnp.broadcast_to(code[:, None, None, :], lead), -own_code], axis=3)
    extra = jnp.concatenate([top, second, jnp.zeros((parts, blocks, EXTRA - 2, length + res), top.dtype)], axis=2)
    mask = jnp.broadcast_to(live[:, :half, None].astype(F32), (parts, half, feat))
    consts = types.SimpleNamespace(extra=extra.astype(BF), sums=sums, mask=mask, idx=idx_row)

    fa = encoder_message(d, edge_input, node_input, weights, consts)
    st = types.SimpleNamespace(**{n: getattr(fa, W_OUT + n) for n in weights})
    fb = encoder_update(d, edge_input, st, fa, consts)
    fd = decoder_update(d, st, fb, edge_cotangent, consts)
    fe = middle_backward(d, edge_input, st, fa, fb, fd, node_cotangent, consts)
    ff = encoder_message_back(d, edge_input, st, fa, fe, node_input, fa.nodes_got, consts)
    total, got = reduce_grads(d, ff.msg, fe.upd, fe.msg, fd.upd, ff.dn_far)
    node_grad, mw1, mw2, mw3, inner, inner_b, outer, uw1, uw2, uw3, bias, gain = unpack(
        d, total, ff.dn_own, got, biases.shape[1], norm_gains.shape[1]
    )
    return (
        fb.node_out, fd.decoded, node_grad, ff.edge_grad, mw1, mw2, mw3, inner, inner_b[:, 0], outer,
        uw1, uw2, uw3, bias.transpose(1, 0, 2), gain.transpose(1, 0, 2),
    )


def solution(mesh):
    def split(*axes):
        return P(*axes)

    by_part = split(AXIS_D)
    by_half = split(AXIS_D, AXIS_S)
    by_layer = split(AXIS_S)
    in_specs = (by_half, by_half, by_part, by_part, by_part, by_half, by_half) + (by_layer,) * 11
    out_specs = (by_half,) * 4 + (by_layer,) * 11
    return jax.shard_map(per_device, mesh=mesh, in_specs=in_specs, out_specs=out_specs, check_vma=False)
```

time: 268 us -> 230 us (0.86)
  Pallas kernels: 255 us -> 222 us
  local copies, waits for them, and re-layouts: 9.42 us -> 4.21 us
    pallas_call x6 -> x5, Pallas kernels: 211 us -> 183 us  [call(): pl.pallas_call(kernel, grid=(d.parts, d.blocks), in_specs=[s for _, _, s...]
    pallas_call x1, Pallas kernels: 42.1 us -> 36.6 us  [reduce_grads(): pl.pallas_call(kernel, in_specs=[vm] * 5, out_specs=[vm, pl.BlockSpec(mem...]
    unnamed x11 -> x3, local copies, waits for them, and re-layouts: 5.75 us -> 0.65 us
where the time goes in v2:
time: 230 us
  Pallas kernels  222 us (97%)
  local copies, waits for them, and re-layouts  4.21 us (2%)
  other arithmetic  2.52 us (1%)
    pallas_call x5, Pallas kernels, call(): pl.pallas_call(kernel, grid=(d.parts, d.blocks), in_specs=[s for _, _, s...  183 us
    pallas_call x1, Pallas kernels, reduce_grads(): pl.pallas_call(kernel, in_specs=[vm] * 5, out_specs=[vm, pl.BlockSpec(mem...  36.6 us

profile of v2, /device:TPU:0, one launch (start us, length us, event | category | flops | bytes accessed | tf_op | source)
XLA Modules:
  0.0 229.8 jit_solution(507037078162926317)
XLA Ops:
  0.7 0.1 pad.9.clone
  0.7 0.8 fusion.6
  1.6 0.8 fusion.7
  2.4 0.8 fusion.3
  3.2 0.1 neg.16
  3.3 0.7 fusion.2.refs_4_
  4.0 1.0 compare_select_fusion
  5.0 0.1 copy.35
  5.2 0.8 reshape.57.refs_1_.refs_2_.refs_14_.refs_11_
  6.0 0.8 broadcast_in_dim.10.refs_3_.refs_4_.refs_6_
  6.8 31.6 %enc_message.1 = (bf16[2,3,144,3072]{3,2,1,0:T(8,128)(2,1)}, bf16[2,3,128,3072]{3,2,1,0:T(8,128)(2,1)}, bf16[2,3,128,3072]{3,2,1,0:T(8,128)(2,1)}, f32[2,3,1,307...) custom-call(bf16[2,192,128]{2,1,0:T(8,128)(2,1)} %refs_2_.2, ...), custom_call_target="tpu_custom_call" | custom-call | tf_op jit(solution)/shard_map/enc_message/pallas_call | solution.py:200
  38.4 41.2 %enc_update.1 = (bf16[2,3,144,3072]{3,2,1,0:T(8,128)(2,1)}, bf16[2,3,128,3072]{3,2,1,0:T(8,128)(2,1)}, bf16[2,3,144,3072]{3,2,1,0:T(8,128)(2,1)}, bf16[2,3,128,3...) custom-call(bf16[2,192,128]{2,1,0:T(8,128)(2,1)} %get-tuple-element., ...), custom_call_target="tpu_custom_call" | custom-call | tf_op jit(solution)/shard_map/enc_update/pallas_call | solution.py:200
  79.5 36.2 %dec_update.1 = (bf16[2,192,48,128]{3,2,1,0:T(8,128)(2,1)}, bf16[2,3,128,3072]{3,2,1,0:T(8,128)(2,1)}, f32[672,128]{1,0:T(8,128)}, f32[2,192,128]{2,1,0:T(8,128)}, bf16[2,192,128]{2,1,0:T(8,128)(2,1)}) custom-call(bf16[2,192,128]{2,1,0:T(8,128)(2,1)} %get-tuple-element.177.refs_0_, bf16[2,192,128]{2,1,0:T(8,128)(2,1)} %get-tuple-element.99.refs_1_, ...), custom_call_target="tpu_custom_call" | custom-call | tf_op jit(solution)/shard_map/dec_update/pallas_call | solution.py:200
  115.7 49.9 %dec_message_back.1 = (bf16[2,3,128,3072]{3,2,1,0:T(8,128)(2,1)}, f32[1696,128]{1,0:T(8,128)}, f32[672,128]{1,0:T(8,128)}, f32[2,192,128]{2,1,0:T(8,128)}, bf16[2,192,128]{2,1,0:T(8,128)(2,1)}) custom-call(bf16[2,192,128]{2,1,0:T(8,128)(2,1)} %refs_0_.3, f32[2,192,128]{2,1,0:T(8,128)} %get-tuple-element.102.refs_1_, ...), custom_call_target="tpu_custom_call" | custom-call | tf_op jit(solution)/shard_map/dec_message_back/pallas_call | solution.py:200
  165.6 0.0 copy-start
  165.6 24.6 %enc_message_back.1 = (bf16[2,192,48,128]{3,2,1,0:T(8,128)(2,1)}, f32[1696,128]{1,0:T(8,128)}, f32[2,192,128]{2,1,0:T(8,128)}, bf16[2,192,128]{2,1,0:T(8,128)(2,1)}) custom-call(f32[2,192,128]{2,1,0:T(8,128)} %get-tuple-element.120.refs_0_, bf16[2,192,128]{2,1,0:T(8,128)(2,1)} %get-tuple-element.121.refs_1_, bf16[2,192,128]{2,1,0:T(8,128)(2,1)} %refs_2_.2, ...), custom_call_target="tpu_custom_call" | custom-call | tf_op jit(solution)/shard_map/enc_message_back/pallas_call | solution.py:200
  190.3 36.6 %reduce.1 = (bf16[2560,128]{1,0:T(8,128)(2,1)}, bf16[2,192,128]{2,1,0:T(8,128)(2,1)}) custom-call(f32[1696,128]{1,0:T(8,128)} %get-tuple-element.132.em, f32[672,128]{1,0:T(8,128)} %get-tuple-element.133.eu, f32[1696,128]{1,0:T(8,128)} %get-tuple-element.134.dm, f32[672,128]{1,0:T(8,128)} %get-tuple-element.135.du, bf16[2,192,128]{2,1,0:T(8,128)(2,1)} %get-tuple-element.136.far), custom_call_target="tpu_custom_call" | custom-call | tf_op jit(solution)/shard_map/reduce/pallas_call | solution.py:1062
  226.8 2.3 unpack.1
  229.1 0.0 copy-done
  229.2 0.6 copy.43
  (5 shorter events, 0.0 us)
Async XLA Ops:
  165.6 63.5 %copy-start = (bf16[2,192,128]{2,1,0:T(8,128)(2,1)S(1)}, bf16[2,192,128]{2,1,0:T(8,128)(2,1)}, u32[]{:S(2)}) copy-start(bf16[2,192,128]{2,1,0:T(8,128)(2,1)} %get-tuple-element.177.refs_0_) | copy-start | bytes 294916

commit v3 on v2

--- a/solution.py
+++ b/solution.py
@@ -76,24 +76,6 @@
     return (dxh - m1 - xh * m2) * rs
 
 
-class Refs:
-    def __init__(self, plain, slots, waits):
-        self.__dict__.update(plain)
-        self._slots, self._waits = slots, waits
-
-    def __getattr__(self, name):
-        slots = self.__dict__.get(SLOTS, {})
-        if name not in slots:
-            raise AttributeError(name)
-        wait = self._waits.pop(name, None)
-        if wait is not None:
-            wait()
-        return slots[name]
-
-
-SLOTS = "_slots"
-
-
 class Phase:
     def __init__(self, dims, collective_id=None):
         self.d = dims
@@ -182,11 +164,13 @@
                 for i, n in outof:
                     copy(i, n, step - 2, now).wait()
 
-            waits = {n: copy(i, n, step, now).wait for i, n in into}
-            named = {n: slots[i].at[now] for i, n in enumerate(self.kinds)}
-            body(Refs({n: x for n, x in plain.items() if n not in named}, named, waits))
-            for wait in waits.values():
-                wait()
+            def ready():
+                for i, n in into:
+                    copy(i, n, step, now).wait()
+
+            plain_or_slot = dict(plain, ready=ready)
+            plain_or_slot.update({n: slots[i].at[now] for i, n in enumerate(self.kinds)})
+            body(types.SimpleNamespace(**plain_or_slot))
             for i, n in outof:
                 copy(i, n, step, now).start()
 
@@ -264,11 +248,11 @@
     cols[...] = aux[...].T
 
 
-def put_table(d, lhs, at, left, n_cat, w1, n_blk, bias_col, first):
-    @pl.when(first)
-    def _():
-        lhs[at : at + d.feat, left : left + d.length] = mm(w1[2 * d.feat :, :].T, n_cat[...], 1, 1).astype(BF)
-
+def put_table(d, lhs, at, left, n_cat, w1):
+    lhs[at : at + d.feat, left : left + d.length] = mm(w1[2 * d.feat :, :].T, n_cat[...], 1, 1).astype(BF)
+
+
+def put_own(d, lhs, at, left, w1, n_blk, bias_col):
     own = mm(w1[0 : d.feat, :].T, n_blk, 1, 1) + bias_col
     lhs[at : at + d.feat, left + d.length :] = own.astype(BF)
 
@@ -418,9 +402,6 @@
                 item.start()
             r.tt[d.feat + d.length :, :] = r.rt[: d.res]
 
-        put_one_hot(d, r.tt, d.feat, r.idx[p, b])
-        r.tt[: d.feat, :] = r.edge[...].reshape(d.rows, d.feat).T
-
         @pl.when(begin)
         def _():
             nodes.wait()
@@ -437,9 +418,13 @@
         def _():
             r.n_cat[: d.half] = r.n_own[p]
             r.n_cat[d.half :] = r.arrive[p]
+            put_table(d, r.lhs, 0, d.feat, r.n_cat, r.mw1.at[0])
 
         n_blk = r.n_own[p, pl.ds(pl.multiple_of(b * d.res, d.res), d.res), :]
-        put_table(d, r.lhs, 0, d.feat, r.n_cat, r.mw1.at[0], n_blk, r.cols[:, 0:1], first)
+        r.ready()
+        put_one_hot(d, r.tt, d.feat, r.idx[p, b])
+        r.tt[: d.feat, :] = r.edge[...].reshape(d.rows, d.feat).T
+        put_own(d, r.lhs, 0, d.feat, r.mw1.at[0], n_blk, r.cols[:, 0:1])
         r.lhs[d.feat :, d.feat :] = r.extra[p, b]
         out = mm(r.lhs[...], r.tt[...])
         att = out[d.feat : d.feat + 1]
@@ -569,10 +554,13 @@
         @pl.when(first)
         def _():
             r.n_cat[: d.half] = r.n_own[p]
-
+            put_table(d, r.lhs, 0, d.feat, r.n_cat, r.uw1.at[0])
+            put_table(d, r.lhs, d.feat, d.feat, r.n_cat, r.mw1.at[1])
+
+        r.ready()
         n_blk = r.n_own[p, pl.ds(pl.multiple_of(b * d.res, d.res), d.res), :]
-        put_table(d, r.lhs, 0, d.feat, r.n_cat, r.uw1.at[0], n_blk, r.e_cols[:, 4:5], first)
-        put_table(d, r.lhs, d.feat, d.feat, r.n_cat, r.mw1.at[1], n_blk, r.d_cols[:, 0:1], first)
+        put_own(d, r.lhs, 0, d.feat, r.uw1.at[0], n_blk, r.e_cols[:, 4:5])
+        put_own(d, r.lhs, d.feat, d.feat, r.mw1.at[1], n_blk, r.d_cols[:, 0:1])
         put_one_hot(d, r.tt, d.feat, r.idx[p, b])
         edge_t = r.edge[...].reshape(d.rows, d.feat).T
         r.tt[: d.feat, :] = edge_t
@@ -708,11 +696,13 @@
         def _():
             r.n_cat[: d.half] = r.n_own[p]
             r.n_cat[d.half :] = r.n_got[p]
+            put_table(d, r.lhs, 0, 0, r.n_cat, r.uw1.at[1])
             zero(r.a_s)
 
+        r.ready()
+        f = d.feat
         n_blk = r.n_own[p, pl.ds(pl.multiple_of(b * d.res, d.res), d.res), :]
-        put_table(d, r.lhs, 0, 0, r.n_cat, r.uw1.at[1], n_blk, r.cols[:, 4:5], first)
-        f = d.feat
+        put_own(d, r.lhs, 0, 0, r.uw1.at[1], n_blk, r.cols[:, 4:5])
         idx = r.idx[p, b]
         put_one_hot(d, r.tt, 0, idx)
         put_one_hot_rows(d, r.tn, idx)
@@ -829,6 +819,7 @@
             node_backward(d, r, p, 1, r.d_aux[...], dn)
 
         f = d.feat
+        r.ready()
         put_one_hot_rows(d, r.tn, r.idx[p, b])
         message_backward(d, r, b, 1, r.both.at[:f])
         r.msg[f : 2 * f] += mm(r.e2[...], r.both[:f], 1, 1)
@@ -910,6 +901,7 @@
             node_backward(d, r, p, 0, r.aux[...], r.dn_a[p] + r.dn_b[p].astype(F32))
 
         f = d.feat
+        r.ready()
         put_one_hot_rows(d, r.tn, r.idx[p, b])
         message_backward(d, r, b, 0, r.da1)
         r.a_w1[...] += mm(r.da1[...], r.edge[...].reshape(d.rows, f))

time: 230 us -> 209 us (0.909)
  Pallas kernels: 222 us -> 201 us
    pallas_call x5, Pallas kernels: 183 us -> 162 us  [call(): pl.pallas_call(kernel, grid=(d.parts, d.blocks), in_specs=[s for _, _, s...]
where the time goes in v3:
time: 209 us
  Pallas kernels  201 us (96%)
  local copies, waits for them, and re-layouts  4.21 us (2%)
  other arithmetic  2.52 us (1%)
    pallas_call x5, Pallas kernels, call(): pl.pallas_call(kernel, grid=(d.parts, d.blocks), in_specs=[s for _, _, s...  162 us
    pallas_call x1, Pallas kernels, reduce_grads(): pl.pallas_call(kernel, in_specs=[vm] * 5, out_specs=[vm, pl.BlockSpec(mem...  36.6 us

profile of v3, /device:TPU:0, one launch (start us, length us, event | category | flops | bytes accessed | tf_op | source)
XLA Modules:
  0.0 208.8 jit_solution(17559482853803226111)
XLA Ops:
  0.7 0.1 pad.9.clone
  0.7 0.8 fusion.6
  1.6 0.8 fusion.7
  2.4 0.8 fusion.3
  3.2 0.1 neg.16
  3.3 0.7 fusion.2.refs_4_
  4.0 1.0 compare_select_fusion
  5.0 0.1 copy.35
  5.2 0.8 reshape.57.refs_1_.refs_2_.refs_14_.refs_11_
  6.0 0.8 broadcast_in_dim.10.refs_3_.refs_4_.refs_6_
  6.8 30.0 %enc_message.1 = (bf16[2,3,144,3072]{3,2,1,0:T(8,128)(2,1)}, bf16[2,3,128,3072]{3,2,1,0:T(8,128)(2,1)}, bf16[2,3,128,3072]{3,2,1,0:T(8,128)(2,1)}, f32[2,3,1,307...) custom-call(bf16[2,192,128]{2,1,0:T(8,128)(2,1)} %refs_2_.2, ...), custom_call_target="tpu_custom_call" | custom-call | tf_op jit(solution)/shard_map/enc_message/pallas_call | solution.py:184
  36.7 36.9 %enc_update.1 = (bf16[2,3,144,3072]{3,2,1,0:T(8,128)(2,1)}, bf16[2,3,128,3072]{3,2,1,0:T(8,128)(2,1)}, bf16[2,3,144,3072]{3,2,1,0:T(8,128)(2,1)}, bf16[2,3,128,3...) custom-call(bf16[2,192,128]{2,1,0:T(8,128)(2,1)} %get-tuple-element., ...), custom_call_target="tpu_custom_call" | custom-call | tf_op jit(solution)/shard_map/enc_update/pallas_call | solution.py:184
  73.6 31.9 %dec_update.1 = (bf16[2,192,48,128]{3,2,1,0:T(8,128)(2,1)}, bf16[2,3,128,3072]{3,2,1,0:T(8,128)(2,1)}, f32[672,128]{1,0:T(8,128)}, f32[2,192,128]{2,1,0:T(8,128)}, bf16[2,192,128]{2,1,0:T(8,128)(2,1)}) custom-call(bf16[2,192,128]{2,1,0:T(8,128)(2,1)} %get-tuple-element.177.refs_0_, bf16[2,192,128]{2,1,0:T(8,128)(2,1)} %get-tuple-element.99.refs_1_, ...), custom_call_target="tpu_custom_call" | custom-call | tf_op jit(solution)/shard_map/dec_update/pallas_call | solution.py:184
  105.5 41.6 %dec_message_back.1 = (bf16[2,3,128,3072]{3,2,1,0:T(8,128)(2,1)}, f32[1696,128]{1,0:T(8,128)}, f32[672,128]{1,0:T(8,128)}, f32[2,192,128]{2,1,0:T(8,128)}, bf16[2,192,128]{2,1,0:T(8,128)(2,1)}) custom-call(bf16[2,192,128]{2,1,0:T(8,128)(2,1)} %refs_0_.3, f32[2,192,128]{2,1,0:T(8,128)} %get-tuple-element.102.refs_1_, ...), custom_call_target="tpu_custom_call" | custom-call | tf_op jit(solution)/shard_map/dec_message_back/pallas_call | solution.py:184
  147.1 0.0 copy-start
  147.1 22.2 %enc_message_back.1 = (bf16[2,192,48,128]{3,2,1,0:T(8,128)(2,1)}, f32[1696,128]{1,0:T(8,128)}, f32[2,192,128]{2,1,0:T(8,128)}, bf16[2,192,128]{2,1,0:T(8,128)(2,1)}) custom-call(f32[2,192,128]{2,1,0:T(8,128)} %get-tuple-element.120.refs_0_, bf16[2,192,128]{2,1,0:T(8,128)(2,1)} %get-tuple-element.121.refs_1_, bf16[2,192,128]{2,1,0:T(8,128)(2,1)} %refs_2_.2, ...), custom_call_target="tpu_custom_call" | custom-call | tf_op jit(solution)/shard_map/enc_message_back/pallas_call | solution.py:184
  169.3 36.6 %reduce.1 = (bf16[2560,128]{1,0:T(8,128)(2,1)}, bf16[2,192,128]{2,1,0:T(8,128)(2,1)}) custom-call(f32[1696,128]{1,0:T(8,128)} %get-tuple-element.132.em, f32[672,128]{1,0:T(8,128)} %get-tuple-element.133.eu, f32[1696,128]{1,0:T(8,128)} %get-tuple-element.134.dm, f32[672,128]{1,0:T(8,128)} %get-tuple-element.135.du, bf16[2,192,128]{2,1,0:T(8,128)(2,1)} %get-tuple-element.136.far), custom_call_target="tpu_custom_call" | custom-call | tf_op jit(solution)/shard_map/reduce/pallas_call | solution.py:1054
  205.9 2.3 %unpack.1 = (bf16[2,192,128]{2,1,0:T(8,128)(2,1)}, f32[1,384,128]{2,1,0:T(8,128)}, f32[1,128,128]{2,1,0:T(8,128)}, f32[1,128,128]{2,1,0:T(8,128)}, f32[1,128,512...) custom-call(bf16[2560,128]{1,0:T(8,128)(2,1)} %get-tuple-element.137, ...), custom_call_target="tpu_custom_call" | custom-call | tf_op jit(solution)/shard_map/unpack/pallas_call | solution.py:1093
  208.2 0.0 copy-done
  208.2 0.6 copy.43
  (5 shorter events, 0.0 us)
Async XLA Ops:
  147.1 61.1 %copy-start = (bf16[2,192,128]{2,1,0:T(8,128)(2,1)S(1)}, bf16[2,192,128]{2,1,0:T(8,128)(2,1)}, u32[]{:S(2)}) copy-start(bf16[2,192,128]{2,1,0:T(8,128)(2,1)} %get-tuple-element.177.refs_0_) | copy-start | bytes 294916

commit v4 on v3

--- a/solution.py
+++ b/solution.py
@@ -96,6 +96,10 @@
         self.raw(**arrays)
         self.kinds.update({n: (False, False, a.shape[2:], a.dtype) for n, a in arrays.items()})
 
+    def stream_top(self, rows, **arrays):
+        self.raw(**arrays)
+        self.kinds.update({n: (False, False, (rows,) + a.shape[3:], a.dtype) for n, a in arrays.items()})
+
     def edges(self, **arrays):
         self.raw(**arrays)
         block = (self.d.res, self.d.near, self.d.feat)
@@ -137,10 +141,12 @@
             now = lax.rem(step, 2)
 
             def copy(i, n, at, slot):
-                out, edges, _, _ = self.kinds[n]
+                out, edges, block, _ = self.kinds[n]
                 p, b = at // d.blocks, lax.rem(at, d.blocks)
                 if edges:
                     far = plain[n].at[p, pl.ds(pl.multiple_of(b * d.res, d.res), d.res)]
+                elif block[0] < plain[n].shape[2]:
+                    far = plain[n].at[p, b, pl.ds(0, block[0])]
                 else:
                     far = plain[n].at[p, b]
                 near = slots[i].at[slot]
@@ -168,11 +174,13 @@
                 for i, n in into:
                     copy(i, n, step, now).wait()
 
-            plain_or_slot = dict(plain, ready=ready)
+            def flush():
+                for i, n in outof:
+                    copy(i, n, step, now).start()
+
+            plain_or_slot = dict(plain, ready=ready, flush=flush)
             plain_or_slot.update({n: slots[i].at[now] for i, n in enumerate(self.kinds)})
             body(types.SimpleNamespace(**plain_or_slot))
-            for i, n in outof:
-                copy(i, n, step, now).start()
 
             @pl.when(step == steps - 1)
             def _():
@@ -257,12 +265,15 @@
     lhs[at : at + d.feat, left + d.length :] = own.astype(BF)
 
 
-def message_part(a1, w2t, b2, att):
+def message_part(a1, w2t, b2, att, kept):
     g1, d1 = gelu_pair(a1)
     a2 = mm(w2t, g1) + b2
     g2, d2 = gelu_pair(a2)
     attb = att.astype(BF)
-    return g1, d1, g2 * attb, d2 * attb
+    feat, rows = g2.shape
+    kept[:feat] = g2 * attb
+    kept[feat:] = jnp.broadcast_to(attb, (16, rows))
+    return g1, d1, d2 * attb
 
 
 def add_node_outs(ph, d):
@@ -271,12 +282,11 @@
     ph.out_whole(F32, r1=shape, ip=(d.parts, d.half, d.wide), r2=shape, big=shape, cnt=shape)
 
 
-def node_step(d, r, p, b, g2m, att, rt):
-    big = mm(rt, g2m, 1, 1) * 0.5
-    cnt = mm(rt, jnp.broadcast_to(att.astype(BF), (16, att.shape[1])), 1, 1)
+def node_step(d, r, p, b):
+    sums = mm(r.rt[: d.res], r.kept[...], 1, 1)
     at = pl.ds(pl.multiple_of(b * d.res, d.res), d.res)
-    r.big[p, at, :] = big
-    r.cnt[p, at, :] = jnp.broadcast_to(cnt[:, 0:1], big.shape)
+    r.big[p, at, :] = sums[:, : d.feat] * 0.5
+    r.cnt[p, at, :] = jnp.broadcast_to(sums[:, d.feat : d.feat + 1], (d.res, d.feat))
 
 
 def node_forward(r, p, n_own, layer, aux):
@@ -337,9 +347,42 @@
     r.dub[...] = dub
 
 
-def encoder_message(d, edge_input, node_input, weights, consts):
+def own_first(d, row):
+    row = row.astype(F32)
+    if row.shape[0] == 1:
+        row = jnp.broadcast_to(row, (8, d.length))
+    return jnp.where(lax.axis_index(AXIS_S) == 0, row, pltpu.roll(row, d.half, 1))
+
+
+def put_positions(d, r):
+    section = lax.axis_index(AXIS_S)
+    centre = d.length // 2
+    line = lax.broadcasted_iota(jnp.int32, (8, d.length), 0)
+    for p in range(d.parts):
+        live = own_first(d, r.live[p : p + 1, :])
+        order = own_first(d, r.order[p : p + 1, :]) - centre
+        code = jnp.where(live > 0.5, order, float(centre))
+        r.codes[p, :8] = jnp.where(line == 0, live, jnp.where(line == 1, code, 0.0)).astype(BF)
+        r.codes[p, 8:] = jnp.zeros((EXTRA - 8, d.length), BF)
+        ids = own_first(d, r.near[p]) - float(d.half) * section.astype(F32)
+        ids = jnp.where(ids < 0.0, ids + float(d.length), ids) - float(centre)
+        r.mask[p] = jnp.broadcast_to(live[0:1], (d.feat, d.length)).T[: d.half]
+        for b in range(d.blocks):
+            own = pltpu.roll(order, (d.length - b * d.res) % d.length, 1) if b else order
+            r.owns[p, b, :8] = jnp.where(line == 1, -own, 0.0)[:, : d.res].astype(BF)
+            r.owns[p, b, 8:] = jnp.zeros((EXTRA - 8, d.res), BF)
+            block = pltpu.roll(ids, (d.length - b * d.res) % d.length, 1) if b else ids
+            spread = mm(block[:, : d.res].astype(BF), r.rt[: d.res])
+            row = jnp.sum(spread * r.pick[...].astype(F32), axis=0, keepdims=True)
+            r.idx[p, b] = row.astype(jnp.int32) + centre
+
+
+def encoder_message(d, edge_input, node_input, neighbors, residue_mask, decode_order, weights, consts):
     ph = Phase(d, 2)
-    ph.whole(n_own=node_input, idx=consts.idx, rt=consts.sums, mask=consts.mask, extra=consts.extra)
+    ph.whole(n_own=node_input, rt=consts.sums, pick=consts.pick, near=neighbors, live=residue_mask, order=decode_order)
+    ph.out_whole(jnp.int32, idx=(d.parts, d.blocks, 1, d.rows))
+    ph.out_whole(F32, mask=(d.parts, d.half, d.feat))
+    ph.temp(BF, codes=(d.parts, EXTRA, d.length), owns=(d.parts, d.blocks, EXTRA, d.res))
     ph.edges(edge=edge_input)
     names = tuple(weights)
     own = {W_IN + n: a for n, a in weights.items()}
@@ -355,7 +398,7 @@
     sq = (d.feat, d.feat)
     wide = d.feat + d.length + d.res
     ph.temp(BF, n_cat=(d.length, d.feat), lhs=(d.feat + EXTRA, wide), w2t=sq, tt=(wide, d.rows))
-    ph.temp(BF, leave=(d.half, d.feat), arrive=node_input.shape)
+    ph.temp(BF, leave=(d.half, d.feat), arrive=node_input.shape, kept=(d.feat + 16, d.rows))
     ph.temp(F32, aux=sq, cols=sq)
     count = len(names)
     ph.sems(send=count + 2, recv=count + 2, local=count, back=2 * count + 1)
@@ -381,9 +424,10 @@
                 for i, n in enumerate(names)
             ]
 
-        def returns():
-            out = [pltpu.make_async_copy(r.arrive, r.nodes_got, r.back.at[2 * count])]
-            for i, n in enumerate(names):
+        def returns(group):
+            out = [pltpu.make_async_copy(r.arrive, r.nodes_got, r.back.at[2 * count])] if group == GROUP_ONE else []
+            for n in group:
+                i = names.index(n)
                 src, dst = getattr(r, n), getattr(r, W_OUT + n)
                 for layer in range(2):
                     sem = r.back.at[2 * i + layer]
@@ -401,9 +445,7 @@
             for item in swaps(GROUP_ONE) + own_copies():
                 item.start()
             r.tt[d.feat + d.length :, :] = r.rt[: d.res]
-
-        @pl.when(begin)
-        def _():
+            put_positions(d, r)
             nodes.wait()
             for item in swaps(GROUP_ONE) + own_copies():
                 item.wait()
@@ -425,31 +467,33 @@
         put_one_hot(d, r.tt, d.feat, r.idx[p, b])
         r.tt[: d.feat, :] = r.edge[...].reshape(d.rows, d.feat).T
         put_own(d, r.lhs, 0, d.feat, r.mw1.at[0], n_blk, r.cols[:, 0:1])
-        r.lhs[d.feat :, d.feat :] = r.extra[p, b]
+        r.lhs[d.feat :, d.feat : d.feat + d.length] = r.codes[p]
+        r.lhs[d.feat :, d.feat + d.length :] = r.owns[p, b]
         out = mm(r.lhs[...], r.tt[...])
         att = out[d.feat : d.feat + 1]
         r.att[p, b] = jnp.where(out[d.feat + 1 : d.feat + 2] < 0.0, 1.0, 0.0)
-        g1, r.d1[...], g2m, r.d2[...] = message_part(out[: d.feat], r.w2t[...], r.cols[:, 1:2], att)
+        g1, r.d1[...], r.d2[...] = message_part(out[: d.feat], r.w2t[...], r.cols[:, 1:2], att, r.kept)
         put_ones(r.g1, g1)
-        node_step(d, r, p, b, g2m, att, r.rt[: d.res])
+        node_step(d, r, p, b)
+        r.flush()
 
         @pl.when(middle)
         def _():
             for item in swaps(GROUP_TWO):
                 item.wait()
-            for item in swaps(GROUP_THREE):
+            for item in swaps(GROUP_THREE) + returns(GROUP_ONE) + returns(GROUP_TWO):
                 item.start()
             r.leave[...] = node_forward(r, 0, r.n_own[0], 0, r.aux[...])
             job.start()
 
         @pl.when(at_end)
         def _():
-            node_forward(r, d.parts - 1, r.n_own[d.parts - 1], 0, r.aux[...])
             for item in swaps(GROUP_THREE):
                 item.wait()
-            for item in returns():
+            for item in returns(GROUP_THREE):
                 item.start()
-            for item in returns():
+            node_forward(r, d.parts - 1, r.n_own[d.parts - 1], 0, r.aux[...])
+            for item in returns(GROUP_ONE) + returns(GROUP_TWO) + returns(GROUP_THREE):
                 item.wait()
             job.wait()
 
@@ -509,8 +553,8 @@
     ph.edges(edge=edge_input)
     ph.whole(**weight_args(st, *NODE_W, *MSG_W, *UPD_W))
     act = (d.parts, d.blocks, d.feat, d.rows)
-    tall = with_ones(d)
-    ph.out_stream(BF, ug1=tall, ud1=act, ug2=tall, ud2=act, uxh=act, e2=act, g1=tall, d1=act, d2=act)
+    two = (d.parts, d.blocks, 2 * d.feat + 16, d.rows)
+    ph.out_stream(BF, ugs=two, ud1=act, ud2=act, uxh=act, e2g=two, d1=act, d2=act)
     ph.out_whole(F32, urs=(d.parts, d.blocks, 1, d.rows))
     add_node_outs(ph, d)
     ph.out_whole(BF, got_in=(d.half, d.feat))
@@ -519,7 +563,7 @@
     wide = d.feat + d.length + d.res
     ph.temp(BF, n_cat=(d.length, d.feat), lhs=(2 * d.feat, wide), tt=(wide, d.rows))
     ph.temp(BF, uw2t=sq, mw1bt=sq, mw2t=sq, w3c=(d.feat, 2 * d.feat), pair=(2 * d.feat, d.rows))
-    ph.temp(BF, leave=(d.parts, d.half, d.feat), lead=(d.half, d.feat), arrive=(d.half, d.feat))
+    ph.temp(BF, kept=(d.feat + 16, d.rows), leave=(d.parts, d.half, d.feat), lead=(d.half, d.feat), arrive=(d.half, d.feat))
     ph.temp(F32, w3c_b=sq, e_aux=sq, e_cols=sq, d_aux=sq, d_cols=sq)
     ph.sems(send=d.parts + 1, recv=d.parts + 1)
 
@@ -569,14 +613,16 @@
         g1, d1, g2, d2, xh, rs, e2 = update_forward(
             d, out[: d.feat], r.uw2t[...], r.w3c, r.e_cols[:, 5:6], r.w3c_b[:, 0:1], r.pair, r.e_cols
         )
-        put_ones(r.ug1, g1)
-        put_ones(r.ug2, g2)
-        r.ud1[...], r.ud2[...], r.uxh[...], r.urs[p, b], r.e2[...] = d1, d2, xh, rs, e2
+        f = d.feat
+        r.ugs[:f] = g2
+        put_ones(r.ugs.at[f:], g1)
+        r.ud1[...], r.ud2[...], r.uxh[...], r.urs[p, b], r.e2g[:f] = d1, d2, xh, rs, e2
         att = r.att[p, b]
         a1 = out[d.feat :] + mm(r.mw1bt[...], e2)
-        g1, r.d1[...], g2m, r.d2[...] = message_part(a1, r.mw2t[...], r.d_cols[:, 1:2], att)
-        put_ones(r.g1, g1)
-        node_step(d, r, p, b, g2m, att, r.rt[: d.res])
+        g1, r.d1[...], r.d2[...] = message_part(a1, r.mw2t[...], r.d_cols[:, 1:2], att, r.kept)
+        put_ones(r.e2g.at[f:], g1)
+        node_step(d, r, p, b)
+        r.flush()
 
         @pl.when(last)
         def _():
@@ -628,11 +674,12 @@
     return (scaled - jnp.mean(scaled, axis=0, keepdims=True)).astype(BF)
 
 
-def update_backward(d, r, dr3, g1, d1, g2, d2, w2, w3, da1):
-    r.a_w3[...] += mm(g2, dr3, 1, 1)
-    da2 = mm(w3, dr3).astype(BF) * d2
-    r.a_w2[...] += mm(g1, da2, 1, 1)
-    da1[...] = mm(w2, da2).astype(BF) * d1
+def update_backward(d, r, dr3, gs, d1, d2, w2, w3, low, da1):
+    f = d.feat
+    low[:f] = dr3
+    low[f:] = mm(w3, dr3).astype(BF) * d2
+    r.a_w23[...] += mm(gs, low[...], 1, 1)
+    da1[...] = mm(w2, low[f:]).astype(BF) * d1
 
 
 def update_small(d, r, b4):
@@ -642,10 +689,10 @@
 
     @pl.when(pl.program_id(0) == d.parts - 1)
     def _():
-        r.upd[3 * f : 4 * f] = 0.5 * r.a_w2[:f]
-        r.upd[4 * f : 5 * f] = 0.5 * r.a_w3[:f]
-        r.upd[at + 5 : at + 6] = r.a_w2[f : f + 1]
-        r.upd[at + 6 : at + 7] = r.a_w3[f : f + 1]
+        r.upd[3 * f : 4 * f] = 0.5 * r.a_w23[f : 2 * f, f:]
+        r.upd[4 * f : 5 * f] = 0.5 * r.a_w23[:f, :f]
+        r.upd[at + 5 : at + 6] = r.a_w23[2 * f : 2 * f + 1, f:]
+        r.upd[at + 6 : at + 7] = r.a_w23[2 * f : 2 * f + 1, :f]
         r.upd[at + 9 : at + 10] = to_row(r.a_b9[...])
         r.upd[at + 12 : at + 13] = to_row(r.a_g2[...])
 
@@ -658,19 +705,18 @@
 def decoder_update(d, st, fb, cot, consts):
     ph = Phase(d)
     ph.whole(n_own=fb.node_out, n_got=fb.got, idx=consts.idx, rt=consts.sums)
-    ph.stream(e2=fb.e2)
+    ph.stream_top(d.feat, e2=fb.e2g)
     ph.edges(cot=cot)
     ph.whole(**weight_args(st, *UPD_W, *AUX_W))
     ph.out_edges(decoded=cot.shape)
     ph.out_stream(BF, part=(d.parts, d.blocks, d.feat, d.rows))
     ph.out_whole(F32, upd=(d.upd_rows, d.feat), dn_own=(d.parts, d.half, d.feat))
-    ph.out_whole(BF, dn_far=(d.parts, d.half, d.feat))
+    ph.out_whole(BF, dn_far=(d.parts, d.half, d.feat), nodes=(d.parts, d.half, d.feat))
     sq = (d.feat, d.feat)
     ph.temp(BF, n_cat=(d.length, d.feat), lhs=(d.feat, d.length + d.res), w1bt=sq, w2t=sq, w2h=sq, w3h=sq)
     ph.temp(BF, tt=(d.length + d.res, d.rows), tn=(d.rows, d.length + 128), da1=(d.feat, d.rows))
-    ph.temp(BF, w3c=(d.feat, 2 * d.feat), gain_mat=sq, pair=(2 * d.feat + 16, d.rows), one=(d.feat + 16, d.rows))
-    tall = (d.feat + 16, d.feat)
-    ph.temp(F32, w3c_b=sq, aux=sq, cols=sq, a_w2=tall, a_w3=tall, a_b9=sq, a_g2=sq)
+    ph.temp(BF, w3c=(d.feat, 2 * d.feat), gain_mat=sq, pair=(3 * d.feat + 16, d.rows), low=(2 * d.feat, d.rows))
+    ph.temp(F32, w3c_b=sq, aux=sq, cols=sq, a_w23=(2 * d.feat + 16, 2 * d.feat), a_b9=sq, a_g2=sq)
     ph.temp(F32, a_s=(d.feat, d.length), a_k=(d.blocks, d.feat, 128))
 
     def body(r):
@@ -679,6 +725,7 @@
 
         @pl.when(first & (p == 0))
         def _():
+            r.nodes[...] = r.n_own[...]
             r.w1bt[...] = r.uw1[1, d.feat : 2 * d.feat, :].T
             r.w2h[...] = half_of(r.uw2[1])
             r.w2t[...] = r.w2h[...].T
@@ -686,9 +733,8 @@
             load_cols(r, 1, r.aux, r.cols)
             centre_weights(r.uw3[1], r.cols[...], r.w3c, r.w3c_b)
             r.gain_mat[...] = gain_matrix(r.cols[...])
-            zero(r.upd, r.a_w2, r.a_w3, r.a_b9, r.a_g2)
-            r.pair[2 * d.feat :] = jnp.ones((16, d.rows), BF)
-            r.one[d.feat :] = jnp.ones((16, d.rows), BF)
+            zero(r.upd, r.a_w23, r.a_b9, r.a_g2)
+            r.pair[3 * d.feat :] = jnp.ones((16, d.rows), BF)
             r.tt[d.length :, :] = r.rt[: d.res]
             r.tn[:, d.length :] = r.rt[...].T
 
@@ -712,16 +758,17 @@
         g1, d1, _, d2, xh, rs, y = update_forward(
             d, a1, r.w2t[...], r.w3c, r.cols[:, 5:6], r.w3c_b[:, 0:1], r.pair, r.cols
         )
-        r.one[:f] = g1
+        r.pair[2 * f : 3 * f] = g1
         r.decoded[...] = y.T.reshape(d.res, d.near, f)
         dy = r.cot[...].reshape(d.rows, f).T
         dr3 = norm_backward(d, r, dy, xh, rs, r.gain_mat[...])
-        update_backward(d, r, dr3, r.one[...], d1, r.pair[f:], d2, r.w2h[...], r.w3h[...], r.da1)
+        update_backward(d, r, dr3, r.pair[f:], d1, d2, r.w2h[...], r.w3h[...], r.low, r.da1)
         r.upd[f : 2 * f] += mm(e2, r.da1[...], 1, 1)
         r.part[...] = (mm(r.uw1[1, f : 2 * f, :], r.da1[...]) + dr3.astype(F32)).astype(BF)
         spread = mm(r.da1[...], r.tn[...])
         r.a_s[...] += spread[:, : d.length]
         r.a_k[b] = spread[:, d.length :]
+        r.flush()
 
         @pl.when(last)
         def _():
@@ -738,23 +785,16 @@
 AUX_W = ("bias", "gain")
 
 
-def message_backward(d, r, b, layer, da1):
+def message_backward(d, r, b, layer, low):
     at = pl.ds(pl.multiple_of(b * d.res, d.res), d.res)
     v = (mm(r.mw3[layer], r.dub[at, :], 1, 1) * 0.5).astype(BF)
-    da2 = mm(v, r.rt[: d.res]).astype(BF) * r.d2[...]
-    r.m_w2[...] += mm(r.g1[...], da2, 1, 1)
-    da1[...] = mm(r.mw2h[...], da2).astype(BF) * r.d1[...]
+    f = d.feat
+    low[:f] = mm(v, r.rt[: d.res]).astype(BF) * r.d2[...]
+    low[f:] = mm(r.mw2h[...], low[:f]).astype(BF) * r.d1[...]
 
 
 def message_small(d, r, b0):
-    f = d.feat
-    at = d.at_small
-    r.msg[at : at + 1] += b0
-
-    @pl.when(pl.program_id(0) == d.parts - 1)
-    def _():
-        r.msg[3 * f : 4 * f] = 0.5 * r.m_w2[:f]
-        r.msg[at + 1 : at + 2] = r.m_w2[f : f + 1]
+    r.msg[d.at_small : d.at_small + 1] += b0
 
 
 def middle_backward(d, edge_input, st, fa, fb, fd, cot_n, consts):
@@ -762,8 +802,7 @@
     ph.whole(cot_n=cot_n, dn_a=fd.dn_own, dn_far_in=fd.dn_far, n_own=fa.node_out, got_a=fa.got, got_b=fb.got_in)
     ph.whole(mask=consts.mask, rt=consts.sums, r1=fb.r1, ip=fb.ip, r2=fb.r2, big=fb.big, cnt=fb.cnt)
     ph.whole(urs=fb.urs, idx=consts.idx)
-    ph.stream(d2=fb.d2, g1=fb.g1, d1=fb.d1, e2=fb.e2, dec_part=fd.part, uxh=fb.uxh)
-    ph.stream(ug2=fb.ug2, ud2=fb.ud2, ug1=fb.ug1, ud1=fb.ud1)
+    ph.stream(d2=fb.d2, d1=fb.d1, e2g=fb.e2g, dec_part=fd.part, uxh=fb.uxh, ugs=fb.ugs, ud2=fb.ud2, ud1=fb.ud1)
     ph.edges(edge=edge_input)
     ph.whole(**weight_args(st, *NODE_W, *MSG_W, *UPD_W))
     ph.out_stream(BF, part=(d.parts, d.blocks, d.feat, d.rows))
@@ -771,11 +810,11 @@
     ph.out_raw(BF, got=(d.parts, d.half, d.feat))
     sq = (d.feat, d.feat)
     ph.temp(BF, n_cat=(d.length, d.feat), dub=(d.half, d.feat), tn=(d.rows, d.length + 128))
-    ph.temp(BF, both=(2 * d.feat, d.rows), w2h=sq, w3h=sq, mw2h=sq, gain_mat=sq)
+    ph.temp(BF, tri=(3 * d.feat, d.rows), low=(2 * d.feat, d.rows), w2h=sq, w3h=sq, mw2h=sq, gain_mat=sq)
     ph.temp(BF, leave=(d.parts, d.half, d.feat), arrive=(d.parts, d.half, d.feat))
     ph.temp(F32, dr1=(d.half, d.feat), e_aux=sq, e_cols=sq, d_aux=sq, d_cols=sq)
-    tall = (d.feat + 16, d.feat)
-    ph.temp(F32, m_w2=tall, a_w2=tall, a_w3=tall, a_b9=sq, a_g2=sq, a_w1=sq)
+    tall = (2 * d.feat + 16, 2 * d.feat)
+    ph.temp(F32, m_w12=tall, a_w23=tall, a_b9=sq, a_g2=sq, a_w1=sq)
     ph.temp(F32, a_s=(2 * d.feat, d.length), a_k=(d.blocks, 2 * d.feat, 128))
     ph.sems(send=2 * d.parts, recv=2 * d.parts)
 
@@ -798,7 +837,7 @@
             r.w3h[...] = half_of(r.uw3[0])
             r.mw2h[...] = half_of(r.mw2[1])
             r.gain_mat[...] = gain_matrix(r.e_cols[...])
-            zero(r.msg, r.upd, r.m_w2, r.a_w2, r.a_w3, r.a_b9, r.a_g2, r.a_w1)
+            zero(r.msg, r.upd, r.m_w12, r.a_w23, r.a_b9, r.a_g2, r.a_w1)
             r.n_cat[d.half :] = r.got_a[...]
 
         @pl.when(first & (p == 1))
@@ -821,19 +860,19 @@
         f = d.feat
         r.ready()
         put_one_hot_rows(d, r.tn, r.idx[p, b])
-        message_backward(d, r, b, 1, r.both.at[:f])
-        r.msg[f : 2 * f] += mm(r.e2[...], r.both[:f], 1, 1)
-        de = mm(r.mw1[1, f : 2 * f, :], r.both[:f])
+        message_backward(d, r, b, 1, r.tri.at[: 2 * f])
+        r.m_w12[...] += mm(r.e2g[...], r.tri[: 2 * f], 1, 1)
+        de = mm(r.mw1[1, f : 2 * f, :], r.tri[f : 2 * f])
         dy = (de + r.dec_part[...].astype(F32)).astype(BF)
         dr3 = norm_backward(d, r, dy, r.uxh[...], r.urs[p, b], r.gain_mat[...])
-        update_backward(
-            d, r, dr3, r.ug1[...], r.ud1[...], r.ug2[...], r.ud2[...], r.w2h[...], r.w3h[...], r.both.at[f:]
-        )
-        r.a_w1[...] += mm(r.both[f:], r.edge[...].reshape(d.rows, f))
-        r.part[...] = (mm(r.uw1[0, f : 2 * f, :], r.both[f:]) + dr3.astype(F32)).astype(BF)
-        spread = mm(r.both[...], r.tn[...])
+        da1 = r.tri.at[2 * f :]
+        update_backward(d, r, dr3, r.ugs[...], r.ud1[...], r.ud2[...], r.w2h[...], r.w3h[...], r.low, da1)
+        r.a_w1[...] += mm(da1[...], r.edge[...].reshape(d.rows, f))
+        r.part[...] = (mm(r.uw1[0, f : 2 * f, :], da1[...]) + dr3.astype(F32)).astype(BF)
+        spread = mm(r.tri[f:], r.tn[...])
         r.a_s[...] += spread[:, : d.length]
         r.a_k[b] = spread[:, d.length :]
+        r.flush()
 
         @pl.when(last)
         def _():
@@ -858,7 +897,11 @@
 
             @pl.when(p == n - 1)
             def _():
-                r.upd[d.feat : 2 * d.feat] = r.a_w1[...].T
+                f, at = d.feat, d.at_small
+                r.upd[f : 2 * f] = r.a_w1[...].T
+                r.msg[f : 2 * f] = r.m_w12[:f, f:]
+                r.msg[3 * f : 4 * f] = 0.5 * r.m_w12[f : 2 * f, :f]
+                r.msg[at + 1 : at + 2] = r.m_w12[2 * f : 2 * f + 1, :f]
                 for job in jobs:
                     job.wait()
 
@@ -878,7 +921,7 @@
     ph.out_whole(BF, dn_far=(d.parts, d.half, d.feat))
     sq = (d.feat, d.feat)
     ph.temp(BF, n_cat=(d.length, d.feat), dub=(d.half, d.feat), tn=(d.rows, d.length + 128))
-    ph.temp(BF, da1=(d.feat, d.rows), mw2h=sq)
+    ph.temp(BF, low=(2 * d.feat, d.rows), mw2h=sq)
     ph.temp(F32, dr1=(d.half, d.feat), aux=sq, cols=sq, a_w1=sq, m_w2=(d.feat + 16, d.feat))
     ph.temp(F32, a_s=(d.feat, d.length), a_k=(d.blocks, d.feat, 128))
 
@@ -903,14 +946,17 @@
         f = d.feat
         r.ready()
         put_one_hot_rows(d, r.tn, r.idx[p, b])
-        message_backward(d, r, b, 0, r.da1)
-        r.a_w1[...] += mm(r.da1[...], r.edge[...].reshape(d.rows, f))
-        de = mm(r.mw1[0, f : 2 * f, :], r.da1[...])
+        message_backward(d, r, b, 0, r.low)
+        da1 = r.low.at[f:]
+        r.m_w2[...] += mm(r.g1[...], r.low[:f], 1, 1)
+        r.a_w1[...] += mm(da1[...], r.edge[...].reshape(d.rows, f))
+        de = mm(r.mw1[0, f : 2 * f, :], da1[...])
         de = (de + r.up_part[...].astype(F32)).astype(BF)
         r.edge_grad[...] = de.T.reshape(d.res, d.near, f)
-        spread = mm(r.da1[...], r.tn[...])
+        spread = mm(da1[...], r.tn[...])
         r.a_s[...] += spread[:, : d.length]
         r.a_k[b] = spread[:, d.length :]
+        r.flush()
 
         @pl.when(last)
         def _():
@@ -923,7 +969,10 @@
 
             @pl.when(p == d.parts - 1)
             def _():
-                r.msg[d.feat : 2 * d.feat] = r.a_w1[...].T
+                f, at = d.feat, d.at_small
+                r.msg[f : 2 * f] = r.a_w1[...].T
+                r.msg[3 * f : 4 * f] = 0.5 * r.m_w2[:f]
+                r.msg[at + 1 : at + 2] = r.m_w2[f : f + 1]
 
     return ph.call("enc_message_back", body)
 
@@ -1115,8 +1164,6 @@
     biases,
     norm_gains,
 ):
-    section = lax.axis_index(AXIS_S)
-    is_first = section == 0
     parts, half, near, feat = edge_input.shape
     length = neighbors.shape[1]
     wide = inner_w.shape[2]
@@ -1136,28 +1183,14 @@
         uw1=update_w1[0], uw2=update_w2[0], uw3=update_w3[0],
         bias=biases.transpose(1, 0, 2), gain=norm_gains.transpose(1, 0, 2),
     )
-    own_ids = lax.dynamic_slice_in_dim(neighbors, section * half, half, 1) - section * half
-    idx_row = jnp.where(own_ids < 0, own_ids + length, own_ids).reshape(parts, blocks, 1, rows)
     sums = np.zeros((128, rows), np.float32)
     sums[np.arange(rows) // near, np.arange(rows)] = 1.0
-    sums = jnp.asarray(sums, BF)
-
-    def own_first(x):
-        return jnp.where(is_first, x, jnp.roll(x, half, axis=1))
-
-    live = own_first(residue_mask)
-    order = own_first(decode_order)
-    centre = length // 2
-    code = jnp.where(live == 1, order - centre, centre)
-    own_code = (order[:, :half] - centre).reshape(parts, blocks, 1, res)
-    lead = (parts, blocks, 1, length)
-    top = jnp.pad(jnp.broadcast_to(live[:, None, None, :], lead), ((0, 0), (0, 0), (0, 0), (0, res)))
-    second = jnp.concatenate([jnp.broadcast_to(code[:, None, None, :], lead), -own_code], axis=3)
-    extra = jnp.concatenate([top, second, jnp.zeros((parts, blocks, EXTRA - 2, length + res), top.dtype)], axis=2)
-    mask = jnp.broadcast_to(live[:, :half, None].astype(F32), (parts, half, feat))
-    consts = types.SimpleNamespace(extra=extra.astype(BF), sums=sums, mask=mask, idx=idx_row)
-
-    fa = encoder_message(d, edge_input, node_input, weights, consts)
+    pick = (np.arange(rows)[None, :] % near == np.arange(near)[:, None]).astype(np.float32)
+    consts = types.SimpleNamespace(sums=jnp.asarray(sums, BF), pick=jnp.asarray(pick, BF))
+    fa = encoder_message(
+        d, edge_input, node_input, neighbors.transpose(0, 2, 1), residue_mask, decode_order, weights, consts
+    )
+    consts.idx, consts.mask = fa.idx, fa.mask
     st = types.SimpleNamespace(**{n: getattr(fa, W_OUT + n) for n in weights})
     fb = encoder_update(d, edge_input, st, fa, consts)
     fd = decoder_update(d, st, fb, edge_cotangent, consts)
@@ -1168,7 +1201,7 @@
         d, total, ff.dn_own, got, biases.shape[1], norm_gains.shape[1]
     )
     return (
-        fb.node_out, fd.decoded, node_grad, ff.edge_grad, mw1, mw2, mw3, inner, inner_b[:, 0], outer,
+        fd.nodes, fd.decoded, node_grad, ff.edge_grad, mw1, mw2, mw3, inner, inner_b[:, 0], outer,
         uw1, uw2, uw3, bias.transpose(1, 0, 2), gain.transpose(1, 0, 2),
     )
 

time: 209 us -> 193 us (0.923)
  Pallas kernels: 201 us -> 191 us
  local copies, waits for them, and re-layouts: 4.21 us -> 0 us
  other arithmetic: 2.52 us -> 0 us
    pallas_call x5, Pallas kernels: 162 us -> 153 us  [call(): pl.pallas_call(kernel, grid=(d.parts, d.blocks), in_specs=[s for _, _, s...]
where the time goes in v4:
time: 193 us; the launch traced here: 192 us
  Pallas kernels  191 us (99%)
    pallas_call x5, Pallas kernels, call(): pl.pallas_call(kernel, grid=(d.parts, d.blocks), in_specs=[s for _, _, s...  153 us
    pallas_call x1, Pallas kernels, reduce_grads(): pl.pallas_call(kernel, in_specs=[vm] * 5, out_specs=[vm, pl.BlockSpec(mem...  36.4 us

profile of v4, /device:TPU:0, one launch (start us, length us, event | category | flops | bytes accessed | tf_op | source)
XLA Modules:
  0.0 192.2 jit_solution(11093807057374464946)
XLA Ops:
  0.7 29.3 %enc_message.1 = (s32[2,3,1,3072]{3,2,1,0:T(1,128)}, f32[2,192,128]{2,1,0:T(8,128)}, bf16[2,3,144,3072]{3,2,1,0:T(8,128)(2,1)}, bf16[2,3,128,3072]{3,2,1,0:T(8,1...) custom-call(bf16[2,192,128]{2,1,0:T(8,128)(2,1)} %refs_2_.2, ...), custom_call_target="tpu_custom_call" | custom-call | tf_op jit(solution)/shard_map/enc_message/pallas_call | solution.py:192
  29.9 33.4 %enc_update.1 = (bf16[2,3,272,3072]{3,2,1,0:T(8,128)(2,1)}, bf16[2,3,128,3072]{3,2,1,0:T(8,128)(2,1)}, bf16[2,3,128,3072]{3,2,1,0:T(8,128)(2,1)}, bf16[2,3,128,3...) custom-call(bf16[2,192,128]{2,1,0:T(8,128)(2,1)} %get-tuple-element., ...), custom_call_target="tpu_custom_call" | custom-call | tf_op jit(solution)/shard_map/enc_update/pallas_call | solution.py:192
  63.3 30.7 %dec_update.1 = (bf16[2,192,48,128]{3,2,1,0:T(8,128)(2,1)}, bf16[2,3,128,3072]{3,2,1,0:T(8,128)(2,1)}, f32[672,128]{1,0:T(8,128)}, f32[2,192,128]{2,1,0:T(8,128)...) custom-call(bf16[2,192,128]{2,1,0:T(8,128)(2,1)} %get-tuple-element.101.refs_0_, ...), custom_call_target="tpu_custom_call" | custom-call | tf_op jit(solution)/shard_map/dec_update/pallas_call | solution.py:192
  94.0 37.5 %dec_message_back.1 = (bf16[2,3,128,3072]{3,2,1,0:T(8,128)(2,1)}, f32[1696,128]{1,0:T(8,128)}, f32[672,128]{1,0:T(8,128)}, f32[2,192,128]{2,1,0:T(8,128)}, bf16[2,192,128]{2,1,0:T(8,128)(2,1)}) custom-call(bf16[2,192,128]{2,1,0:T(8,128)(2,1)} %refs_0_.3, f32[2,192,128]{2,1,0:T(8,128)} %get-tuple-element.106.refs_1_, ...), custom_call_target="tpu_custom_call" | custom-call | tf_op jit(solution)/shard_map/dec_message_back/pallas_call | solution.py:192
  131.6 21.7 %enc_message_back.1 = (bf16[2,192,48,128]{3,2,1,0:T(8,128)(2,1)}, f32[1696,128]{1,0:T(8,128)}, f32[2,192,128]{2,1,0:T(8,128)}, bf16[2,192,128]{2,1,0:T(8,128)(2,1)}) custom-call(f32[2,192,128]{2,1,0:T(8,128)} %get-tuple-element.122.refs_0_, bf16[2,192,128]{2,1,0:T(8,128)(2,1)} %get-tuple-element.123.refs_1_, bf16[2,192,128]{2,1,0:T(8,128)(2,1)} %refs_2_.2, ...), custom_call_target="tpu_custom_call" | custom-call | tf_op jit(solution)/shard_map/enc_message_back/pallas_call | solution.py:192
  153.3 36.4 %reduce.1 = (bf16[2560,128]{1,0:T(8,128)(2,1)}, bf16[2,192,128]{2,1,0:T(8,128)(2,1)}) custom-call(f32[1696,128]{1,0:T(8,128)} %get-tuple-element.134.em, f32[672,128]{1,0:T(8,128)} %get-tuple-element.135.eu, f32[1696,128]{1,0:T(8,128)} %get-tuple-element.136.dm, f32[672,128]{1,0:T(8,128)} %get-tuple-element.137.du, bf16[2,192,128]{2,1,0:T(8,128)(2,1)} %get-tuple-element.138.far), custom_call_target="tpu_custom_call" | custom-call | tf_op jit(solution)/shard_map/reduce/pallas_call | solution.py:1103
  189.7 2.3 %unpack.1 = (bf16[2,192,128]{2,1,0:T(8,128)(2,1)}, f32[1,384,128]{2,1,0:T(8,128)}, f32[1,128,128]{2,1,0:T(8,128)}, f32[1,128,128]{2,1,0:T(8,128)}, f32[1,128,512...) custom-call(bf16[2560,128]{1,0:T(8,128)(2,1)} %get-tuple-element.139, ...), custom_call_target="tpu_custom_call" | custom-call | tf_op jit(solution)/shard_map/unpack/pallas_call | solution.py:1142

commit v5 on v4

--- a/solution.py
+++ b/solution.py
@@ -80,14 +80,15 @@
     def __init__(self, dims, collective_id=None):
         self.d = dims
         self.collective_id = collective_id
-        self.ins, self.outs, self.temps, self.kinds = [], [], [], {}
+        self.ins, self.outs, self.temps, self.kinds, self.wholes = [], [], [], {}, {}
 
     def whole_spec(self, shape):
         rank = len(shape)
         return pl.BlockSpec(tuple(shape), lambda p, b: (0,) * rank)
 
     def whole(self, **arrays):
-        self.ins += [(n, a, self.whole_spec(a.shape)) for n, a in arrays.items()]
+        self.raw(**arrays)
+        self.wholes.update({n: pltpu.VMEM(a.shape, a.dtype) for n, a in arrays.items()})
 
     def raw(self, **arrays):
         self.ins += [(n, a, pl.BlockSpec(memory_space=pl.ANY)) for n, a in arrays.items()]
@@ -135,7 +136,8 @@
         count = len(self.kinds)
 
         def kernel(*refs):
-            refs, slots, sems = refs[: len(names)], refs[len(names) : len(names) + count], refs[len(names) + count :]
+            refs, rest = refs[: len(names)], refs[len(names) :]
+            slots, sems, kept = rest[:count], rest[count : 2 * count], rest[2 * count : -1]
             plain = dict(zip(names, refs))
             step = pl.program_id(0) * d.blocks + pl.program_id(1)
             now = lax.rem(step, 2)
@@ -155,8 +157,19 @@
             into = [(i, n) for i, n in enumerate(self.kinds) if not self.kinds[n][0]]
             outof = [(i, n) for i, n in enumerate(self.kinds) if self.kinds[n][0]]
 
+            def loads():
+                return [
+                    pltpu.make_async_copy(plain[n], kept[i], rest[-1].at[i]) for i, n in enumerate(self.wholes)
+                ]
+
+            def load():
+                for item in loads():
+                    item.wait()
+
             @pl.when(step == 0)
             def _():
+                for item in loads():
+                    item.start()
                 for i, n in into:
                     copy(i, n, step, now).start()
 
@@ -178,7 +191,8 @@
                 for i, n in outof:
                     copy(i, n, step, now).start()
 
-            plain_or_slot = dict(plain, ready=ready, flush=flush)
+            plain_or_slot = dict(plain, ready=ready, flush=flush, load=load)
+            plain_or_slot.update(zip(self.wholes, kept))
             plain_or_slot.update({n: slots[i].at[now] for i, n in enumerate(self.kinds)})
             body(types.SimpleNamespace(**plain_or_slot))
 
@@ -195,7 +209,10 @@
             in_specs=[s for _, _, s in self.ins],
             out_specs=[s for _, _, s in self.outs],
             out_shape=[s for _, s, _ in self.outs],
-            scratch_shapes=[s for _, s in self.temps] + buffers + [pltpu.SemaphoreType.DMA((2,))] * count,
+            scratch_shapes=[s for _, s in self.temps] + buffers
+            + [pltpu.SemaphoreType.DMA((2,))] * count
+            + list(self.wholes.values())
+            + [pltpu.SemaphoreType.DMA((len(self.wholes),))],
             compiler_params=pltpu.CompilerParams(
                 dimension_semantics=(pltpu.ARBITRARY,) * 2,
                 vmem_limit_bytes=60 << 20,
@@ -311,11 +328,14 @@
 
 
 def node_backward(d, r, p, layer, aux, dn):
-    r1, ip, r2, big, cnt = r.r1[p], r.ip[p], r.r2[p], r.big[p], r.cnt[p]
+    def rows_of(ref):
+        return ref[...].reshape(-1, ref.shape[2]) if p is None else ref[p]
+
+    r1, ip, r2, big, cnt = rows_of(r.r1), rows_of(r.ip), rows_of(r.r2), rows_of(r.big), rows_of(r.cnt)
     xh1, rs1 = norm_rows(r1)
     normed = xh1 * aux[10:11] + aux[7:8]
     xh2, rs2 = norm_rows(r2)
-    dy2 = dn * r.mask[p]
+    dy2 = dn * rows_of(r.mask)
     dr2 = norm_back_rows(dy2 * aux[11:12], xh2, rs2)
     low_outer = dr2.astype(BF)
     hid, slope = gelu_pair_wide(ip)
@@ -343,8 +363,12 @@
         rows[16 + i] = dib[:, i * d.feat : (i + 1) * d.feat]
     for row, value in rows.items():
         r.msg[d.at_small + row : d.at_small + row + 1] += value
-    r.dr1[...] = dr1
-    r.dub[...] = dub
+    if p is None:
+        r.dr1[...] = dr1.reshape(r.dr1.shape)
+        r.dub[...] = dub.reshape(r.dub.shape)
+    else:
+        r.dr1[p] = dr1
+        r.dub[p] = dub
 
 
 def own_first(d, row):
@@ -379,6 +403,7 @@
 
 def encoder_message(d, edge_input, node_input, neighbors, residue_mask, decode_order, weights, consts):
     ph = Phase(d, 2)
+    ph.raw(n_far=node_input)
     ph.whole(n_own=node_input, rt=consts.sums, pick=consts.pick, near=neighbors, live=residue_mask, order=decode_order)
     ph.out_whole(jnp.int32, idx=(d.parts, d.blocks, 1, d.rows))
     ph.out_whole(F32, mask=(d.parts, d.half, d.feat))
@@ -408,7 +433,7 @@
         first, last = b == 0, b == d.blocks - 1
         section = lax.axis_index(AXIS_S)
         job = to_partner(r.leave, r.got, r.send.at[count], r.recv.at[count])
-        nodes = to_partner(r.n_own, r.arrive, r.send.at[count + 1], r.recv.at[count + 1])
+        nodes = to_partner(r.n_far, r.arrive, r.send.at[count + 1], r.recv.at[count + 1])
 
         def swaps(group):
             out = []
@@ -444,6 +469,7 @@
             nodes.start()
             for item in swaps(GROUP_ONE) + own_copies():
                 item.start()
+            r.load()
             r.tt[d.feat + d.length :, :] = r.rt[: d.res]
             put_positions(d, r)
             nodes.wait()
@@ -549,6 +575,7 @@
 
 def encoder_update(d, edge_input, st, fa, consts):
     ph = Phase(d, 3)
+    ph.raw(n_far=fa.node_out)
     ph.whole(n_own=fa.node_out, got_a=fa.got, idx=consts.idx, rt=consts.sums, mask=consts.mask, att=fa.att)
     ph.edges(edge=edge_input)
     ph.whole(**weight_args(st, *NODE_W, *MSG_W, *UPD_W))
@@ -563,21 +590,21 @@
     wide = d.feat + d.length + d.res
     ph.temp(BF, n_cat=(d.length, d.feat), lhs=(2 * d.feat, wide), tt=(wide, d.rows))
     ph.temp(BF, uw2t=sq, mw1bt=sq, mw2t=sq, w3c=(d.feat, 2 * d.feat), pair=(2 * d.feat, d.rows))
-    ph.temp(BF, kept=(d.feat + 16, d.rows), leave=(d.parts, d.half, d.feat), lead=(d.half, d.feat), arrive=(d.half, d.feat))
+    ph.temp(BF, kept=(d.feat + 16, d.rows), leave=(d.parts, d.half, d.feat), arrive=(d.half, d.feat))
     ph.temp(F32, w3c_b=sq, e_aux=sq, e_cols=sq, d_aux=sq, d_cols=sq)
     ph.sems(send=d.parts + 1, recv=d.parts + 1)
 
     def body(r):
         p, b = pl.program_id(0), pl.program_id(1)
         first, last = b == 0, b == d.blocks - 1
-        early = to_partner(r.lead, r.arrive, r.send.at[d.parts], r.recv.at[d.parts])
+        early = to_partner(r.n_far.at[d.parts - 1], r.arrive, r.send.at[d.parts], r.recv.at[d.parts])
         jobs = [to_partner(r.leave.at[i], r.got.at[i], r.send.at[i], r.recv.at[i]) for i in range(d.parts)]
 
         @pl.when(first & (p == 0))
         def _():
             greet_partner()
-            r.lead[...] = r.n_own[d.parts - 1]
             early.start()
+            r.load()
             r.tt[d.feat + d.length :, :] = r.rt[: d.res]
             r.lhs[: d.feat, : d.feat] = r.uw1[0, d.feat : 2 * d.feat, :].T
             r.lhs[d.feat :, : d.feat] = jnp.zeros((d.feat, d.feat), BF)
@@ -713,8 +740,9 @@
     ph.out_whole(F32, upd=(d.upd_rows, d.feat), dn_own=(d.parts, d.half, d.feat))
     ph.out_whole(BF, dn_far=(d.parts, d.half, d.feat), nodes=(d.parts, d.half, d.feat))
     sq = (d.feat, d.feat)
-    ph.temp(BF, n_cat=(d.length, d.feat), lhs=(d.feat, d.length + d.res), w1bt=sq, w2t=sq, w2h=sq, w3h=sq)
-    ph.temp(BF, tt=(d.length + d.res, d.rows), tn=(d.rows, d.length + 128), da1=(d.feat, d.rows))
+    wide = d.length + d.res
+    ph.temp(BF, n_cat=(d.length, d.feat), lhs=(d.feat, wide), w1bt=sq, w2t=sq, w2h=sq, w3h=sq)
+    ph.temp(BF, tt=(wide, d.rows), tn=(d.rows, d.length + 128), da1=(d.feat, d.rows))
     ph.temp(BF, w3c=(d.feat, 2 * d.feat), gain_mat=sq, pair=(3 * d.feat + 16, d.rows), low=(2 * d.feat, d.rows))
     ph.temp(F32, w3c_b=sq, aux=sq, cols=sq, a_w23=(2 * d.feat + 16, 2 * d.feat), a_b9=sq, a_g2=sq)
     ph.temp(F32, a_s=(d.feat, d.length), a_k=(d.blocks, d.feat, 128))
@@ -725,6 +753,7 @@
 
         @pl.when(first & (p == 0))
         def _():
+            r.load()
             r.nodes[...] = r.n_own[...]
             r.w1bt[...] = r.uw1[1, d.feat : 2 * d.feat, :].T
             r.w2h[...] = half_of(r.uw2[1])
@@ -787,7 +816,7 @@
 
 def message_backward(d, r, b, layer, low):
     at = pl.ds(pl.multiple_of(b * d.res, d.res), d.res)
-    v = (mm(r.mw3[layer], r.dub[at, :], 1, 1) * 0.5).astype(BF)
+    v = (mm(r.mw3[layer], r.dub[pl.program_id(0), at, :], 1, 1) * 0.5).astype(BF)
     f = d.feat
     low[:f] = mm(v, r.rt[: d.res]).astype(BF) * r.d2[...]
     low[f:] = mm(r.mw2h[...], low[:f]).astype(BF) * r.d1[...]
@@ -799,7 +828,8 @@
 
 def middle_backward(d, edge_input, st, fa, fb, fd, cot_n, consts):
     ph = Phase(d, 4)
-    ph.whole(cot_n=cot_n, dn_a=fd.dn_own, dn_far_in=fd.dn_far, n_own=fa.node_out, got_a=fa.got, got_b=fb.got_in)
+    ph.raw(dn_far_in=fd.dn_far)
+    ph.whole(cot_n=cot_n, dn_a=fd.dn_own, n_own=fa.node_out, got_a=fa.got, got_b=fb.got_in)
     ph.whole(mask=consts.mask, rt=consts.sums, r1=fb.r1, ip=fb.ip, r2=fb.r2, big=fb.big, cnt=fb.cnt)
     ph.whole(urs=fb.urs, idx=consts.idx)
     ph.stream(d2=fb.d2, d1=fb.d1, e2g=fb.e2g, dec_part=fd.part, uxh=fb.uxh, ugs=fb.ugs, ud2=fb.ud2, ud1=fb.ud1)
@@ -809,10 +839,10 @@
     ph.out_whole(F32, msg=(d.msg_rows, d.feat), upd=(d.upd_rows, d.feat), dn_own=(d.parts, d.half, d.feat))
     ph.out_raw(BF, got=(d.parts, d.half, d.feat))
     sq = (d.feat, d.feat)
-    ph.temp(BF, n_cat=(d.length, d.feat), dub=(d.half, d.feat), tn=(d.rows, d.length + 128))
+    ph.temp(BF, n_cat=(d.length, d.feat), dub=(d.parts, d.half, d.feat), tt=(d.length + d.res, d.rows))
     ph.temp(BF, tri=(3 * d.feat, d.rows), low=(2 * d.feat, d.rows), w2h=sq, w3h=sq, mw2h=sq, gain_mat=sq)
     ph.temp(BF, leave=(d.parts, d.half, d.feat), arrive=(d.parts, d.half, d.feat))
-    ph.temp(F32, dr1=(d.half, d.feat), e_aux=sq, e_cols=sq, d_aux=sq, d_cols=sq)
+    ph.temp(F32, dr1=(d.parts, d.half, d.feat), e_aux=sq, e_cols=sq, d_aux=sq, d_cols=sq)
     tall = (2 * d.feat + 16, 2 * d.feat)
     ph.temp(F32, m_w12=tall, a_w23=tall, a_b9=sq, a_g2=sq, a_w1=sq)
     ph.temp(F32, a_s=(2 * d.feat, d.length), a_k=(d.blocks, 2 * d.feat, 128))
@@ -830,9 +860,10 @@
             greet_partner()
             for job in early:
                 job.start()
+            r.load()
             load_cols(r, 0, r.e_aux, r.e_cols)
             load_cols(r, 1, r.d_aux, r.d_cols)
-            r.tn[:, d.length :] = r.rt[...].T
+            r.tt[d.length :, :] = r.rt[: d.res]
             r.w2h[...] = half_of(r.uw2[0])
             r.w3h[...] = half_of(r.uw3[0])
             r.mw2h[...] = half_of(r.mw2[1])
@@ -859,7 +890,7 @@
 
         f = d.feat
         r.ready()
-        put_one_hot_rows(d, r.tn, r.idx[p, b])
+        put_one_hot(d, r.tt, 0, r.idx[p, b])
         message_backward(d, r, b, 1, r.tri.at[: 2 * f])
         r.m_w12[...] += mm(r.e2g[...], r.tri[: 2 * f], 1, 1)
         de = mm(r.mw1[1, f : 2 * f, :], r.tri[f : 2 * f])
@@ -869,9 +900,9 @@
         update_backward(d, r, dr3, r.ugs[...], r.ud1[...], r.ud2[...], r.w2h[...], r.w3h[...], r.low, da1)
         r.a_w1[...] += mm(da1[...], r.edge[...].reshape(d.rows, f))
         r.part[...] = (mm(r.uw1[0, f : 2 * f, :], da1[...]) + dr3.astype(F32)).astype(BF)
-        spread = mm(r.tri[f:], r.tn[...])
+        spread = mm(r.tri[f:], r.tt[...], 1, 1)
         r.a_s[...] += spread[:, : d.length]
-        r.a_k[b] = spread[:, d.length :]
+        r.a_k[b, :, : d.res] = spread[:, d.length :]
         r.flush()
 
         @pl.when(last)
@@ -884,7 +915,7 @@
             own_u, far_u, b4 = spread_nodes(
                 d, r.a_s[d.feat :], [x[d.feat :] for x in a_k], r.uw1[0], n_cat, r.upd, 0
             )
-            r.dn_own[p] = own_m + own_u + r.dr1[...]
+            r.dn_own[p] = own_m + own_u + r.dr1[p]
             r.leave[p] = (far_m + far_u).astype(BF)
             for i in range(n):
 
@@ -920,9 +951,9 @@
     ph.out_whole(F32, msg=(d.msg_rows, d.feat), dn_own=(d.parts, d.half, d.feat))
     ph.out_whole(BF, dn_far=(d.parts, d.half, d.feat))
     sq = (d.feat, d.feat)
-    ph.temp(BF, n_cat=(d.length, d.feat), dub=(d.half, d.feat), tn=(d.rows, d.length + 128))
+    ph.temp(BF, n_cat=(d.length, d.feat), dub=(d.parts, d.half, d.feat), tn=(d.rows, d.length + 128))
     ph.temp(BF, low=(2 * d.feat, d.rows), mw2h=sq)
-    ph.temp(F32, dr1=(d.half, d.feat), aux=sq, cols=sq, a_w1=sq, m_w2=(d.feat + 16, d.feat))
+    ph.temp(F32, dr1=(d.parts, d.half, d.feat), aux=sq, cols=sq, a_w1=sq, m_w2=(d.feat + 16, d.feat))
     ph.temp(F32, a_s=(d.feat, d.length), a_k=(d.blocks, d.feat, 128))
 
     def body(r):
@@ -931,17 +962,19 @@
 
         @pl.when(first & (p == 0))
         def _():
+            r.load()
             load_cols(r, 0, r.aux, r.cols)
             r.tn[:, d.length :] = r.rt[...].T
             r.mw2h[...] = half_of(r.mw2[0])
             zero(r.msg, r.m_w2, r.a_w1)
+            dn = r.dn_a[...] + r.dn_b[...].astype(F32)
+            node_backward(d, r, None, 0, r.aux[...], dn.reshape(-1, d.feat))
 
         @pl.when(first)
         def _():
             r.n_cat[: d.half] = r.n_own[p]
             r.n_cat[d.half :] = r.n_got[p]
             zero(r.a_s)
-            node_backward(d, r, p, 0, r.aux[...], r.dn_a[p] + r.dn_b[p].astype(F32))
 
         f = d.feat
         r.ready()
@@ -963,7 +996,7 @@
             own, far, b0 = spread_nodes(
                 d, r.a_s[...], [r.a_k[i] for i in range(d.blocks)], r.mw1[0], r.n_cat[...], r.msg, 0
             )
-            r.dn_own[p] = own + r.dr1[...]
+            r.dn_own[p] = own + r.dr1[p]
             r.dn_far[p] = far.astype(BF)
             message_small(d, r, b0)
 
@@ -977,138 +1010,187 @@
     return ph.call("enc_message_back", body)
 
 
+class Reducer:
+    def __init__(self, devices, feat, shares):
+        self.feat = feat
+        self.bits = bits = devices.bit_length() - 1
+        self.groups = [16 * devices * share for share in shares]
+        self.rows = sum(self.groups)
+        self.bases = [sum(self.groups[:i]) for i in range(len(shares))]
+        pairs, top = [], bits
+        while top > 1:
+            low = max(1, top - 2)
+            pairs.insert(0, (low, top - low))
+            top = low
+        dims = [ACROSS] + pairs
+        turn = min(3, len(dims))
+        self.plans = []
+        for g, size in enumerate(self.groups):
+            head = dims[:turn]
+            order = ([(0, 1)] if bits else []) + head[g % turn :] + head[: g % turn] + dims[turn:]
+            both, plan = True, []
+            for dim in order:
+                if dim == ACROSS:
+                    both = False
+                else:
+                    size >>= dim[1]
+                plan.append((dim, size, both))
+            self.plans.append(plan)
+        self.backs = [[step for step in reversed(plan) if step[0] != ACROSS] for plan in self.plans]
+        self.halving = len(self.plans[0])
+        self.stages = self.halving + len(self.backs[0])
+        self.dims = ([(0, 1)] if bits else []) + dims
+        self.sem_at, self.buffer_at, self.shapes = {}, {}, []
+        for g, plan in enumerate(self.plans):
+            for k, (dim, size, both) in enumerate(plan):
+                for o in self.offsets(dim):
+                    self.sem_at[(g, k, o)] = len(self.sem_at)
+                    self.buffer_at[(g, k, o)] = len(self.shapes)
+                    self.shapes += [(2, size, feat) if both else (size, feat)] * 2
+            for k, (dim, _, _) in enumerate(self.backs[g]):
+                for o in self.offsets(dim):
+                    self.sem_at[(g, self.halving + k, o)] = len(self.sem_at)
+
+    def scratch(self):
+        temps = [pltpu.VMEM((2, self.rows, self.feat), F32), pltpu.VMEM((self.rows, self.feat), BF)]
+        temps += [pltpu.VMEM(shape, BF) for shape in self.shapes]
+        return temps + [pltpu.SemaphoreType.DMA((len(self.sem_at),))] * 2
+
+    def bind(self, refs):
+        self.acc, self.gathered = refs[:2]
+        self.buffers, (self.send, self.recv) = refs[2:-2], refs[-2:]
+
+    def offsets(self, dim):
+        return range(1, 2 if dim == ACROSS else 1 << dim[1])
+
+    def code(self, dim):
+        return lax.rem(lax.axis_index(AXIS_D) // (1 << dim[0]), 1 << dim[1])
+
+    def peer(self, dim, o):
+        if dim == ACROSS:
+            return other_section()
+        code = self.code(dim)
+        other = lax.rem(code + o, 1 << dim[1])
+        return {AXIS_D: lax.axis_index(AXIS_D) + (other - code) * (1 << dim[0])}
+
+    def greet(self):
+        barrier = pltpu.get_barrier_semaphore()
+        count = 0
+        for dim in self.dims:
+            for o in self.offsets(dim):
+                pl.semaphore_signal(barrier, inc=1, device_id=self.peer(dim, o), device_id_type=MESH)
+                count += 1
+        pl.semaphore_wait(barrier, count)
+
+    def begin(self, g, k):
+        start = self.bases[g]
+        for dim, size, _ in self.plans[g][:k]:
+            if dim != ACROSS:
+                start = start + self.code(dim) * size
+        return start
+
+    def span(self, start, size):
+        return pl.ds(pl.multiple_of(start, 16), size)
+
+    def job(self, src, dst, key, dim):
+        at = self.sem_at[key]
+        return pltpu.make_async_remote_copy(
+            src_ref=src, dst_ref=dst, send_sem=self.send.at[at], recv_sem=self.recv.at[at],
+            device_id=self.peer(dim, key[2]), device_id_type=MESH,
+        )
+
+    def jobs(self, g, k):
+        plan = self.plans[g]
+        if k < self.halving:
+            out = []
+            for o in self.offsets(plan[k][0]):
+                at = self.buffer_at[(g, k, o)]
+                out.append(self.job(self.buffers[at], self.buffers[at + 1], (g, k, o), plan[k][0]))
+            return out
+        dim, size, _ = self.backs[g][k - self.halving]
+        start = self.begin(g, [step[0] for step in plan].index(dim) + 1)
+        part = self.gathered.at[self.span(start, size), :]
+        return [self.job(part, part, (g, k, o), dim) for o in self.offsets(dim)]
+
+    def start(self, g, k):
+        section = lax.axis_index(AXIS_S)
+        plan = self.plans[g]
+        if k < self.halving:
+            dim, size, both = plan[k]
+            start = self.begin(g, k)
+            for o in self.offsets(dim):
+                out = self.buffers[self.buffer_at[(g, k, o)]]
+                if dim == ACROSS:
+                    out[...] = self.acc[1 - section, self.span(start, size), :].astype(BF)
+                    continue
+                give = self.span(start + lax.rem(self.code(dim) + o, 1 << dim[1]) * size, size)
+                if both:
+                    out[...] = self.acc[:, give, :].astype(BF)
+                else:
+                    out[...] = self.acc[section, give, :].astype(BF)
+        elif k == self.halving:
+            keep = self.span(self.begin(g, self.halving), plan[-1][1])
+            self.gathered[keep, :] = self.acc[section, keep, :].astype(BF)
+        for job in self.jobs(g, k):
+            job.start()
+
+    def finish(self, g, k):
+        section = lax.axis_index(AXIS_S)
+        for job in self.jobs(g, k):
+            job.wait()
+        if k >= self.halving:
+            return
+        dim, size, both = self.plans[g][k]
+        keep = self.span(self.begin(g, k + 1), size)
+        for o in self.offsets(dim):
+            into = self.buffers[self.buffer_at[(g, k, o)] + 1]
+            if both:
+                self.acc[:, keep, :] += into[...].astype(F32)
+            else:
+                self.acc[section, keep, :] += into[...].astype(F32)
+
+    def run(self):
+        count = len(self.plans)
+        for g in range(count):
+            self.start(g, 0)
+        for k in range(self.stages):
+            for g in range(count):
+                self.finish(g, k)
+                if k + 1 < self.stages:
+                    self.start(g, k + 1)
+        if self.stages == self.halving:
+            self.gathered[...] = self.acc[lax.axis_index(AXIS_S)].astype(BF)
+
+
+ACROSS = (-1, 0)
+
+
 def reduce_grads(d, enc_msg, enc_upd, dec_msg, dec_upd, dn_far):
-    devices = d.devices
-    bits = devices.bit_length() - 1
-    unit = 16 * devices
-    feat = d.feat
-    need = -(-(d.msg_rows + d.upd_rows) // unit)
-    shares = [need // 3 + (1 if need % 3 > i else 0) for i in range(3)]
-    groups = [unit * share for share in shares if share]
-    rows = sum(groups)
-    bases = [sum(groups[:i]) for i in range(len(groups))]
-    across = -1
-    dims = [across] + list(range(1, bits))
-    turn = min(3, len(dims))
-    orders = []
-    for g in range(len(groups)):
-        head = dims[:turn]
-        head = head[g % turn :] + head[: g % turn]
-        orders.append(([0] if bits else []) + head + dims[turn:])
-    stages = len(orders[0])
-    plans = []
-    for g, order in enumerate(orders):
-        size, both, plan = groups[g], True, []
-        for dim in order:
-            if dim == across:
-                both = False
-                plan.append((dim, size, False))
-            else:
-                size //= 2
-                plan.append((dim, size, both))
-        plans.append(plan)
-    turns = len(groups) * stages
-
-    def kernel(em, eu, dm, du, far, res, got, acc, gathered, *rest):
-        buffers, (send, recv) = rest[: 2 * turns], rest[2 * turns :]
-        section, me = lax.axis_index(AXIS_S), lax.axis_index(AXIS_D)
-
-        def flag(bit):
-            return lax.rem(me // (1 << bit), 2)
-
-        def peer(dim):
-            if dim == across:
-                return other_section()
-            return {AXIS_D: me + (1 - 2 * flag(dim)) * (1 << dim)}
-
-        barrier = pltpu.get_barrier_semaphore()
-        for dim in [across] + list(range(bits)):
-            pl.semaphore_signal(barrier, inc=1, device_id=peer(dim), device_id_type=MESH)
-        pl.semaphore_wait(barrier, bits + 1)
-
-        def remote(src, dst, at, dim):
-            return pltpu.make_async_remote_copy(
-                src_ref=src, dst_ref=dst, send_sem=send.at[at], recv_sem=recv.at[at],
-                device_id=peer(dim), device_id_type=MESH,
-            )
-
-        nodes = remote(far, got, 2 * turns, across)
+    m, u = d.msg_rows, d.upd_rows
+    units = -(-(m + u) // (16 * d.devices))
+    red = Reducer(d.devices, d.feat, [2] * (units // 2) + [1] * (units % 2))
+
+    def kernel(em, eu, dm, du, far, res, got, far_sems, *refs):
+        red.bind(refs)
+        red.greet()
+        nodes = to_partner(far, got, far_sems.at[0], far_sems.at[1])
         nodes.start()
-        m, u = d.msg_rows, d.upd_rows
         for layer, (msg, upd) in enumerate(((em, eu), (dm, du))):
-            acc[layer, :m] = msg[...]
-            acc[layer, m : m + u] = upd[...]
-            if rows > m + u:
-                acc[layer, m + u :] = jnp.zeros((rows - m - u, feat), F32)
-
-        def span(start, size):
-            return pl.ds(pl.multiple_of(start, 16), size)
-
-        starts = list(bases)
-        for k in range(stages):
-            jobs, spans = [], []
-            for g, plan in enumerate(plans):
-                dim, size, both = plan[k]
-                at = g * stages + k
-                out, into = buffers[2 * at], buffers[2 * at + 1]
-                if dim == across:
-                    keep = span(starts[g], size)
-                    out[...] = acc[1 - section, keep, :].astype(BF)
-                else:
-                    side = flag(dim)
-                    keep = span(starts[g] + side * size, size)
-                    give = span(starts[g] + (1 - side) * size, size)
-                    if both:
-                        out[...] = acc[:, give, :].astype(BF)
-                    else:
-                        out[...] = acc[section, give, :].astype(BF)
-                    starts[g] = starts[g] + side * size
-                job = remote(out, into, at, dim)
-                job.start()
-                jobs.append(job)
-                spans.append(keep)
-            for g, plan in enumerate(plans):
-                dim, size, both = plan[k]
-                jobs[g].wait()
-                into = buffers[2 * (g * stages + k) + 1]
-                if both:
-                    acc[:, spans[g], :] += into[...].astype(F32)
-                else:
-                    acc[section, spans[g], :] += into[...].astype(F32)
-        sizes = [plan[-1][1] for plan in plans]
-        for g in range(len(groups)):
-            keep = span(starts[g], sizes[g])
-            gathered[keep, :] = acc[section, keep, :].astype(BF)
-        backs = [[step for step in reversed(plan) if step[0] != across] for plan in plans]
-        for k in range(bits):
-            jobs = []
-            for g, back in enumerate(backs):
-                dim, size, _ = back[k]
-                part = gathered.at[span(starts[g], size), :]
-                job = remote(part, part, turns + g * bits + k, dim)
-                job.start()
-                jobs.append(job)
-                starts[g] = starts[g] - flag(dim) * size
-            for job in jobs:
-                job.wait()
-        res[...] = gathered[...]
+            red.acc[layer, :m] = msg[...]
+            red.acc[layer, m : m + u] = upd[...]
+            if red.rows > m + u:
+                red.acc[layer, m + u :] = jnp.zeros((red.rows - m - u, d.feat), F32)
+        red.run()
+        res[...] = red.gathered[...]
         nodes.wait()
 
     vm = pl.BlockSpec(memory_space=pltpu.VMEM)
-    scratch = [pltpu.VMEM((2, rows, feat), F32), pltpu.VMEM((rows, feat), BF)]
-    for plan in plans:
-        for _, size, both in plan:
-            scratch += [pltpu.VMEM((2, size, feat) if both else (size, feat), BF)] * 2
-    scratch += [pltpu.SemaphoreType.DMA((2 * turns + 1,))] * 2
     return pl.pallas_call(
         kernel,
         in_specs=[vm] * 5,
         out_specs=[vm, pl.BlockSpec(memory_space=pl.ANY)],
-        out_shape=[
-            jax.ShapeDtypeStruct((rows, feat), BF),
-            jax.ShapeDtypeStruct(dn_far.shape, BF),
-        ],
-        scratch_shapes=scratch,
+        out_shape=[jax.ShapeDtypeStruct((red.rows, d.feat), BF), jax.ShapeDtypeStruct(dn_far.shape, BF)],
+        scratch_shapes=[pltpu.SemaphoreType.DMA((2,))] + red.scratch(),
         compiler_params=pltpu.CompilerParams(vmem_limit_bytes=58 << 20, collective_id=5, has_side_effects=True),
         name="reduce",
     )(enc_msg, enc_upd, dec_msg, dec_upd, dn_far)

time: 193 us -> 179 us (0.927)
  Pallas kernels: 191 us -> 178 us
    pallas_call x1, Pallas kernels: 36.4 us -> 28.3 us  [reduce_grads(): pl.pallas_call(kernel, in_specs=[vm] * 5, out_specs=[vm, pl.BlockSpec(mem...]
    pallas_call x5, Pallas kernels: 153 us -> 148 us  [call(): pl.pallas_call(kernel, grid=(d.parts, d.blocks), in_specs=[s for _, _, s...]
where the time goes in v5:
time: 179 us
  Pallas kernels  178 us (99%)
    pallas_call x5, Pallas kernels, call(): pl.pallas_call(kernel, grid=(d.parts, d.blocks), in_specs=[s for _, _, s...  148 us
    pallas_call x1, Pallas kernels, reduce_grads(): pl.pallas_call(kernel, in_specs=[vm] * 5, out_specs=[vm, pl.BlockSpec(mem...  28.3 us

profile of v5, /device:TPU:0, one launch (start us, length us, event | category | flops | bytes accessed | tf_op | source)
XLA Modules:
  0.0 179.2 jit_solution(10313978413868969537)
XLA Ops:
  0.7 28.2 %enc_message.1 = (s32[2,3,1,3072]{3,2,1,0:T(1,128)}, f32[2,192,128]{2,1,0:T(8,128)}, bf16[2,3,144,3072]{3,2,1,0:T(8,128)(2,1)}, bf16[2,3,128,3072]{3,2,1,0:T(8,1...) custom-call(bf16[2,192,128]{2,1,0:T(8,128)(2,1)} %refs_2_.2, ...), custom_call_target="tpu_custom_call" | custom-call | tf_op jit(solution)/shard_map/enc_message/pallas_call | solution.py:206
  28.9 31.9 %enc_update.1 = (bf16[2,3,272,3072]{3,2,1,0:T(8,128)(2,1)}, bf16[2,3,128,3072]{3,2,1,0:T(8,128)(2,1)}, bf16[2,3,128,3072]{3,2,1,0:T(8,128)(2,1)}, bf16[2,3,128,3...) custom-call(bf16[2,192,128]{2,1,0:T(8,128)(2,1)} %get-tuple-element., ...), custom_call_target="tpu_custom_call" | custom-call | tf_op jit(solution)/shard_map/enc_update/pallas_call | solution.py:206
  60.8 30.1 %dec_update.1 = (bf16[2,192,48,128]{3,2,1,0:T(8,128)(2,1)}, bf16[2,3,128,3072]{3,2,1,0:T(8,128)(2,1)}, f32[672,128]{1,0:T(8,128)}, f32[2,192,128]{2,1,0:T(8,128)...) custom-call(bf16[2,192,128]{2,1,0:T(8,128)(2,1)} %get-tuple-element.101.refs_0_, ...), custom_call_target="tpu_custom_call" | custom-call | tf_op jit(solution)/shard_map/dec_update/pallas_call | solution.py:206
  90.9 36.1 %dec_message_back.1 = (bf16[2,3,128,3072]{3,2,1,0:T(8,128)(2,1)}, f32[1696,128]{1,0:T(8,128)}, f32[672,128]{1,0:T(8,128)}, f32[2,192,128]{2,1,0:T(8,128)}, bf16[2,192,128]{2,1,0:T(8,128)(2,1)}) custom-call(bf16[2,192,128]{2,1,0:T(8,128)(2,1)} %get-tuple-element.106.refs_0_, bf16[2,192,128]{2,1,0:T(8,128)(2,1)} %refs_1_.3, ...), custom_call_target="tpu_custom_call" | custom-call | tf_op jit(solution)/shard_map/dec_message_back/pallas_call | solution.py:206
  127.1 21.4 %enc_message_back.1 = (bf16[2,192,48,128]{3,2,1,0:T(8,128)(2,1)}, f32[1696,128]{1,0:T(8,128)}, f32[2,192,128]{2,1,0:T(8,128)}, bf16[2,192,128]{2,1,0:T(8,128)(2,1)}) custom-call(f32[2,192,128]{2,1,0:T(8,128)} %get-tuple-element.122.refs_0_, bf16[2,192,128]{2,1,0:T(8,128)(2,1)} %get-tuple-element.123.refs_1_, bf16[2,192,128]{2,1,0:T(8,128)(2,1)} %refs_2_.2, ...), custom_call_target="tpu_custom_call" | custom-call | tf_op jit(solution)/shard_map/enc_message_back/pallas_call | solution.py:206
  148.5 28.3 %reduce.1 = (bf16[2560,128]{1,0:T(8,128)(2,1)}, bf16[2,192,128]{2,1,0:T(8,128)(2,1)}) custom-call(f32[1696,128]{1,0:T(8,128)} %get-tuple-element.134.em, f32[672,128]{1,0:T(8,128)} %get-tuple-element.135.eu, f32[1696,128]{1,0:T(8,128)} %get-tuple-element.136.dm, f32[672,128]{1,0:T(8,128)} %get-tuple-element.137.du, bf16[2,192,128]{2,1,0:T(8,128)(2,1)} %get-tuple-element.138.far), custom_call_target="tpu_custom_call" | custom-call | tf_op jit(solution)/shard_map/reduce/pallas_call | solution.py:1188
  176.8 2.3 %unpack.1 = (bf16[2,192,128]{2,1,0:T(8,128)(2,1)}, f32[1,384,128]{2,1,0:T(8,128)}, f32[1,128,128]{2,1,0:T(8,128)}, f32[1,128,128]{2,1,0:T(8,128)}, f32[1,128,512...) custom-call(bf16[2560,128]{1,0:T(8,128)(2,1)} %get-tuple-element.139, ...), custom_call_target="tpu_custom_call" | custom-call | tf_op jit(solution)/shard_map/unpack/pallas_call | solution.py:1224

commit v6 on v5

--- a/solution.py
+++ b/solution.py
@@ -80,7 +80,7 @@
     def __init__(self, dims, collective_id=None):
         self.d = dims
         self.collective_id = collective_id
-        self.ins, self.outs, self.temps, self.kinds, self.wholes = [], [], [], {}, {}
+        self.ins, self.outs, self.temps, self.kinds, self.wholes, self.later = [], [], [], {}, {}, ()
 
     def whole_spec(self, shape):
         rank = len(shape)
@@ -162,9 +162,10 @@
                     pltpu.make_async_copy(plain[n], kept[i], rest[-1].at[i]) for i, n in enumerate(self.wholes)
                 ]
 
-            def load():
-                for item in loads():
-                    item.wait()
+            def load(*later):
+                for item, n in zip(loads(), self.wholes):
+                    if (n in later) if later else (n not in self.later):
+                        item.wait()
 
             @pl.when(step == 0)
             def _():
@@ -405,10 +406,11 @@
     ph = Phase(d, 2)
     ph.raw(n_far=node_input)
     ph.whole(n_own=node_input, rt=consts.sums, pick=consts.pick, near=neighbors, live=residue_mask, order=decode_order)
+    ph.whole(edge=edge_input)
+    ph.later = (EDGE,)
     ph.out_whole(jnp.int32, idx=(d.parts, d.blocks, 1, d.rows))
     ph.out_whole(F32, mask=(d.parts, d.half, d.feat))
     ph.temp(BF, codes=(d.parts, EXTRA, d.length), owns=(d.parts, d.blocks, EXTRA, d.res))
-    ph.edges(edge=edge_input)
     names = tuple(weights)
     own = {W_IN + n: a for n, a in weights.items()}
     ph.raw(**own)
@@ -422,7 +424,7 @@
         ph.temp(a.dtype, **{n: (2,) + a.shape})
     sq = (d.feat, d.feat)
     wide = d.feat + d.length + d.res
-    ph.temp(BF, n_cat=(d.length, d.feat), lhs=(d.feat + EXTRA, wide), w2t=sq, tt=(wide, d.rows))
+    ph.temp(BF, n_cat=(d.length, d.feat), lhs=(d.feat + EXTRA, wide), w2t=sq, tt=(d.parts * d.blocks, wide, d.rows))
     ph.temp(BF, leave=(d.half, d.feat), arrive=node_input.shape, kept=(d.feat + 16, d.rows))
     ph.temp(F32, aux=sq, cols=sq)
     count = len(names)
@@ -470,12 +472,22 @@
             for item in swaps(GROUP_ONE) + own_copies():
                 item.start()
             r.load()
-            r.tt[d.feat + d.length :, :] = r.rt[: d.res]
             put_positions(d, r)
+            r.load(EDGE)
+            for q in range(d.parts):
+
+                @pl.loop(0, d.blocks)
+                def _(c, q=q):
+                    table = r.tt.at[q * d.blocks + c]
+                    put_one_hot(d, table, d.feat, r.idx[q, c])
+                    table[d.feat + d.length :, :] = r.rt[: d.res]
+                    own = r.edge[q, pl.ds(pl.multiple_of(c * d.res, d.res), d.res)]
+                    table[: d.feat, :] = own.reshape(d.rows, d.feat).T
+
             nodes.wait()
             for item in swaps(GROUP_ONE) + own_copies():
                 item.wait()
-            for item in swaps(GROUP_TWO):
+            for item in swaps(GROUP_TWO) + swaps(GROUP_THREE):
                 item.start()
             r.lhs[: d.feat, : d.feat] = r.mw1[0, d.feat : 2 * d.feat, :].T
             r.lhs[d.feat :, : d.feat] = jnp.zeros((EXTRA, d.feat), BF)
@@ -490,12 +502,10 @@
 
         n_blk = r.n_own[p, pl.ds(pl.multiple_of(b * d.res, d.res), d.res), :]
         r.ready()
-        put_one_hot(d, r.tt, d.feat, r.idx[p, b])
-        r.tt[: d.feat, :] = r.edge[...].reshape(d.rows, d.feat).T
         put_own(d, r.lhs, 0, d.feat, r.mw1.at[0], n_blk, r.cols[:, 0:1])
         r.lhs[d.feat :, d.feat : d.feat + d.length] = r.codes[p]
         r.lhs[d.feat :, d.feat + d.length :] = r.owns[p, b]
-        out = mm(r.lhs[...], r.tt[...])
+        out = mm(r.lhs[...], r.tt[p * d.blocks + b])
         att = out[d.feat : d.feat + 1]
         r.att[p, b] = jnp.where(out[d.feat + 1 : d.feat + 2] < 0.0, 1.0, 0.0)
         g1, r.d1[...], r.d2[...] = message_part(out[: d.feat], r.w2t[...], r.cols[:, 1:2], att, r.kept)
@@ -505,19 +515,15 @@
 
         @pl.when(middle)
         def _():
-            for item in swaps(GROUP_TWO):
+            for item in swaps(GROUP_TWO) + swaps(GROUP_THREE):
                 item.wait()
-            for item in swaps(GROUP_THREE) + returns(GROUP_ONE) + returns(GROUP_TWO):
+            for item in returns(GROUP_ONE) + returns(GROUP_TWO) + returns(GROUP_THREE):
                 item.start()
             r.leave[...] = node_forward(r, 0, r.n_own[0], 0, r.aux[...])
             job.start()
 
         @pl.when(at_end)
         def _():
-            for item in swaps(GROUP_THREE):
-                item.wait()
-            for item in returns(GROUP_THREE):
-                item.start()
             node_forward(r, d.parts - 1, r.n_own[d.parts - 1], 0, r.aux[...])
             for item in returns(GROUP_ONE) + returns(GROUP_TWO) + returns(GROUP_THREE):
                 item.wait()
@@ -527,6 +533,7 @@
 
 
 W_IN, W_OUT = "i_", "o_"
+EDGE = "edge"
 GROUP_ONE = ("mw1", "mw2", "bias", "gain")
 GROUP_TWO = ("mw3", "inner", "inner_b", "outer")
 GROUP_THREE = ("uw1", "uw2", "uw3")
@@ -589,7 +596,7 @@
     sq = (d.feat, d.feat)
     wide = d.feat + d.length + d.res
     ph.temp(BF, n_cat=(d.length, d.feat), lhs=(2 * d.feat, wide), tt=(wide, d.rows))
-    ph.temp(BF, uw2t=sq, mw1bt=sq, mw2t=sq, w3c=(d.feat, 2 * d.feat), pair=(2 * d.feat, d.rows))
+    ph.temp(BF, uw2t=sq, mw2t=sq, w3c=(d.feat, 2 * d.feat), pair=(2 * d.feat, d.rows))
     ph.temp(BF, kept=(d.feat + 16, d.rows), leave=(d.parts, d.half, d.feat), arrive=(d.half, d.feat))
     ph.temp(F32, w3c_b=sq, e_aux=sq, e_cols=sq, d_aux=sq, d_cols=sq)
     ph.sems(send=d.parts + 1, recv=d.parts + 1)
@@ -607,9 +614,8 @@
             r.load()
             r.tt[d.feat + d.length :, :] = r.rt[: d.res]
             r.lhs[: d.feat, : d.feat] = r.uw1[0, d.feat : 2 * d.feat, :].T
-            r.lhs[d.feat :, : d.feat] = jnp.zeros((d.feat, d.feat), BF)
+            r.lhs[d.feat :, : d.feat] = r.mw1[1, d.feat : 2 * d.feat, :].T
             r.uw2t[...] = half_of(r.uw2[0]).T
-            r.mw1bt[...] = r.mw1[1, d.feat : 2 * d.feat, :].T
             r.mw2t[...] = half_of(r.mw2[1]).T
             load_cols(r, 0, r.e_aux, r.e_cols)
             load_cols(r, 1, r.d_aux, r.d_cols)
@@ -636,16 +642,16 @@
         edge_t = r.edge[...].reshape(d.rows, d.feat).T
         r.tt[: d.feat, :] = edge_t
         r.pair[: d.feat] = edge_t
-        out = mm(r.lhs[...], r.tt[...])
         g1, d1, g2, d2, xh, rs, e2 = update_forward(
-            d, out[: d.feat], r.uw2t[...], r.w3c, r.e_cols[:, 5:6], r.w3c_b[:, 0:1], r.pair, r.e_cols
+            d, mm(r.lhs[: d.feat], r.tt[...]), r.uw2t[...], r.w3c, r.e_cols[:, 5:6], r.w3c_b[:, 0:1], r.pair, r.e_cols
         )
         f = d.feat
         r.ugs[:f] = g2
         put_ones(r.ugs.at[f:], g1)
         r.ud1[...], r.ud2[...], r.uxh[...], r.urs[p, b], r.e2g[:f] = d1, d2, xh, rs, e2
         att = r.att[p, b]
-        a1 = out[d.feat :] + mm(r.mw1bt[...], e2)
+        r.tt[:f] = e2
+        a1 = mm(r.lhs[f:], r.tt[...])
         g1, r.d1[...], r.d2[...] = message_part(a1, r.mw2t[...], r.d_cols[:, 1:2], att, r.kept)
         put_ones(r.e2g.at[f:], g1)
         node_step(d, r, p, b)
@@ -1170,27 +1176,33 @@
     units = -(-(m + u) // (16 * d.devices))
     red = Reducer(d.devices, d.feat, [2] * (units // 2) + [1] * (units % 2))
 
-    def kernel(em, eu, dm, du, far, res, got, far_sems, *refs):
+    def kernel(em, eu, dm, du, far, res, got, far_sems, load_sems, *refs):
         red.bind(refs)
+        loads = []
+        for layer, (msg, upd) in enumerate(((em, eu), (dm, du))):
+            spots = (red.acc.at[layer, pl.ds(0, m)], red.acc.at[layer, pl.ds(m, u)])
+            for i, (src, dst) in enumerate(zip((msg, upd), spots)):
+                loads.append(pltpu.make_async_copy(src, dst, load_sems.at[2 * layer + i]))
+        for item in loads:
+            item.start()
+        if red.rows > m + u:
+            red.acc[:, m + u :] = jnp.zeros((2, red.rows - m - u, d.feat), F32)
         red.greet()
         nodes = to_partner(far, got, far_sems.at[0], far_sems.at[1])
         nodes.start()
-        for layer, (msg, upd) in enumerate(((em, eu), (dm, du))):
-            red.acc[layer, :m] = msg[...]
-            red.acc[layer, m : m + u] = upd[...]
-            if red.rows > m + u:
-                red.acc[layer, m + u :] = jnp.zeros((red.rows - m - u, d.feat), F32)
+        for item in loads:
+            item.wait()
         red.run()
         res[...] = red.gathered[...]
         nodes.wait()
 
-    vm = pl.BlockSpec(memory_space=pltpu.VMEM)
+    vm, anywhere = pl.BlockSpec(memory_space=pltpu.VMEM), pl.BlockSpec(memory_space=pl.ANY)
     return pl.pallas_call(
         kernel,
-        in_specs=[vm] * 5,
-        out_specs=[vm, pl.BlockSpec(memory_space=pl.ANY)],
+        in_specs=[anywhere] * 5,
+        out_specs=[vm, anywhere],
         out_shape=[jax.ShapeDtypeStruct((red.rows, d.feat), BF), jax.ShapeDtypeStruct(dn_far.shape, BF)],
-        scratch_shapes=[pltpu.SemaphoreType.DMA((2,))] + red.scratch(),
+        scratch_shapes=[pltpu.SemaphoreType.DMA((2,)), pltpu.SemaphoreType.DMA((4,))] + red.scratch(),
         compiler_params=pltpu.CompilerParams(vmem_limit_bytes=58 << 20, collective_id=5, has_side_effects=True),
         name="reduce",
     )(enc_msg, enc_upd, dec_msg, dec_upd, dn_far)

time: 179 us -> 175 us (0.978)
  Pallas kernels: 178 us -> 174 us
    pallas_call x5, Pallas kernels: 148 us -> 145 us  [call(): pl.pallas_call(kernel, grid=(d.parts, d.blocks), in_specs=[s for _, _, s...]
where the time goes in v6:
time: 175 us
  Pallas kernels  174 us (99%)
    pallas_call x5, Pallas kernels, call(): pl.pallas_call(kernel, grid=(d.parts, d.blocks), in_specs=[s for _, _, s...  145 us
    pallas_call x1, Pallas kernels, reduce_grads(): pl.pallas_call(kernel, in_specs=[anywhere] * 5, out_specs=[vm, anywhere],...  27.2 us

profile of v6, /device:TPU:0, one launch (start us, length us, event | category | flops | bytes accessed | tf_op | source)
XLA Modules:
  0.0 175.1 jit_solution(4148032924040061171)
XLA Ops:
  0.7 26.8 %enc_message.1 = (s32[2,3,1,3072]{3,2,1,0:T(1,128)}, f32[2,192,128]{2,1,0:T(8,128)}, bf16[2,3,144,3072]{3,2,1,0:T(8,128)(2,1)}, bf16[2,3,128,3072]{3,2,1,0:T(8,1...) custom-call(bf16[2,192,128]{2,1,0:T(8,128)(2,1)} %refs_2_.2, ...), custom_call_target="tpu_custom_call" | custom-call | tf_op jit(solution)/shard_map/enc_message/pallas_call | solution.py:207
  27.5 30.6 %enc_update.1 = (bf16[2,3,272,3072]{3,2,1,0:T(8,128)(2,1)}, bf16[2,3,128,3072]{3,2,1,0:T(8,128)(2,1)}, bf16[2,3,128,3072]{3,2,1,0:T(8,128)(2,1)}, bf16[2,3,128,3...) custom-call(bf16[2,192,128]{2,1,0:T(8,128)(2,1)} %get-tuple-element., ...), custom_call_target="tpu_custom_call" | custom-call | tf_op jit(solution)/shard_map/enc_update/pallas_call | solution.py:207
  58.1 30.1 %dec_update.1 = (bf16[2,192,48,128]{3,2,1,0:T(8,128)(2,1)}, bf16[2,3,128,3072]{3,2,1,0:T(8,128)(2,1)}, f32[672,128]{1,0:T(8,128)}, f32[2,192,128]{2,1,0:T(8,128)...) custom-call(bf16[2,192,128]{2,1,0:T(8,128)(2,1)} %get-tuple-element.101.refs_0_, ...), custom_call_target="tpu_custom_call" | custom-call | tf_op jit(solution)/shard_map/dec_update/pallas_call | solution.py:207
  88.2 35.8 %dec_message_back.1 = (bf16[2,3,128,3072]{3,2,1,0:T(8,128)(2,1)}, f32[1696,128]{1,0:T(8,128)}, f32[672,128]{1,0:T(8,128)}, f32[2,192,128]{2,1,0:T(8,128)}, bf16[2,192,128]{2,1,0:T(8,128)(2,1)}) custom-call(bf16[2,192,128]{2,1,0:T(8,128)(2,1)} %get-tuple-element.106.refs_0_, bf16[2,192,128]{2,1,0:T(8,128)(2,1)} %refs_1_.3, ...), custom_call_target="tpu_custom_call" | custom-call | tf_op jit(solution)/shard_map/dec_message_back/pallas_call | solution.py:207
  124.0 21.4 %enc_message_back.1 = (bf16[2,192,48,128]{3,2,1,0:T(8,128)(2,1)}, f32[1696,128]{1,0:T(8,128)}, f32[2,192,128]{2,1,0:T(8,128)}, bf16[2,192,128]{2,1,0:T(8,128)(2,1)}) custom-call(f32[2,192,128]{2,1,0:T(8,128)} %get-tuple-element.122.refs_0_, bf16[2,192,128]{2,1,0:T(8,128)(2,1)} %get-tuple-element.123.refs_1_, bf16[2,192,128]{2,1,0:T(8,128)(2,1)} %refs_2_.2, ...), custom_call_target="tpu_custom_call" | custom-call | tf_op jit(solution)/shard_map/enc_message_back/pallas_call | solution.py:207
  145.4 27.2 %reduce.1 = (bf16[2560,128]{1,0:T(8,128)(2,1)}, bf16[2,192,128]{2,1,0:T(8,128)(2,1)}) custom-call(f32[1696,128]{1,0:T(8,128)} %get-tuple-element.134.em, f32[672,128]{1,0:T(8,128)} %get-tuple-element.135.eu, f32[1696,128]{1,0:T(8,128)} %get-tuple-element.136.dm, f32[672,128]{1,0:T(8,128)} %get-tuple-element.137.du, bf16[2,192,128]{2,1,0:T(8,128)(2,1)} %get-tuple-element.138.far), custom_call_target="tpu_custom_call" | custom-call | tf_op jit(solution)/shard_map/reduce/pallas_call | solution.py:1200
  172.6 2.3 %unpack.1 = (bf16[2,192,128]{2,1,0:T(8,128)(2,1)}, f32[1,384,128]{2,1,0:T(8,128)}, f32[1,128,128]{2,1,0:T(8,128)}, f32[1,128,128]{2,1,0:T(8,128)}, f32[1,128,512...) custom-call(bf16[2560,128]{1,0:T(8,128)(2,1)} %get-tuple-element.139, ...), custom_call_target="tpu_custom_call" | custom-call | tf_op jit(solution)/shard_map/unpack/pallas_call | solution.py:1236

commit v7 on v6

--- a/solution.py
+++ b/solution.py
@@ -13,7 +13,7 @@
 C1 = 0.7978845608
 C2 = C1 * 0.044715
 EPS = 1e-5
-BLOCK_RES = 64
+BLOCK_RES = 96
 EXTRA = 16
 SMALL = 32
 MESH = pl.DeviceIdType.MESH
@@ -428,14 +428,17 @@
     ph.temp(BF, leave=(d.half, d.feat), arrive=node_input.shape, kept=(d.feat + 16, d.rows))
     ph.temp(F32, aux=sq, cols=sq)
     count = len(names)
-    ph.sems(send=count + 2, recv=count + 2, local=count, back=2 * count + 1)
+    ph.sems(send=count + 1 + d.parts, recv=count + 1 + d.parts, local=count, back=2 * count + 1)
 
     def body(r):
         p, b = pl.program_id(0), pl.program_id(1)
         first, last = b == 0, b == d.blocks - 1
         section = lax.axis_index(AXIS_S)
         job = to_partner(r.leave, r.got, r.send.at[count], r.recv.at[count])
-        nodes = to_partner(r.n_far, r.arrive, r.send.at[count + 1], r.recv.at[count + 1])
+        nodes = [
+            to_partner(r.n_far.at[q], r.arrive.at[q], r.send.at[count + 1 + q], r.recv.at[count + 1 + q])
+            for q in range(d.parts)
+        ]
 
         def swaps(group):
             out = []
@@ -468,8 +471,7 @@
         @pl.when(begin)
         def _():
             greet_partner()
-            nodes.start()
-            for item in swaps(GROUP_ONE) + own_copies():
+            for item in nodes[:1] + swaps(GROUP_ONE) + own_copies() + nodes[1:]:
                 item.start()
             r.load()
             put_positions(d, r)
@@ -484,8 +486,7 @@
                     own = r.edge[q, pl.ds(pl.multiple_of(c * d.res, d.res), d.res)]
                     table[: d.feat, :] = own.reshape(d.rows, d.feat).T
 
-            nodes.wait()
-            for item in swaps(GROUP_ONE) + own_copies():
+            for item in nodes[:1] + swaps(GROUP_ONE) + own_copies():
                 item.wait()
             for item in swaps(GROUP_TWO) + swaps(GROUP_THREE):
                 item.start()
@@ -493,6 +494,12 @@
             r.lhs[d.feat :, : d.feat] = jnp.zeros((EXTRA, d.feat), BF)
             r.w2t[...] = half_of(r.mw2[0]).T
             load_cols(r, 0, r.aux, r.cols)
+
+        for q in range(1, d.parts):
+
+            @pl.when(first & (p == q))
+            def _(q=q):
+                nodes[q].wait()
 
         @pl.when(first)
         def _():
@@ -728,6 +735,16 @@
         r.upd[at + 6 : at + 7] = r.a_w23[2 * f : 2 * f + 1, :f]
         r.upd[at + 9 : at + 10] = to_row(r.a_b9[...])
         r.upd[at + 12 : at + 13] = to_row(r.a_g2[...])
+
+
+def block_before(d):
+    step = jnp.maximum(pl.program_id(0) * d.blocks + pl.program_id(1) - 1, 0)
+    return step // d.blocks, lax.rem(step, d.blocks)
+
+
+def put_spread(d, r, q, c, spread):
+    r.a_s[q] += spread[:, : d.length]
+    r.a_k[q, c] = spread[:, d.length :]
 
 
 def zero(*refs):
@@ -957,17 +974,17 @@
     ph.out_whole(F32, msg=(d.msg_rows, d.feat), dn_own=(d.parts, d.half, d.feat))
     ph.out_whole(BF, dn_far=(d.parts, d.half, d.feat))
     sq = (d.feat, d.feat)
-    ph.temp(BF, n_cat=(d.length, d.feat), dub=(d.parts, d.half, d.feat), tn=(d.rows, d.length + 128))
+    ph.temp(BF, dub=(d.parts, d.half, d.feat), tn=(d.rows, d.length + 128))
     ph.temp(BF, low=(2 * d.feat, d.rows), mw2h=sq)
     ph.temp(F32, dr1=(d.parts, d.half, d.feat), aux=sq, cols=sq, a_w1=sq, m_w2=(d.feat + 16, d.feat))
-    ph.temp(F32, a_s=(d.feat, d.length), a_k=(d.blocks, d.feat, 128))
+    ph.temp(F32, a_s=(d.parts, d.feat, d.length), a_k=(d.parts, d.blocks, d.feat, 128))
 
     def body(r):
         p, b = pl.program_id(0), pl.program_id(1)
-        first, last = b == 0, b == d.blocks - 1
-
-        @pl.when(first & (p == 0))
-        def _():
+
+        @pl.when((b == 0) & (p == 0))
+        def _():
+            zero(r.a_s, r.low, r.tn)
             r.load()
             load_cols(r, 0, r.aux, r.cols)
             r.tn[:, d.length :] = r.rt[...].T
@@ -976,14 +993,9 @@
             dn = r.dn_a[...] + r.dn_b[...].astype(F32)
             node_backward(d, r, None, 0, r.aux[...], dn.reshape(-1, d.feat))
 
-        @pl.when(first)
-        def _():
-            r.n_cat[: d.half] = r.n_own[p]
-            r.n_cat[d.half :] = r.n_got[p]
-            zero(r.a_s)
-
         f = d.feat
         r.ready()
+        put_spread(d, r, *block_before(d), mm(r.low[f:], r.tn[...]))
         put_one_hot_rows(d, r.tn, r.idx[p, b])
         message_backward(d, r, b, 0, r.low)
         da1 = r.low.at[f:]
@@ -992,26 +1004,22 @@
         de = mm(r.mw1[0, f : 2 * f, :], da1[...])
         de = (de + r.up_part[...].astype(F32)).astype(BF)
         r.edge_grad[...] = de.T.reshape(d.res, d.near, f)
-        spread = mm(da1[...], r.tn[...])
-        r.a_s[...] += spread[:, : d.length]
-        r.a_k[b] = spread[:, d.length :]
         r.flush()
 
-        @pl.when(last)
-        def _():
-            own, far, b0 = spread_nodes(
-                d, r.a_s[...], [r.a_k[i] for i in range(d.blocks)], r.mw1[0], r.n_cat[...], r.msg, 0
-            )
-            r.dn_own[p] = own + r.dr1[p]
-            r.dn_far[p] = far.astype(BF)
-            message_small(d, r, b0)
-
-            @pl.when(p == d.parts - 1)
-            def _():
-                f, at = d.feat, d.at_small
-                r.msg[f : 2 * f] = r.a_w1[...].T
-                r.msg[3 * f : 4 * f] = 0.5 * r.m_w2[:f]
-                r.msg[at + 1 : at + 2] = r.m_w2[f : f + 1]
+        @pl.when((b == d.blocks - 1) & (p == d.parts - 1))
+        def _():
+            put_spread(d, r, p, b, mm(da1[...], r.tn[...]))
+            for q in range(d.parts):
+                nodes = jnp.concatenate([r.n_own[q], r.n_got[q]], axis=0)
+                sums = [r.a_k[q, i] for i in range(d.blocks)]
+                own, far, b0 = spread_nodes(d, r.a_s[q], sums, r.mw1[0], nodes, r.msg, 0)
+                r.dn_own[q] = own + r.dr1[q]
+                r.dn_far[q] = far.astype(BF)
+                message_small(d, r, b0)
+            at = d.at_small
+            r.msg[f : 2 * f] = r.a_w1[...].T
+            r.msg[3 * f : 4 * f] = 0.5 * r.m_w2[:f]
+            r.msg[at + 1 : at + 2] = r.m_w2[f : f + 1]
 
     return ph.call("enc_message_back", body)
 

time: 175 us -> 173 us (0.989)
  Pallas kernels: 174 us -> 172 us
    pallas_call x5, Pallas kernels: 145 us -> 143 us  [call(): pl.pallas_call(kernel, grid=(d.parts, d.blocks), in_specs=[s for _, _, s...]
where the time goes in v7:
time: 173 us
  Pallas kernels  172 us (99%)
    pallas_call x5, Pallas kernels, call(): pl.pallas_call(kernel, grid=(d.parts, d.blocks), in_specs=[s for _, _, s...  143 us
    pallas_call x1, Pallas kernels, reduce_grads(): pl.pallas_call(kernel, in_specs=[anywhere] * 5, out_specs=[vm, anywhere],...  27.1 us

profile of v7, /device:TPU:0, one launch (start us, length us, event | category | flops | bytes accessed | tf_op | source)
XLA Modules:
  0.0 172.9 jit_solution(6341710074120660369)
XLA Ops:
  0.7 26.6 %enc_message.1 = (s32[2,2,1,4608]{3,2,1,0:T(1,128)}, f32[2,192,128]{2,1,0:T(8,128)}, bf16[2,2,144,4608]{3,2,1,0:T(8,128)(2,1)}, bf16[2,2,128,4608]{3,2,1,0:T(8,1...) custom-call(bf16[2,192,128]{2,1,0:T(8,128)(2,1)} %refs_2_.2, ...), custom_call_target="tpu_custom_call" | custom-call | tf_op jit(solution)/shard_map/enc_message/pallas_call | solution.py:207
  27.3 28.3 %enc_update.1 = (bf16[2,2,272,4608]{3,2,1,0:T(8,128)(2,1)}, bf16[2,2,128,4608]{3,2,1,0:T(8,128)(2,1)}, bf16[2,2,128,4608]{3,2,1,0:T(8,128)(2,1)}, bf16[2,2,128,4...) custom-call(bf16[2,192,128]{2,1,0:T(8,128)(2,1)} %get-tuple-element., ...), custom_call_target="tpu_custom_call" | custom-call | tf_op jit(solution)/shard_map/enc_update/pallas_call | solution.py:207
  55.6 30.1 %dec_update.1 = (bf16[2,192,48,128]{3,2,1,0:T(8,128)(2,1)}, bf16[2,2,128,4608]{3,2,1,0:T(8,128)(2,1)}, f32[672,128]{1,0:T(8,128)}, f32[2,192,128]{2,1,0:T(8,128)...) custom-call(bf16[2,192,128]{2,1,0:T(8,128)(2,1)} %get-tuple-element.101.refs_0_, ...), custom_call_target="tpu_custom_call" | custom-call | tf_op jit(solution)/shard_map/dec_update/pallas_call | solution.py:207
  85.6 36.6 %dec_message_back.1 = (bf16[2,2,128,4608]{3,2,1,0:T(8,128)(2,1)}, f32[1696,128]{1,0:T(8,128)}, f32[672,128]{1,0:T(8,128)}, f32[2,192,128]{2,1,0:T(8,128)}, bf16[2,192,128]{2,1,0:T(8,128)(2,1)}) custom-call(bf16[2,192,128]{2,1,0:T(8,128)(2,1)} %get-tuple-element.106.refs_0_, bf16[2,192,128]{2,1,0:T(8,128)(2,1)} %refs_1_.3, ...), custom_call_target="tpu_custom_call" | custom-call | tf_op jit(solution)/shard_map/dec_message_back/pallas_call | solution.py:207
  122.3 21.1 %enc_message_back.1 = (bf16[2,192,48,128]{3,2,1,0:T(8,128)(2,1)}, f32[1696,128]{1,0:T(8,128)}, f32[2,192,128]{2,1,0:T(8,128)}, bf16[2,192,128]{2,1,0:T(8,128)(2,1)}) custom-call(f32[2,192,128]{2,1,0:T(8,128)} %get-tuple-element.122.refs_0_, bf16[2,192,128]{2,1,0:T(8,128)(2,1)} %get-tuple-element.123.refs_1_, bf16[2,192,128]{2,1,0:T(8,128)(2,1)} %refs_2_.2, ...), custom_call_target="tpu_custom_call" | custom-call | tf_op jit(solution)/shard_map/enc_message_back/pallas_call | solution.py:207
  143.3 27.1 %reduce.1 = (bf16[2560,128]{1,0:T(8,128)(2,1)}, bf16[2,192,128]{2,1,0:T(8,128)(2,1)}) custom-call(f32[1696,128]{1,0:T(8,128)} %get-tuple-element.134.em, f32[672,128]{1,0:T(8,128)} %get-tuple-element.135.eu, f32[1696,128]{1,0:T(8,128)} %get-tuple-element.136.dm, f32[672,128]{1,0:T(8,128)} %get-tuple-element.137.du, bf16[2,192,128]{2,1,0:T(8,128)(2,1)} %get-tuple-element.138.far), custom_call_target="tpu_custom_call" | custom-call | tf_op jit(solution)/shard_map/reduce/pallas_call | solution.py:1208
  170.4 2.3 %unpack.1 = (bf16[2,192,128]{2,1,0:T(8,128)(2,1)}, f32[1,384,128]{2,1,0:T(8,128)}, f32[1,128,128]{2,1,0:T(8,128)}, f32[1,128,128]{2,1,0:T(8,128)}, f32[1,128,512...) custom-call(bf16[2560,128]{1,0:T(8,128)(2,1)} %get-tuple-element.139, ...), custom_call_target="tpu_custom_call" | custom-call | tf_op jit(solution)/shard_map/unpack/pallas_call | solution.py:1244

commit v8 on v7

--- a/solution.py
+++ b/solution.py
@@ -174,11 +174,6 @@
                 for i, n in into:
                     copy(i, n, step, now).start()
 
-            @pl.when(step + 1 < steps)
-            def _():
-                for i, n in into:
-                    copy(i, n, step + 1, 1 - now).start()
-
             @pl.when(step >= 2)
             def _():
                 for i, n in outof:
@@ -187,6 +182,11 @@
             def ready():
                 for i, n in into:
                     copy(i, n, step, now).wait()
+
+                @pl.when(step + 1 < steps)
+                def _():
+                    for i, n in into:
+                        copy(i, n, step + 1, 1 - now).start()
 
             def flush():
                 for i, n in outof:
@@ -768,11 +768,11 @@
     ph.temp(BF, tt=(wide, d.rows), tn=(d.rows, d.length + 128), da1=(d.feat, d.rows))
     ph.temp(BF, w3c=(d.feat, 2 * d.feat), gain_mat=sq, pair=(3 * d.feat + 16, d.rows), low=(2 * d.feat, d.rows))
     ph.temp(F32, w3c_b=sq, aux=sq, cols=sq, a_w23=(2 * d.feat + 16, 2 * d.feat), a_b9=sq, a_g2=sq)
-    ph.temp(F32, a_s=(d.feat, d.length), a_k=(d.blocks, d.feat, 128))
+    ph.temp(F32, a_s=(d.parts, d.feat, d.length), a_k=(d.parts, d.blocks, d.feat, 128))
 
     def body(r):
         p, b = pl.program_id(0), pl.program_id(1)
-        first, last = b == 0, b == d.blocks - 1
+        first = b == 0
 
         @pl.when(first & (p == 0))
         def _():
@@ -785,7 +785,7 @@
             load_cols(r, 1, r.aux, r.cols)
             centre_weights(r.uw3[1], r.cols[...], r.w3c, r.w3c_b)
             r.gain_mat[...] = gain_matrix(r.cols[...])
-            zero(r.upd, r.a_w23, r.a_b9, r.a_g2)
+            zero(r.upd, r.a_w23, r.a_b9, r.a_g2, r.a_s)
             r.pair[3 * d.feat :] = jnp.ones((16, d.rows), BF)
             r.tt[d.length :, :] = r.rt[: d.res]
             r.tn[:, d.length :] = r.rt[...].T
@@ -795,7 +795,6 @@
             r.n_cat[: d.half] = r.n_own[p]
             r.n_cat[d.half :] = r.n_got[p]
             put_table(d, r.lhs, 0, 0, r.n_cat, r.uw1.at[1])
-            zero(r.a_s)
 
         r.ready()
         f = d.feat
@@ -817,19 +816,20 @@
         update_backward(d, r, dr3, r.pair[f:], d1, d2, r.w2h[...], r.w3h[...], r.low, r.da1)
         r.upd[f : 2 * f] += mm(e2, r.da1[...], 1, 1)
         r.part[...] = (mm(r.uw1[1, f : 2 * f, :], r.da1[...]) + dr3.astype(F32)).astype(BF)
-        spread = mm(r.da1[...], r.tn[...])
-        r.a_s[...] += spread[:, : d.length]
-        r.a_k[b] = spread[:, d.length :]
+        put_spread(d, r, p, b, mm(r.da1[...], r.tn[...]))
         r.flush()
 
-        @pl.when(last)
-        def _():
-            own, far, b4 = spread_nodes(
-                d, r.a_s[...], [r.a_k[i] for i in range(d.blocks)], r.uw1[1], r.n_cat[...], r.upd, 0
-            )
-            r.dn_own[p] = own
-            r.dn_far[p] = far.astype(BF)
-            update_small(d, r, b4)
+        @pl.when((b == d.blocks - 1) & (p == d.parts - 1))
+        def _():
+            total = jnp.zeros((1, f), F32)
+            for q in range(d.parts):
+                nodes = jnp.concatenate([r.n_own[q], r.n_got[q]], axis=0)
+                sums = [r.a_k[q, i] for i in range(d.blocks)]
+                own, far, b4 = spread_nodes(d, r.a_s[q], sums, r.uw1[1], nodes, r.upd, 0)
+                r.dn_own[q] = own
+                r.dn_far[q] = far.astype(BF)
+                total = total + b4
+            update_small(d, r, total)
 
     return ph.call("dec_update", body)
 

time: 173 us -> 172 us (level)
  no operation moved by 1% of the time
where the time goes in v8:
time: 172 us
  Pallas kernels  171 us (99%)
    pallas_call x5, Pallas kernels, call(): pl.pallas_call(kernel, grid=(d.parts, d.blocks), in_specs=[s for _, _, s...  142 us
    pallas_call x1, Pallas kernels, reduce_grads(): pl.pallas_call(kernel, in_specs=[anywhere] * 5, out_specs=[vm, anywhere],...  27.1 us

profile of v8, /device:TPU:0, one launch (start us, length us, event | category | flops | bytes accessed | tf_op | source)
XLA Modules:
  0.0 171.9 jit_solution(16009120601900733459)
XLA Ops:
  0.7 26.6 %enc_message.1 = (s32[2,2,1,4608]{3,2,1,0:T(1,128)}, f32[2,192,128]{2,1,0:T(8,128)}, bf16[2,2,144,4608]{3,2,1,0:T(8,128)(2,1)}, bf16[2,2,128,4608]{3,2,1,0:T(8,1...) custom-call(bf16[2,192,128]{2,1,0:T(8,128)(2,1)} %refs_2_.2, ...), custom_call_target="tpu_custom_call" | custom-call | tf_op jit(solution)/shard_map/enc_message/pallas_call | solution.py:207
  27.3 28.4 %enc_update.1 = (bf16[2,2,272,4608]{3,2,1,0:T(8,128)(2,1)}, bf16[2,2,128,4608]{3,2,1,0:T(8,128)(2,1)}, bf16[2,2,128,4608]{3,2,1,0:T(8,128)(2,1)}, bf16[2,2,128,4...) custom-call(bf16[2,192,128]{2,1,0:T(8,128)(2,1)} %get-tuple-element., ...), custom_call_target="tpu_custom_call" | custom-call | tf_op jit(solution)/shard_map/enc_update/pallas_call | solution.py:207
  55.7 29.2 %dec_update.1 = (bf16[2,192,48,128]{3,2,1,0:T(8,128)(2,1)}, bf16[2,2,128,4608]{3,2,1,0:T(8,128)(2,1)}, f32[672,128]{1,0:T(8,128)}, f32[2,192,128]{2,1,0:T(8,128)...) custom-call(bf16[2,192,128]{2,1,0:T(8,128)(2,1)} %get-tuple-element.101.refs_0_, ...), custom_call_target="tpu_custom_call" | custom-call | tf_op jit(solution)/shard_map/dec_update/pallas_call | solution.py:207
  84.9 36.5 %dec_message_back.1 = (bf16[2,2,128,4608]{3,2,1,0:T(8,128)(2,1)}, f32[1696,128]{1,0:T(8,128)}, f32[672,128]{1,0:T(8,128)}, f32[2,192,128]{2,1,0:T(8,128)}, bf16[2,192,128]{2,1,0:T(8,128)(2,1)}) custom-call(bf16[2,192,128]{2,1,0:T(8,128)(2,1)} %get-tuple-element.106.refs_0_, bf16[2,192,128]{2,1,0:T(8,128)(2,1)} %refs_1_.3, ...), custom_call_target="tpu_custom_call" | custom-call | tf_op jit(solution)/shard_map/dec_message_back/pallas_call | solution.py:207
  121.4 21.0 %enc_message_back.1 = (bf16[2,192,48,128]{3,2,1,0:T(8,128)(2,1)}, f32[1696,128]{1,0:T(8,128)}, f32[2,192,128]{2,1,0:T(8,128)}, bf16[2,192,128]{2,1,0:T(8,128)(2,1)}) custom-call(f32[2,192,128]{2,1,0:T(8,128)} %get-tuple-element.122.refs_0_, bf16[2,192,128]{2,1,0:T(8,128)(2,1)} %get-tuple-element.123.refs_1_, bf16[2,192,128]{2,1,0:T(8,128)(2,1)} %refs_2_.2, ...), custom_call_target="tpu_custom_call" | custom-call | tf_op jit(solution)/shard_map/enc_message_back/pallas_call | solution.py:207
  142.4 27.1 %reduce.1 = (bf16[2560,128]{1,0:T(8,128)(2,1)}, bf16[2,192,128]{2,1,0:T(8,128)(2,1)}) custom-call(f32[1696,128]{1,0:T(8,128)} %get-tuple-element.134.em, f32[672,128]{1,0:T(8,128)} %get-tuple-element.135.eu, f32[1696,128]{1,0:T(8,128)} %get-tuple-element.136.dm, f32[672,128]{1,0:T(8,128)} %get-tuple-element.137.du, bf16[2,192,128]{2,1,0:T(8,128)(2,1)} %get-tuple-element.138.far), custom_call_target="tpu_custom_call" | custom-call | tf_op jit(solution)/shard_map/reduce/pallas_call | solution.py:1208
  169.4 2.3 %unpack.1 = (bf16[2,192,128]{2,1,0:T(8,128)(2,1)}, f32[1,384,128]{2,1,0:T(8,128)}, f32[1,128,128]{2,1,0:T(8,128)}, f32[1,128,128]{2,1,0:T(8,128)}, f32[1,128,512...) custom-call(bf16[2560,128]{1,0:T(8,128)(2,1)} %get-tuple-element.139, ...), custom_call_target="tpu_custom_call" | custom-call | tf_op jit(solution)/shard_map/unpack/pallas_call | solution.py:1244

commit v9 on v8

--- a/solution.py
+++ b/solution.py
@@ -81,6 +81,7 @@
         self.d = dims
         self.collective_id = collective_id
         self.ins, self.outs, self.temps, self.kinds, self.wholes, self.later = [], [], [], {}, {}, ()
+        self.only = {}
 
     def whole_spec(self, shape):
         rank = len(shape)
@@ -158,9 +159,13 @@
             outof = [(i, n) for i, n in enumerate(self.kinds) if self.kinds[n][0]]
 
             def loads():
-                return [
-                    pltpu.make_async_copy(plain[n], kept[i], rest[-1].at[i]) for i, n in enumerate(self.wholes)
-                ]
+                out = []
+                for i, n in enumerate(self.wholes):
+                    src, dst = plain[n], kept[i]
+                    if n in self.only:
+                        src, dst = src.at[self.only[n]], dst.at[self.only[n]]
+                    out.append(pltpu.make_async_copy(src, dst, rest[-1].at[i]))
+                return out
 
             def load(*later):
                 for item, n in zip(loads(), self.wholes):
@@ -608,6 +613,8 @@
     ph.temp(F32, w3c_b=sq, e_aux=sq, e_cols=sq, d_aux=sq, d_cols=sq)
     ph.sems(send=d.parts + 1, recv=d.parts + 1)
 
+    ph.only = dict(mw1=1, mw2=1, mw3=1, inner=1, inner_b=1, outer=1, uw1=0, uw2=0, uw3=0)
+
     def body(r):
         p, b = pl.program_id(0), pl.program_id(1)
         first, last = b == 0, b == d.blocks - 1
@@ -770,6 +777,8 @@
     ph.temp(F32, w3c_b=sq, aux=sq, cols=sq, a_w23=(2 * d.feat + 16, 2 * d.feat), a_b9=sq, a_g2=sq)
     ph.temp(F32, a_s=(d.parts, d.feat, d.length), a_k=(d.parts, d.blocks, d.feat, 128))
 
+    ph.only = dict(uw1=1, uw2=1, uw3=1)
+
     def body(r):
         p, b = pl.program_id(0), pl.program_id(1)
         first = b == 0
@@ -871,6 +880,8 @@
     ph.temp(F32, a_s=(2 * d.feat, d.length), a_k=(d.blocks, 2 * d.feat, 128))
     ph.sems(send=2 * d.parts, recv=2 * d.parts)
 
+    ph.only = dict(mw1=1, mw2=1, mw3=1, inner=1, inner_b=1, outer=1, uw1=0, uw2=0, uw3=0)
+
     def body(r):
         p, b = pl.program_id(0), pl.program_id(1)
         first, last = b == 0, b == d.blocks - 1
@@ -978,6 +989,8 @@
     ph.temp(BF, low=(2 * d.feat, d.rows), mw2h=sq)
     ph.temp(F32, dr1=(d.parts, d.half, d.feat), aux=sq, cols=sq, a_w1=sq, m_w2=(d.feat + 16, d.feat))
     ph.temp(F32, a_s=(d.parts, d.feat, d.length), a_k=(d.parts, d.blocks, d.feat, 128))
+
+    ph.only = dict(mw1=0, mw2=0, mw3=0, inner=0, inner_b=0, outer=0)
 
     def body(r):
         p, b = pl.program_id(0), pl.program_id(1)

time: 172 us -> 172 us (level)
  no operation moved by 1% of the time
where the time goes in v9:
time: 172 us
  Pallas kernels  171 us (99%)
    pallas_call x5, Pallas kernels, call(): pl.pallas_call(kernel, grid=(d.parts, d.blocks), in_specs=[s for _, _, s...  141 us
    pallas_call x1, Pallas kernels, reduce_grads(): pl.pallas_call(kernel, in_specs=[anywhere] * 5, out_specs=[vm, anywhere],...  27.1 us

profile of v9, /device:TPU:0, one launch (start us, length us, event | category | flops | bytes accessed | tf_op | source)
XLA Modules:
  0.0 171.5 jit_solution(9364746782878939812)
XLA Ops:
  0.7 26.6 %enc_message.1 = (s32[2,2,1,4608]{3,2,1,0:T(1,128)}, f32[2,192,128]{2,1,0:T(8,128)}, bf16[2,2,144,4608]{3,2,1,0:T(8,128)(2,1)}, bf16[2,2,128,4608]{3,2,1,0:T(8,1...) custom-call(bf16[2,192,128]{2,1,0:T(8,128)(2,1)} %refs_2_.2, ...), custom_call_target="tpu_custom_call" | custom-call | tf_op jit(solution)/shard_map/enc_message/pallas_call | solution.py:212
  27.3 28.3 %enc_update.1 = (bf16[2,2,272,4608]{3,2,1,0:T(8,128)(2,1)}, bf16[2,2,128,4608]{3,2,1,0:T(8,128)(2,1)}, bf16[2,2,128,4608]{3,2,1,0:T(8,128)(2,1)}, bf16[2,2,128,4...) custom-call(bf16[2,192,128]{2,1,0:T(8,128)(2,1)} %get-tuple-element., ...), custom_call_target="tpu_custom_call" | custom-call | tf_op jit(solution)/shard_map/enc_update/pallas_call | solution.py:212
  55.6 29.2 %dec_update.1 = (bf16[2,192,48,128]{3,2,1,0:T(8,128)(2,1)}, bf16[2,2,128,4608]{3,2,1,0:T(8,128)(2,1)}, f32[672,128]{1,0:T(8,128)}, f32[2,192,128]{2,1,0:T(8,128)...) custom-call(bf16[2,192,128]{2,1,0:T(8,128)(2,1)} %get-tuple-element.101.refs_0_, ...), custom_call_target="tpu_custom_call" | custom-call | tf_op jit(solution)/shard_map/dec_update/pallas_call | solution.py:212
  84.8 36.3 %dec_message_back.1 = (bf16[2,2,128,4608]{3,2,1,0:T(8,128)(2,1)}, f32[1696,128]{1,0:T(8,128)}, f32[672,128]{1,0:T(8,128)}, f32[2,192,128]{2,1,0:T(8,128)}, bf16[2,192,128]{2,1,0:T(8,128)(2,1)}) custom-call(bf16[2,192,128]{2,1,0:T(8,128)(2,1)} %get-tuple-element.106.refs_0_, bf16[2,192,128]{2,1,0:T(8,128)(2,1)} %refs_1_.3, ...), custom_call_target="tpu_custom_call" | custom-call | tf_op jit(solution)/shard_map/dec_message_back/pallas_call | solution.py:212
  121.1 20.8 %enc_message_back.1 = (bf16[2,192,48,128]{3,2,1,0:T(8,128)(2,1)}, f32[1696,128]{1,0:T(8,128)}, f32[2,192,128]{2,1,0:T(8,128)}, bf16[2,192,128]{2,1,0:T(8,128)(2,1)}) custom-call(f32[2,192,128]{2,1,0:T(8,128)} %get-tuple-element.122.refs_0_, bf16[2,192,128]{2,1,0:T(8,128)(2,1)} %get-tuple-element.123.refs_1_, bf16[2,192,128]{2,1,0:T(8,128)(2,1)} %refs_2_.2, ...), custom_call_target="tpu_custom_call" | custom-call | tf_op jit(solution)/shard_map/enc_message_back/pallas_call | solution.py:212
  141.9 27.1 %reduce.1 = (bf16[2560,128]{1,0:T(8,128)(2,1)}, bf16[2,192,128]{2,1,0:T(8,128)(2,1)}) custom-call(f32[1696,128]{1,0:T(8,128)} %get-tuple-element.134.em, f32[672,128]{1,0:T(8,128)} %get-tuple-element.135.eu, f32[1696,128]{1,0:T(8,128)} %get-tuple-element.136.dm, f32[672,128]{1,0:T(8,128)} %get-tuple-element.137.du, bf16[2,192,128]{2,1,0:T(8,128)(2,1)} %get-tuple-element.138.far), custom_call_target="tpu_custom_call" | custom-call | tf_op jit(solution)/shard_map/reduce/pallas_call | solution.py:1221
  169.0 2.3 %unpack.1 = (bf16[2,192,128]{2,1,0:T(8,128)(2,1)}, f32[1,384,128]{2,1,0:T(8,128)}, f32[1,128,128]{2,1,0:T(8,128)}, f32[1,128,128]{2,1,0:T(8,128)}, f32[1,128,512...) custom-call(bf16[2560,128]{1,0:T(8,128)(2,1)} %get-tuple-element.139, ...), custom_call_target="tpu_custom_call" | custom-call | tf_op jit(solution)/shard_map/unpack/pallas_call | solution.py:1257
